TPU v7x, 1024 devices: a whole 8x8x8 slice. The times are simulated.
1024 devices in a mesh: expert: 64 (over x, y), dp: 16 (over z, core).
Axes of the slice: x: 8, y: 8, z: 8, core: 2. Of those that a mesh axis runs over, the one named last changes fastest.
Arguments:
- tokens: bfloat16 [131072, 2048], P(('expert', 'dp')), may hold values from -6 to 6
- cotangent: bfloat16 [131072, 2048], P(('expert', 'dp')), may hold values from -6 to 6
- expert_ids: int32 [131072, 1], P(('expert', 'dp')), may hold values from 0 to 63; in each aligned block of 128 rows (0 to 127, 128 to 255, ...) at most 3 rows name the same one
- route_weight: float32 [131072, 1], P(('expert', 'dp')), may hold values from 0.25 to 1
- w_gate: bfloat16 [64, 2048, 768], P('expert'), may hold values from -0.125 to 0.125
- w_up: bfloat16 [64, 2048, 768], P('expert'), may hold values from -0.125 to 0.125
- w_down: bfloat16 [2048, 64, 768], P('dp', 'expert'), may hold values from -0.21875 to 0.21875
Outputs:
- token_grad: bfloat16 [131072, 2048], P(('expert', 'dp'))
- down_grad: float32 [2048, 64, 768], P('dp', 'expert')
Inputs may be any that keep to these rules, and one draw needn't show every extreme that they name: `expert_ids`: each token names 1 different experts. Among the 128 tokens of one device no expert is named more than 3 times, a bound that some block reaches.
All inputs are finite; a program needn't handle non-finite values.
Results may differ from a plain program's by a relative error of at most 0.02.
Values may be sent and summed in bfloat16 or wider, within the bound.
No kernel may reach another device: no remote copies, remote signals or barrier semaphores. Data moves between devices by JAX's collectives and lax.ppermute only.
A program may use at most 64 MiB of HBM per device.

v0:
```python
import jax
import jax.numpy as jnp
from jax import lax
from jax.sharding import PartitionSpec as P


def slot_numbers(expert_ids, experts, capacity):
    tok_rows, topk = expert_ids.shape
    assigned = tok_rows * topk
    flat_ids = expert_ids.reshape(assigned)
    choose = (flat_ids[:, None] == jnp.arange(experts, dtype=jnp.int32)[None, :]).astype(
        jnp.float32
    )
    earlier = (jnp.arange(assigned)[:, None] > jnp.arange(assigned)[None, :]).astype(jnp.float32)
    counted = jnp.dot(earlier, choose, precision=lax.Precision.HIGHEST)
    rank = jnp.sum(counted * choose, axis=1).astype(jnp.int32)
    return flat_ids * capacity + rank


def forward_hidden(rows_four, w_gate, w_up):
    gate = jnp.einsum("ilcd,ldf->ilcf", rows_four, w_gate, preferred_element_type=jnp.float32)
    up = jnp.einsum("ilcd,ldf->ilcf", rows_four, w_up, preferred_element_type=jnp.float32)
    hidden = (jax.nn.silu(gate) * up).astype(jnp.bfloat16)
    return (gate, up, hidden)


def on_device(tokens, cotangent, expert_ids, route_weight, w_gate, w_up, w_down):
    tok_rows, width = tokens.shape
    topk = expert_ids.shape[1]
    exp_dev = w_gate.shape[0]
    n_peers = lax.axis_size("expert")
    experts = exp_dev * n_peers
    capacity = 3 * tok_rows * topk // (2 * experts)
    slot_count = experts * capacity
    assigned = tok_rows * topk
    slots = slot_numbers(expert_ids, experts, capacity)
    slot_iota = jnp.arange(slot_count, dtype=jnp.int32)
    placing = (slot_iota[:, None] == slots[None, :]).astype(jnp.bfloat16)
    collecting = jnp.sum(
        (slots.reshape(tok_rows, topk)[:, :, None] == slot_iota[None, None, :]).astype(jnp.float32),
        axis=1,
    ).astype(jnp.bfloat16)
    spread_rows = tokens[:, None, :].reshape(assigned, width)
    scaled = (
        (route_weight[:, :, None] * cotangent[:, None, :])
        .astype(jnp.bfloat16)
        .reshape(assigned, width)
    )
    sent_rows = jnp.dot(placing, spread_rows, preferred_element_type=jnp.float32).astype(
        jnp.bfloat16
    )
    sent_cot = jnp.dot(placing, scaled, preferred_element_type=jnp.float32).astype(jnp.bfloat16)
    shape_four = (n_peers, exp_dev, capacity, width)
    got_rows, got_cot = (
        lax.all_to_all(sent_rows, "expert", split_axis=0, concat_axis=0, tiled=True),
        lax.all_to_all(sent_cot, "expert", split_axis=0, concat_axis=0, tiled=True),
    )
    gate, up, hidden = forward_hidden(got_rows.reshape(shape_four), w_gate, w_up)
    cot_four = got_cot.reshape(shape_four)
    full_down = lax.all_gather(w_down, "dp", axis=0, tiled=True)
    hidden_grad = jnp.einsum(
        "ilcd,dlf->ilcf", cot_four, full_down, preferred_element_type=jnp.float32
    )
    sig = jax.nn.sigmoid(gate)
    gate_grad = (hidden_grad * up * sig * (1.0 + gate * (1.0 - sig))).astype(jnp.bfloat16)
    up_grad = (hidden_grad * (gate * sig)).astype(jnp.bfloat16)
    token_part = (
        jnp.einsum("ilcf,ldf->ilcd", gate_grad, w_gate, preferred_element_type=jnp.float32)
        + jnp.einsum("ilcf,ldf->ilcd", up_grad, w_up, preferred_element_type=jnp.float32)
    ).astype(jnp.bfloat16)
    returned = lax.all_to_all(
        token_part.reshape(slot_count, width), "expert", split_axis=0, concat_axis=0, tiled=True
    )
    token_grad = jnp.dot(collecting, returned, preferred_element_type=jnp.float32).astype(
        jnp.bfloat16
    )
    down_grad = lax.psum_scatter(
        jnp.einsum("ilcd,ilcf->dlf", cot_four, hidden, preferred_element_type=jnp.float32).astype(
            jnp.bfloat16
        ),
        "dp",
        scatter_dimension=0,
        tiled=True,
    ).astype(jnp.float32)
    return (token_grad, down_grad)


def solution(mesh):
    in_specs = (
        P(("expert", "dp"), None),
        P(("expert", "dp"), None),
        P(("expert", "dp"), None),
        P(("expert", "dp"), None),
        P("expert", None, None),
        P("expert", None, None),
        P("dp", "expert", None),
    )
    out_specs = (P(("expert", "dp"), None), P("dp", "expert", None))
    return jax.shard_map(
        on_device, mesh=mesh, in_specs=in_specs, out_specs=out_specs, check_vma=False
    )
```

profile of v0, /device:TPU:14, one launch (start us, length us, event | category | flops | bytes accessed | tf_op | source)
XLA Modules:
  0.0 187.7 jit_solution(9065091232513287189)
XLA Ops:
  7.2 0.7 all-gather.2.cloned.1.call-update
  7.9 1.0 fusion.26
  9.6 2.3 %convolution_convert_fusion = bf16[192,2048]{1,0:T(8,128)(2,1)} fusion(bf16[128,2048]{1,0:T(8,128)(2,1)} %param.7, s32[128]{0:T(128)S(1)} %convert_add_fusion), kind=kOutput, calls=%fused_computation.14 | convolution fusion | flops 101081088 | bytes 1311232 | tf_op jit(solution)/shard_map/dot_general | solution.py:49
  11.9 3.3 %all_to_all.20 = bf16[64,3,2048]{2,1,0:T(4,128)(2,1)} reshape(bf16[192,2048]{1,0:T(8,128)(2,1)} %convolution_convert_fusion) | data formatting | bytes 1572864 | tf_op jit(solution)/shard_map/all_to_all | solution.py:55
  15.1 18.3 %all-to-all-start.1 = ((bf16[64,3,2048]{2,1,0:T(4,128)(2,1)}), bf16[64,3,2048]{2,1,0:T(4,128)(2,1)}, u32[]{:S(2)}, u32[]{:S(2)}) async-start(bf16[64,3,2048]{2,1,0:T(4,128)(2,1)} %all_to_all.20), calls=%async_computation.1 | async-start | bytes 2097152 | tf_op jit(solution)/shard_map/all_to_all | solution.py:55
  33.4 2.4 %convolution_convert_fusion.1 = bf16[192,2048]{1,0:T(8,128)(2,1)} fusion(bf16[128,2048]{1,0:T(8,128)(2,1)} %param.8, f32[128]{0:T(128)S(1)} %bitcast.74, s32[128]{0:T(128)S(1)} %convert_add_fusion), kind=kOutput, calls=%fused_computation.15 | convolution fusion | flops 101867520 | bytes 1311744 | tf_op jit(solution)/shard_map/dot_general | solution.py:52
  35.8 3.3 %all_to_all.18 = bf16[64,3,2048]{2,1,0:T(4,128)(2,1)} reshape(bf16[192,2048]{1,0:T(8,128)(2,1)} %convolution_convert_fusion.1) | data formatting | bytes 1572864 | tf_op jit(solution)/shard_map/all_to_all | solution.py:56
  39.1 18.6 %all-to-all-done.1 = bf16[64,3,2048]{2,1,0:T(4,128)(2,1)} async-done(((bf16[64,3,2048]{2,1,0:T(4,128)(2,1)}), bf16[64,3,2048]{2,1,0:T(4,128)(2,1)}, u32[]{:S(2)}, u32[]{:S(2)}) %all-to-all-start.1) | async-done | bytes 786464 | tf_op jit(solution)/shard_map/all_to_all | solution.py:55
  57.7 7.5 %all-to-all-start = ((bf16[64,3,2048]{2,1,0:T(4,128)(2,1)}), bf16[64,3,2048]{2,1,0:T(4,128)(2,1)}, u32[]{:S(2)}, u32[]{:S(2)}) async-start(bf16[64,3,2048]{2,1,0:T(4,128)(2,1)} %all_to_all.18), calls=%async_computation | async-start | bytes 2097152 | tf_op jit(solution)/shard_map/all_to_all | solution.py:56
  65.5 3.7 %fusion.23 = f32[64,1,3,768]{3,0,2,1:T(8,128)} fusion(bf16[1,2048,768]{2,1,0:T(8,128)(2,1)S(1)} %copy-done, bf16[64,3,2048]{2,1,0:T(4,128)(2,1)} %all-to-all-done.1), kind=kOutput, calls=%fused_computation.19 | convolution fusion | flops 603979776 | bytes 4521984 | tf_op jit(solution)/shard_map/ilcd,ldf->ilcf/dot_general | solution.py:21
  69.2 3.6 %fusion.20 = f32[64,1,3,768]{3,0,2,1:T(8,128)} fusion(bf16[1,2048,768]{2,1,0:T(8,128)(2,1)S(1)} %copy-done.1, bf16[64,3,2048]{2,1,0:T(4,128)(2,1)} %all-to-all-done.1), kind=kOutput, calls=%fused_computation.18 | convolution fusion | flops 603979776 | bytes 4521984 | tf_op jit(solution)/shard_map/ilcd,ldf->ilcf/dot_general | solution.py:22
  72.7 19.9 %all-to-all-done = bf16[64,3,2048]{2,1,0:T(4,128)(2,1)} async-done(((bf16[64,3,2048]{2,1,0:T(4,128)(2,1)}), bf16[64,3,2048]{2,1,0:T(4,128)(2,1)}, u32[]{:S(2)}, u32[]{:S(2)}) %all-to-all-start) | async-done | bytes 786464 | tf_op jit(solution)/shard_map/all_to_all | solution.py:56
  92.6 4.9 %fusion.10 = bf16[2048,768]{0,1:T(8,128)(2,1)} fusion(bf16[64,3,2048]{2,1,0:T(4,128)(2,1)} %all-to-all-done, f32[64,1,3,768]{3,0,2,1:T(8,128)} %fusion.20, f32[64,1,3,768]{3,0,2,1:T(8,128)} %fusion.23), kind=kOutput, calls=%fused_computation.11 | convolution fusion | flops 606437376 | bytes 5111808 | tf_op jit(solution)/shard_map/ilcd,ilcf->dlf/dot_general | solution.py:78
  97.5 4.6 %copy.24 = bf16[2048,768]{1,0:T(8,128)(2,1)} copy(bf16[2048,768]{0,1:T(8,128)(2,1)} %fusion.10) | data formatting | bytes 6291456
  102.2 3.8 %fusion.17 = f32[64,1,3,768]{3,0,2,1:T(8,128)S(1)} fusion(bf16[2048,1,768]{2,0,1:T(8,128)(2,1)} %all-gather.2.cloned.1.call-done, bf16[64,3,2048]{2,1,0:T(4,128)(2,1)} %all-to-all-done), kind=kOutput, calls=%fused_computation.17 | convolution fusion | flops 603979776 | bytes 4521984 | tf_op jit(solution)/shard_map/ilcd,dlf->ilcf/dot_general | solution.py:61
  106.0 1.2 fusion
  107.9 1.2 fusion.14
  109.8 35.6 %all_to_all.27 = bf16[64,3,2048]{2,1,0:T(4,128)(2,1)} all-to-all(bf16[64,3,2048]{2,1,0:T(4,128)(2,1)S(1)} %copy.19), channel_id=1, replica_groups=mesh['expert'=64,'dp'=16] {'expert'}, dimensions={0} | all-to-all | bytes 1572864 | tf_op jit(solution)/shard_map/all_to_all | solution.py:71
  145.3 3.2 %all_to_all.23 = bf16[192,2048]{1,0:T(8,128)(2,1)} reshape(bf16[64,3,2048]{2,1,0:T(4,128)(2,1)} %all_to_all.27) | data formatting | bytes 1572864 | tf_op jit(solution)/shard_map/all_to_all | solution.py:71
  148.5 2.3 %convolution_convert_fusion.2 = bf16[128,2048]{1,0:T(8,128)(2,1)} fusion(bf16[192,2048]{1,0:T(8,128)(2,1)} %all_to_all.23, s32[128]{0:T(128)S(1)} %convert_add_fusion), kind=kOutput, calls=%fused_computation.16 | convolution fusion | flops 100999168 | bytes 1311232 | tf_op jit(solution)/shard_map/dot_general | solution.py:74
  150.8 26.4 %reduce-scatter.4.cloned.1.call-done = bf16[128,768]{1,0:T(8,128)(2,1)} async-done(((bf16[2048,768]{1,0:T(8,128)(2,1)}), bf16[128,768]{1,0:T(8,128)(2,1)}) %reduce-scatter.4.cloned.1.call-update) | async-done | bytes 196624
  177.2 1.7 copy.25
  178.9 1.0 bitcast_convert_fusion.1
  179.9 1.0 copy.21
  (18 shorter events, 2.3 us)
Async XLA Ops:
  7.2 58.3 %copy-start = (bf16[1,2048,768]{2,1,0:T(8,128)(2,1)S(1)}, bf16[1,2048,768]{2,1,0:T(8,128)(2,1)}, u32[]{:S(2)}) copy-start(bf16[1,2048,768]{2,1,0:T(8,128)(2,1)} %param.11) | copy-start | bytes 9437188
  7.2 26.2 %copy-start.4 = (f32[128,1]{0,1:T(1,128)S(1)}, f32[128,1]{0,1:T(1,128)}, u32[]{:S(2)}) copy-start(f32[128,1]{0,1:T(1,128)} %param.10) | copy-start | bytes 1540
  7.2 95.0 %all-gather.2.cloned.1.call-start = ((), (), s32[]{:S(2)}) async-start(), calls=%async_computation.4 | async-start | bytes 3342336 | tf_op jit(solution)/shard_map/all_gather | solution.py:60
  15.1 42.6 %all-to-all-start.1 = ((bf16[64,3,2048]{2,1,0:T(4,128)(2,1)}), bf16[64,3,2048]{2,1,0:T(4,128)(2,1)}, u32[]{:S(2)}, u32[]{:S(2)}) async-start(bf16[64,3,2048]{2,1,0:T(4,128)(2,1)} %all_to_all.20), calls=%async_computation.1 | async-start | bytes 2097152 | tf_op jit(solution)/shard_map/all_to_all | solution.py:55
  57.7 34.9 %all-to-all-start = ((bf16[64,3,2048]{2,1,0:T(4,128)(2,1)}), bf16[64,3,2048]{2,1,0:T(4,128)(2,1)}, u32[]{:S(2)}, u32[]{:S(2)}) async-start(bf16[64,3,2048]{2,1,0:T(4,128)(2,1)} %all_to_all.18), calls=%async_computation | async-start | bytes 2097152 | tf_op jit(solution)/shard_map/all_to_all | solution.py:56
  65.2 111.9 %reduce-scatter.4.cloned.1.call-start = ((), (), s32[]{:S(2)}) async-start(), calls=%async_computation.5 | async-start | bytes 3342336
  65.5 3.7 %copy-start.1 = (bf16[1,2048,768]{2,1,0:T(8,128)(2,1)S(1)}, bf16[1,2048,768]{2,1,0:T(8,128)(2,1)}, u32[]{:S(2)}) copy-start(bf16[1,2048,768]{2,1,0:T(8,128)(2,1)} %param.12) | copy-start | bytes 9437188
  102.2 3.8 %copy-start.3 = (f32[64,1,3,768]{3,0,2,1:T(8,128)S(1)}, f32[64,1,3,768]{3,0,2,1:T(8,128)}, u32[]{:S(2)}) copy-start(f32[64,1,3,768]{3,0,2,1:T(8,128)} %fusion.23) | copy-start | bytes 1769476
  102.2 3.8 %copy-start.5 = (f32[64,1,3,768]{3,0,2,1:T(8,128)S(1)}, f32[64,1,3,768]{3,0,2,1:T(8,128)}, u32[]{:S(2)}) copy-start(f32[64,1,3,768]{3,0,2,1:T(8,128)} %fusion.20) | copy-start | bytes 1769476
  106.0 1.9 %copy-start.2 = (bf16[1,2048,768]{2,1,0:T(8,128)(2,1)S(1)}, bf16[1,2048,768]{2,1,0:T(8,128)(2,1)}, u32[]{:S(2)}) copy-start(bf16[1,2048,768]{2,1,0:T(8,128)(2,1)} %param.12) | copy-start | bytes 9437188
Sparse Core Ops, SparseCore 0:
  10.7 59.5 all-gather.1
  102.3 74.8 reduce-scatter.3
where the time goes:
time: 189 us; the launch traced here: 188 us
  waiting for transfers between devices  65.6 us (35%)
  blocking collectives  35.6 us (19%)
  matrix products  26.2 us (14%)
  starting transfers between devices  26.1 us (14%)
  local copies, waits for them, and re-layouts  18.5 us (10%)
  between operations  14.2 us (8%)
    all_to_all x1, blocking collectives, on_device(): lax.all_to_all(token_part.reshape(slot_count, width), 'expert', split_axi...  35.6 us
    unnamed x3, waiting for transfers between devices  27.1 us
    all_to_all x1, waiting for transfers between devices, on_device(): lax.all_to_all(sent_cot, 'expert', split_axis=0, concat_axis=0, tiled=True)  19.9 us
    all_to_all x1, waiting for transfers between devices, on_device(): lax.all_to_all(sent_rows, 'expert', split_axis=0, concat_axis=0, tiled=True)  18.6 us
    all_to_all x1, starting transfers between devices, on_device(): lax.all_to_all(sent_rows, 'expert', split_axis=0, concat_axis=0, tiled=True)  18.3 us
    unnamed x15, local copies, waits for them, and re-layouts  8.08 us
    all_to_all x1, starting transfers between devices, on_device(): lax.all_to_all(sent_cot, 'expert', split_axis=0, concat_axis=0, tiled=True)  7.53 us
    dot_general x1, matrix products, on_device(): jnp.einsum('ilcd,ilcf->dlf', cot_four, hidden, preferred_element_type=jnp...  4.86 us
  transfers between devices with their start and end apart: 4, of which 3 were waited for; matrix products, arithmetic and copies ran while one was open for 17% of the time, Pallas kernels for 0%

commit v1 on v0

v1 whole, which is shorter than its diff:
```python
import functools

import jax
import jax.numpy as jnp
from jax import lax
from jax.experimental import pallas as pl
from jax.experimental.pallas import tpu as pltpu
from jax.sharding import PartitionSpec as P

CAP = 3
LANE = 128
BF16 = jnp.bfloat16
F32 = jnp.float32

VMEM = pl.BlockSpec(memory_space=pltpu.VMEM)
SMEM = pl.BlockSpec(memory_space=pltpu.SMEM)
HBM = pl.BlockSpec(memory_space=pltpu.HBM)


def mm(a, b, ca=1, cb=0):
    return lax.dot_general(a, b, (((ca,), (cb,)), ((), ())), preferred_element_type=F32)


def slots_of(ids_row, peers):
    n = ids_row.shape[1]
    across = jnp.broadcast_to(ids_row, (n, n))
    down = across.T
    row = lax.broadcasted_iota(jnp.int32, (n, n), 0)
    col = lax.broadcasted_iota(jnp.int32, (n, n), 1)
    earlier = jnp.where((across == down) & (row < col), 1.0, 0.0).astype(F32)
    rank = jnp.sum(earlier, axis=0, keepdims=True).astype(jnp.int32)
    return rank * peers + ids_row


def placing_of(ids_row, peers):
    n = ids_row.shape[1]
    lines = lax.broadcasted_iota(jnp.int32, (CAP * peers, n), 0)
    return jnp.where(lines == slots_of(ids_row, peers), 1.0, 0.0).astype(BF16)


def lanes(q, count=1):
    return slice(q * LANE, (q + count) * LANE)


def pack_kernel(
    peers, ids_ref, weight_ref, tok_hbm, cot_hbm, out_hbm, tok, cot, out, scr, sems
):
    copies = [
        pltpu.make_async_copy(tok_hbm, tok, sems.at[0]),
        pltpu.make_async_copy(cot_hbm, cot, sems.at[1]),
    ]
    for copy in copies:
        copy.start()
    n, width = tok.shape
    chunks = width // LANE
    placing = placing_of(ids_ref[...], peers)
    weight = jnp.broadcast_to(weight_ref[...], (n, n)).T[:, :1]
    sent = []
    for which in range(2):
        copies[which].wait()
        for c in range(0, chunks, 2):
            if which == 0:
                rows = tok[:, lanes(c, 2)]
            else:
                rows = (weight * cot[:, lanes(c, 2)].astype(F32)).astype(BF16)
            placed = mm(placing, rows)
            for s in range(CAP):
                for h in range(2):
                    scr[CAP * which + s, pl.ds(c + h, peers, stride=chunks), :] = placed[
                        s * peers : (s + 1) * peers, lanes(h)
                    ]
        for q in range(CAP * which, CAP * which + CAP):
            out[which, :, :, lanes(q % CAP)] = (
                scr[q].reshape(peers, chunks, LANE).astype(BF16)
            )
        copy = pltpu.make_async_copy(
            out.at[which], out_hbm.at[:, :, pl.ds(which * CAP * LANE, CAP * LANE)], sems.at[2 + which]
        )
        copy.start()
        sent.append(copy)
    for copy in sent:
        copy.wait()


def to_rows(got, scr):
    peers, chunks, _ = got.shape
    for s in range(CAP):
        scr[s] = got[:, :, lanes(s)].astype(F32).reshape(peers * chunks, LANE)
    for s in range(CAP):
        for c in range(chunks):
            yield slice(s * peers, (s + 1) * peers), c, scr[s, pl.ds(c, peers, stride=chunks), :]


def expert_kernel(
    core_ref, got_hbm, wg_hbm, wu_hbm, down_hbm,
    part_hbm, keep_hbm, send_hbm,
    got, wg, wu, down, scr, rows, cot, own, other, keep, send, part, sems,
):
    sources = [
        (got_hbm.at[:, :, pl.ds(0, CAP * LANE)], got.at[0]),
        (got_hbm.at[:, :, pl.ds(CAP * LANE, CAP * LANE)], got.at[1]),
        (wg_hbm, wg),
        (wu_hbm, wu),
        (down_hbm, down),
    ]
    copies = [
        pltpu.make_async_copy(a, b, sems.at[i]) for i, (a, b) in enumerate(sources)
    ]
    for copy in copies:
        copy.start()
    peers, chunks, _ = part.shape
    first = core_ref[0] == 0
    copies[0].wait()
    for lines, c, value in to_rows(got.at[0], scr):
        rows[lines, lanes(c)] = value.astype(BF16)
    copies[2].wait()
    gate = mm(rows[...], wg[...])
    sig = jax.nn.sigmoid(gate)
    copies[3].wait()
    up = mm(rows[...], wu[...])
    hidden = (gate * sig * up).astype(BF16)
    copies[1].wait()
    even = None
    for lines, c, value in to_rows(got.at[1], scr):
        cot[lines, lanes(c)] = value.astype(BF16)
        if c % 2 == 0:
            even = value
        else:
            own[lines, lanes(c // 2)] = jnp.where(first, even, value).astype(BF16)
            other[lines, lanes(c // 2)] = jnp.where(first, value, even).astype(BF16)
    sent = []
    for i, (source, target, target_hbm) in enumerate(
        ((other, send, send_hbm), (own, keep, keep_hbm))
    ):
        for b in range(chunks // 2):
            target[b] = mm(source[:, lanes(b)], hidden, 0, 0).astype(BF16)
        copy = pltpu.make_async_copy(target, target_hbm, sems.at[5 + i])
        copy.start()
        sent.append(copy)
    copies[4].wait()
    grad = mm(cot[...], down[...])
    gate_grad = (grad * up * sig * (1.0 + gate * (1.0 - sig))).astype(BF16)
    up_grad = (grad * (gate * sig)).astype(BF16)
    for c in range(0, chunks, 2):
        at = lanes(c, 2)
        value = mm(gate_grad, wg[at, :], 1, 1) + mm(up_grad, wu[at, :], 1, 1)
        for s in range(CAP):
            for h in range(2):
                scr[s, pl.ds(c + h, peers, stride=chunks), :] = value[
                    s * peers : (s + 1) * peers, lanes(h)
                ]
    for s in range(CAP):
        part[:, :, lanes(s)] = scr[s].reshape(peers, chunks, LANE).astype(BF16)
    copy = pltpu.make_async_copy(part, part_hbm, sems.at[7])
    copy.start()
    sent.append(copy)
    for copy in sent:
        copy.wait()


def collect_kernel(peers, ids_ref, got_hbm, out_ref, got, scr, rows, sem):
    copy = pltpu.make_async_copy(got_hbm, got, sem)
    copy.start()
    placing = placing_of(ids_ref[...], peers)
    copy.wait()
    for lines, c, value in to_rows(got, scr):
        rows[lines, lanes(c)] = value.astype(BF16)
    out_ref[...] = mm(placing, rows[...], 0, 0).astype(BF16)


def call(kernel, out_shape, in_specs, out_specs, scratch, limit, flops, moved, name):
    return pl.pallas_call(
        kernel,
        out_shape=out_shape,
        in_specs=in_specs,
        out_specs=out_specs,
        scratch_shapes=scratch,
        compiler_params=pltpu.CompilerParams(vmem_limit_bytes=limit << 20),
        cost_estimate=pl.CostEstimate(flops=flops, bytes_accessed=moved, transcendentals=0),
        name=name,
    )


def reduce_features(keep, send):
    ranks = lax.axis_size("dp")
    chips = ranks // 2
    me = lax.axis_index("dp")
    z = me // 2
    step = 1 - 2 * (me % 2)
    swapped = lax.ppermute(send, "dp", [(d, d ^ 1) for d in range(ranks)])
    onward = [
        (d, (d // 2 + 1 - 2 * (d % 2)) % chips * 2 + d % 2) for d in range(ranks)
    ]

    def term(k):
        at = lax.rem(z - k * step + 2 * chips, chips)
        mine = lax.dynamic_index_in_dim(keep, at, 0, keepdims=False)
        theirs = lax.dynamic_index_in_dim(swapped, at, 0, keepdims=False)
        return mine.astype(F32) + theirs.astype(F32)

    total = term(1)
    for k in range(1, chips):
        arrived = lax.ppermute(total.astype(BF16), "dp", onward)
        total = term(k + 1) + arrived.astype(F32)
    return total


def on_device(tokens, cotangent, expert_ids, route_weight, w_gate, w_up, w_down):
    n, width = tokens.shape
    peers = lax.axis_size("expert")
    ranks = lax.axis_size("dp")
    hidden = w_gate.shape[2]
    chunks = width // LANE
    slots = CAP * peers
    product = 2 * slots * width * hidden
    core = (lax.axis_index("dp") % 2).astype(jnp.int32).reshape(1)
    ids = expert_ids.reshape(1, n)
    weight = route_weight.reshape(1, n)
    wg = w_gate.reshape(width, hidden)
    wu = w_up.reshape(width, hidden)
    full_down = lax.all_gather(w_down.reshape(width // ranks, hidden), "dp", axis=0, tiled=True)

    shape = jax.ShapeDtypeStruct
    packed = call(
        functools.partial(pack_kernel, peers),
        shape((peers, chunks, 2 * CAP * LANE), BF16),
        [VMEM, VMEM, HBM, HBM],
        HBM,
        [
            pltpu.VMEM((n, width), BF16),
            pltpu.VMEM((n, width), BF16),
            pltpu.VMEM((2, peers, chunks, CAP * LANE), BF16),
            pltpu.VMEM((2 * CAP, peers * chunks, LANE), F32),
            pltpu.SemaphoreType.DMA((4,)),
        ],
        58, 4 * slots * n * width, 4 << 20, "pack",
    )(ids, weight, tokens, cotangent)
    got = lax.all_to_all(packed, "expert", split_axis=0, concat_axis=0, tiled=True)

    part, keep, send = call(
        expert_kernel,
        (
            shape((peers, chunks, CAP * LANE), BF16),
            shape((chunks // 2, LANE, hidden), BF16),
            shape((chunks // 2, LANE, hidden), BF16),
        ),
        [SMEM, HBM, HBM, HBM, HBM],
        (HBM, HBM, HBM),
        [
            pltpu.VMEM((2, peers, chunks, CAP * LANE), BF16),
            pltpu.VMEM((width, hidden), BF16),
            pltpu.VMEM((width, hidden), BF16),
            pltpu.VMEM((width, hidden), BF16),
            pltpu.VMEM((CAP, peers * chunks, LANE), F32),
            pltpu.VMEM((slots, width), BF16),
            pltpu.VMEM((slots, width), BF16),
            pltpu.VMEM((slots, width // 2), BF16),
            pltpu.VMEM((slots, width // 2), BF16),
            pltpu.VMEM((chunks // 2, LANE, hidden), BF16),
            pltpu.VMEM((chunks // 2, LANE, hidden), BF16),
            pltpu.VMEM((peers, chunks, CAP * LANE), BF16),
            pltpu.SemaphoreType.DMA((8,)),
        ],
        48, 6 * product, 16 << 20, "expert",
    )(core, got, wg, wu, full_down)

    down_part = reduce_features(keep, send)
    returned = lax.all_to_all(part, "expert", split_axis=0, concat_axis=0, tiled=True)

    token_grad = call(
        functools.partial(collect_kernel, peers),
        shape((n, width), BF16),
        [VMEM, HBM],
        VMEM,
        [
            pltpu.VMEM((peers, chunks, CAP * LANE), BF16),
            pltpu.VMEM((CAP, peers * chunks, LANE), F32),
            pltpu.VMEM((slots, width), BF16),
            pltpu.SemaphoreType.DMA,
        ],
        16, 2 * slots * n * width, 2 << 20, "collect",
    )(ids, returned)
    return (token_grad, down_part.reshape(w_down.shape))


def solution(mesh):
    in_specs = (
        P(("expert", "dp"), None),
        P(("expert", "dp"), None),
        P(("expert", "dp"), None),
        P(("expert", "dp"), None),
        P("expert", None, None),
        P("expert", None, None),
        P("dp", "expert", None),
    )
    out_specs = (P(("expert", "dp"), None), P("dp", "expert", None))
    return jax.shard_map(
        on_device, mesh=mesh, in_specs=in_specs, out_specs=out_specs, check_vma=False
    )
```

time: 189 us -> 171 us (0.905)
  blocking collectives: 35.6 us -> 0 us
  matrix products: 26.2 us -> 0 us
  waiting for transfers between devices: 65.6 us -> 90.8 us
  local copies, waits for them, and re-layouts: 18.5 us -> 1.16 us
  starting transfers between devices: 26.1 us -> 42.9 us
  Pallas kernels: 0 us -> 15.8 us
  other arithmetic: 1.62 us -> 5.22 us
    ppermute x0 -> x8, waiting for transfers between devices: none -> 49.4 us  [the longest x7 46.1 us: reduce_features(): arrived = lax.ppermute(total.astype(BF16), 'dp', onward)]
    all_to_all x1 -> x0, blocking collectives: 35.6 us -> none  [on_device(): lax.all_to_all(token_part.reshape(slot_count, width), 'expert', split_axi...]
    unnamed x3 -> x1, waiting for transfers between devices: 27.1 us -> 0.68 us
    dot_general x10 -> x0, matrix products: 26.2 us -> none  [the longest x1 4.86 us: on_device(): jnp.einsum('ilcd,ilcf->dlf', cot_four, hidden, preferred_element_type=jnp...]
    pallas_call x0 -> x3, Pallas kernels: none -> 15.8 us  [the longest x1 9.81 us: on_device(): call(expert_kernel, (shape((peers, chunks, CAP * LANE), BF16), shape((chu...]
    ppermute x0 -> x8, starting transfers between devices: none -> 15.8 us  [the longest x7 13.6 us: reduce_features(): arrived = lax.ppermute(total.astype(BF16), 'dp', onward)]
    all_to_all x3 -> x0, local copies, waits for them, and re-layouts: 9.74 us -> none  [the longest x1 3.28 us: on_device(): lax.all_to_all(sent_cot, 'expert', split_axis=0, concat_axis=0, tiled=True)]
    unnamed x15 -> x5, local copies, waits for them, and re-layouts: 8.08 us -> 1.16 us
  transfers between devices with their start and end apart: 4 -> 11, of which waited for: 3 -> 9; matrix products, arithmetic and copies ran while one was open for 17% -> 2% of each run, Pallas kernels for 0% -> 4%
where the time goes in v1:
time: 171 us; the launch traced here: 170 us
  waiting for transfers between devices  90.8 us (53%)
  starting transfers between devices  42.9 us (25%)
  Pallas kernels  15.8 us (9%)
  between operations  14.4 us (8%)
  other arithmetic  5.22 us (3%)
    ppermute x7, waiting for transfers between devices, reduce_features(): arrived = lax.ppermute(total.astype(BF16), 'dp', onward)  46.1 us
    all_to_all x1, waiting for transfers between devices, on_device(): lax.all_to_all(packed, 'expert', split_axis=0, concat_axis=0, tiled=True)  35.9 us
    all_to_all x1, starting transfers between devices, on_device(): lax.all_to_all(packed, 'expert', split_axis=0, concat_axis=0, tiled=True)  17.5 us
    ppermute x7, starting transfers between devices, reduce_features(): arrived = lax.ppermute(total.astype(BF16), 'dp', onward)  13.6 us
    pallas_call x1, Pallas kernels, on_device(): call(expert_kernel, (shape((peers, chunks, CAP * LANE), BF16), shape((chu...  9.81 us
    all_to_all x1, starting transfers between devices, on_device(): lax.all_to_all(part, 'expert', split_axis=0, concat_axis=0, tiled=True)  9.66 us
    all_gather x1, waiting for transfers between devices, on_device(): lax.all_gather(w_down.reshape(width // ranks, hidden), 'dp', axis=0, tile...  4.83 us
    convert_element_type x7, other arithmetic, reduce_features(): arrived = lax.ppermute(total.astype(BF16), 'dp', onward)  4.23 us
  transfers between devices with their start and end apart: 11, of which 9 were waited for; matrix products, arithmetic and copies ran while one was open for 2% of the time, Pallas kernels for 4%

profile of v1, /device:TPU:14, one launch (start us, length us, event | category | flops | bytes accessed | tf_op | source)
XLA Modules:
  0.0 170.3 jit_solution(17049184318847735824)
XLA Ops:
  7.9 4.1 %pack.1 = bf16[64,16,768]{2,1,0:T(8,128)(2,1)} custom-call(s32[1,128]{1,0:T(1,128)} %bitcast.38, f32[1,128]{1,0:T(1,128)} %bitcast.40, bf16[128,2048]{1,0:T(8,128)(2,1)} %tok_hbm.1, bf16[128,2048]{1,0:T(8,128)(2,1)} %cot_hbm.1), custom_call_target="tpu_custom_call" | custom-call | flops 201326592 | bytes 4194304 | tf_op jit(solution)/shard_map/pack/pallas_call | solution.py:224
  12.1 17.5 %all-to-all-start = ((bf16[64,16,768]{2,1,0:T(8,128)(2,1)}), bf16[64,16,768]{2,1,0:T(8,128)(2,1)S(1)}, u32[]{:S(2)}, u32[]{:S(2)}) async-start(bf16[64,16,768]{2,1,0:T(8,128)(2,1)} %pack.1), calls=%async_computation | async-start | bytes 3145728 | tf_op jit(solution)/shard_map/all_to_all | solution.py:238
  29.6 35.9 %all-to-all-done.got_hbm = bf16[64,16,768]{2,1,0:T(8,128)(2,1)S(1)} async-done(((bf16[64,16,768]{2,1,0:T(8,128)(2,1)}), bf16[64,16,768]{2,1,0:T(8,128)(2,1)S(1)}, u32[]{:S(2)}, u32[]{:S(2)}) %all-to-all-start) | async-done | bytes 1572896 | tf_op jit(solution)/shard_map/all_to_all | solution.py:238
  65.5 4.8 %all-gather.3.cloned.1.call-done = bf16[2048,1,768]{2,0,1:T(8,128)(2,1)} async-done(((bf16[128,1,768]{2,0,1:T(8,128)(2,1)}), bf16[2048,1,768]{2,0,1:T(8,128)(2,1)}) %all-gather.3.cloned.1.call-update) | async-done | bytes 3145744 | tf_op jit(solution)/shard_map/all_gather | solution.py:221
  70.3 9.8 %expert.1 = (bf16[64,16,384]{2,1,0:T(8,128)(2,1)}, bf16[8,128,768]{2,1,0:T(8,128)(2,1)S(1)}, bf16[8,128,768]{2,1,0:T(8,128)(2,1)}) custom-call(s32[1]{0:T(128)} %bitcast.1.core_ref, bf16[64,16,768]{2,1,0:T(8,128)(2,1)S(1)} %all-to-all-done.got_hbm, bf16[2048,768]{1,0:T(8,128)(2,1)} %bitcast.41, bf16[2048,768]{1,0:T(8,128)(2,1)} %bitcast.42, ...), custom_call_target="tpu_custom_call" | custom-call | flops 3623878656 | bytes 16777216 | tf_op jit(solution)/shard_map/expert/pallas_call | solution.py:240
  80.1 2.2 %collective-permute-start = (bf16[8,128,768]{2,1,0:T(8,128)(2,1)}, bf16[8,128,768]{2,1,0:T(8,128)(2,1)S(1)}, u32[]{:S(2)}, u32[]{:S(2)}) collective-permute-start(bf16[8,128,768]{2,1,0:T(8,128)(2,1)} %get-tuple-element.7), channel_id=1, source_target_pairs={{0,1},{1,0},{2,3},{3,2},{4,5},{5,4},{6,7},{7,6},{8,9},{9,8},{10,11... | collective-permute-start | bytes 4718600 | tf_op jit(solution)/shard_map/ppermute | solution.py:190
  82.3 3.3 %collective-permute-done = bf16[8,128,768]{2,1,0:T(8,128)(2,1)S(1)} collective-permute-done((bf16[8,128,768]{2,1,0:T(8,128)(2,1)}, bf16[8,128,768]{2,1,0:T(8,128)(2,1)S(1)}, u32[]{:S(2)}, u32[]{:S(2)}) %collective-permute-start) | collective-permute-done | bytes 1572896 | tf_op jit(solution)/shard_map/ppermute | solution.py:190
  85.7 2.1 %collective-permute-start.1 = (bf16[128,768]{1,0:T(8,128)(2,1)S(1)}, bf16[128,768]{1,0:T(8,128)(2,1)S(1)}, u32[]{:S(2)}, u32[]{:S(2)}) collective-permute-start(bf16[128,768]{1,0:T(8,128)(2,1)S(1)} %fusion.7), channel_id=1, source_target_pairs={{0,2},{1,15},{2,4},{3,1},{4,6},{5,3},{6,8},{7,5},{8,10},{9,7},{10,... | collective-permute-start | bytes 589832 | tf_op jit(solution)/shard_map/ppermute | solution.py:203
  87.8 13.8 %collective-permute-done.1 = bf16[128,768]{1,0:T(8,128)(2,1)S(1)} collective-permute-done((bf16[128,768]{1,0:T(8,128)(2,1)S(1)}, bf16[128,768]{1,0:T(8,128)(2,1)S(1)}, u32[]{:S(2)}, u32[]{:S(2)}) %collective-permute-start.1) | collective-permute-done | bytes 196640 | tf_op jit(solution)/shard_map/ppermute | solution.py:203
  101.7 1.9 %collective-permute-start.2 = (bf16[128,768]{1,0:T(8,128)(2,1)S(1)}, bf16[128,768]{1,0:T(8,128)(2,1)S(1)}, u32[]{:S(2)}, u32[]{:S(2)}) collective-permute-start(bf16[128,768]{1,0:T(8,128)(2,1)S(1)} %fusion), channel_id=1, source_target_pairs={{0,2},{1,15},{2,4},{3,1},{4,6},{5,3},{6,8},{7,5},{8,10},{9,7},{10,... | collective-permute-start | bytes 589832 | tf_op jit(solution)/shard_map/ppermute | solution.py:203
  103.7 6.8 %collective-permute-done.2 = bf16[128,768]{1,0:T(8,128)(2,1)S(1)} collective-permute-done((bf16[128,768]{1,0:T(8,128)(2,1)S(1)}, bf16[128,768]{1,0:T(8,128)(2,1)S(1)}, u32[]{:S(2)}, u32[]{:S(2)}) %collective-permute-start.2) | collective-permute-done | bytes 196640 | tf_op jit(solution)/shard_map/ppermute | solution.py:203
  110.6 1.9 %collective-permute-start.3 = (bf16[128,768]{1,0:T(8,128)(2,1)S(1)}, bf16[128,768]{1,0:T(8,128)(2,1)S(1)}, u32[]{:S(2)}, u32[]{:S(2)}) collective-permute-start(bf16[128,768]{1,0:T(8,128)(2,1)S(1)} %fusion.1), channel_id=1, source_target_pairs={{0,2},{1,15},{2,4},{3,1},{4,6},{5,3},{6,8},{7,5},{8,10},{9,7},{10,... | collective-permute-start | bytes 589832 | tf_op jit(solution)/shard_map/ppermute | solution.py:203
  112.5 9.7 %all-to-all-start.1 = ((bf16[64,16,384]{2,1,0:T(8,128)(2,1)}), bf16[64,16,384]{2,1,0:T(8,128)(2,1)S(1)}, u32[]{:S(2)}, u32[]{:S(2)}) async-start(bf16[64,16,384]{2,1,0:T(8,128)(2,1)} %get-tuple-element.5), calls=%async_computation.1 | async-start | bytes 1572864 | tf_op jit(solution)/shard_map/all_to_all | solution.py:268
  122.2 1.0 fusion.2
  123.2 1.9 %collective-permute-start.4 = (bf16[128,768]{1,0:T(8,128)(2,1)S(1)}, bf16[128,768]{1,0:T(8,128)(2,1)S(1)}, u32[]{:S(2)}, u32[]{:S(2)}) collective-permute-start(bf16[128,768]{1,0:T(8,128)(2,1)S(1)} %fusion.2), channel_id=1, source_target_pairs={{0,2},{1,15},{2,4},{3,1},{4,6},{5,3},{6,8},{7,5},{8,10},{9,7},{10,... | collective-permute-start | bytes 589832 | tf_op jit(solution)/shard_map/ppermute | solution.py:203
  125.2 6.8 %collective-permute-done.4 = bf16[128,768]{1,0:T(8,128)(2,1)S(1)} collective-permute-done((bf16[128,768]{1,0:T(8,128)(2,1)S(1)}, bf16[128,768]{1,0:T(8,128)(2,1)S(1)}, u32[]{:S(2)}, u32[]{:S(2)}) %collective-permute-start.4) | collective-permute-done | bytes 196640 | tf_op jit(solution)/shard_map/ppermute | solution.py:203
  133.0 1.9 %collective-permute-start.5 = (bf16[128,768]{1,0:T(8,128)(2,1)S(1)}, bf16[128,768]{1,0:T(8,128)(2,1)S(1)}, u32[]{:S(2)}, u32[]{:S(2)}) collective-permute-start(bf16[128,768]{1,0:T(8,128)(2,1)S(1)} %fusion.3), channel_id=1, source_target_pairs={{0,2},{1,15},{2,4},{3,1},{4,6},{5,3},{6,8},{7,5},{8,10},{9,7},{10,... | collective-permute-start | bytes 589832 | tf_op jit(solution)/shard_map/ppermute | solution.py:203
  134.9 6.8 %collective-permute-done.5 = bf16[128,768]{1,0:T(8,128)(2,1)S(1)} collective-permute-done((bf16[128,768]{1,0:T(8,128)(2,1)S(1)}, bf16[128,768]{1,0:T(8,128)(2,1)S(1)}, u32[]{:S(2)}, u32[]{:S(2)}) %collective-permute-start.5) | collective-permute-done | bytes 196640 | tf_op jit(solution)/shard_map/ppermute | solution.py:203
  142.8 1.9 %collective-permute-start.6 = (bf16[128,768]{1,0:T(8,128)(2,1)S(1)}, bf16[128,768]{1,0:T(8,128)(2,1)S(1)}, u32[]{:S(2)}, u32[]{:S(2)}) collective-permute-start(bf16[128,768]{1,0:T(8,128)(2,1)S(1)} %fusion.4), channel_id=1, source_target_pairs={{0,2},{1,15},{2,4},{3,1},{4,6},{5,3},{6,8},{7,5},{8,10},{9,7},{10,... | collective-permute-start | bytes 589832 | tf_op jit(solution)/shard_map/ppermute | solution.py:203
  144.7 6.8 %collective-permute-done.6 = bf16[128,768]{1,0:T(8,128)(2,1)S(1)} collective-permute-done((bf16[128,768]{1,0:T(8,128)(2,1)S(1)}, bf16[128,768]{1,0:T(8,128)(2,1)S(1)}, u32[]{:S(2)}, u32[]{:S(2)}) %collective-permute-start.6) | collective-permute-done | bytes 196640 | tf_op jit(solution)/shard_map/ppermute | solution.py:203
  152.6 1.9 %collective-permute-start.7 = (bf16[128,768]{1,0:T(8,128)(2,1)S(1)}, bf16[128,768]{1,0:T(8,128)(2,1)S(1)}, u32[]{:S(2)}, u32[]{:S(2)}) collective-permute-start(bf16[128,768]{1,0:T(8,128)(2,1)S(1)} %fusion.5), channel_id=1, source_target_pairs={{0,2},{1,15},{2,4},{3,1},{4,6},{5,3},{6,8},{7,5},{8,10},{9,7},{10,... | collective-permute-start | bytes 589832 | tf_op jit(solution)/shard_map/ppermute | solution.py:203
  154.5 1.9 %collect.1 = bf16[128,2048]{1,0:T(8,128)(2,1)} custom-call(s32[1,128]{1,0:T(1,128)S(1)} %bitcast.39, bf16[64,16,384]{2,1,0:T(8,128)(2,1)S(1)} %all-to-all-done.1.got_hbm), custom_call_target="tpu_custom_call" | custom-call | flops 100663296 | bytes 2097152 | tf_op jit(solution)/shard_map/collect/pallas_call | solution.py:270
  156.4 4.9 %collective-permute-done.7 = bf16[128,768]{1,0:T(8,128)(2,1)S(1)} collective-permute-done((bf16[128,768]{1,0:T(8,128)(2,1)S(1)}, bf16[128,768]{1,0:T(8,128)(2,1)S(1)}, u32[]{:S(2)}, u32[]{:S(2)}) %collective-permute-start.7) | collective-permute-done | bytes 196640 | tf_op jit(solution)/shard_map/ppermute | solution.py:203
  162.3 1.2 copy.9
  (15 shorter events, 4.9 us)
Async XLA Ops:
  7.2 63.1 %all-gather.3.cloned.1.call-start = ((), (), s32[]{:S(2)}) async-start(), calls=%async_computation.2 | async-start | bytes 3342336 | tf_op jit(solution)/shard_map/all_gather | solution.py:221
  12.1 53.4 %all-to-all-start = ((bf16[64,16,768]{2,1,0:T(8,128)(2,1)}), bf16[64,16,768]{2,1,0:T(8,128)(2,1)S(1)}, u32[]{:S(2)}, u32[]{:S(2)}) async-start(bf16[64,16,768]{2,1,0:T(8,128)(2,1)} %pack.1), calls=%async_computation | async-start | bytes 3145728 | tf_op jit(solution)/shard_map/all_to_all | solution.py:238
  80.1 5.5 %collective-permute-start = (bf16[8,128,768]{2,1,0:T(8,128)(2,1)}, bf16[8,128,768]{2,1,0:T(8,128)(2,1)S(1)}, u32[]{:S(2)}, u32[]{:S(2)}) collective-permute-start(bf16[8,128,768]{2,1,0:T(8,128)(2,1)} %get-tuple-element.7), channel_id=1, source_target_pairs={{0,1},{1,0},{2,3},{3,2},{4,5},{5,4},{6,7},{7,6},{8,9},{9,8},{10,11... | collective-permute-start | bytes 4718600 | tf_op jit(solution)/shard_map/ppermute | solution.py:190
  85.6 26.9 %copy-start.1 = (bf16[8,128,768]{2,1,0:T(8,128)(2,1)}, bf16[8,128,768]{2,1,0:T(8,128)(2,1)S(1)}, u32[]{:S(2)}) copy-start(bf16[8,128,768]{2,1,0:T(8,128)(2,1)S(1)} %collective-permute-done) | copy-start | bytes 4718596
  85.7 16.0 %collective-permute-start.1 = (bf16[128,768]{1,0:T(8,128)(2,1)S(1)}, bf16[128,768]{1,0:T(8,128)(2,1)S(1)}, u32[]{:S(2)}, u32[]{:S(2)}) collective-permute-start(bf16[128,768]{1,0:T(8,128)(2,1)S(1)} %fusion.7), channel_id=1, source_target_pairs={{0,2},{1,15},{2,4},{3,1},{4,6},{5,3},{6,8},{7,5},{8,10},{9,7},{10,... | collective-permute-start | bytes 589832 | tf_op jit(solution)/shard_map/ppermute | solution.py:203
  101.7 8.8 %collective-permute-start.2 = (bf16[128,768]{1,0:T(8,128)(2,1)S(1)}, bf16[128,768]{1,0:T(8,128)(2,1)S(1)}, u32[]{:S(2)}, u32[]{:S(2)}) collective-permute-start(bf16[128,768]{1,0:T(8,128)(2,1)S(1)} %fusion), channel_id=1, source_target_pairs={{0,2},{1,15},{2,4},{3,1},{4,6},{5,3},{6,8},{7,5},{8,10},{9,7},{10,... | collective-permute-start | bytes 589832 | tf_op jit(solution)/shard_map/ppermute | solution.py:203
  110.6 11.6 %collective-permute-start.3 = (bf16[128,768]{1,0:T(8,128)(2,1)S(1)}, bf16[128,768]{1,0:T(8,128)(2,1)S(1)}, u32[]{:S(2)}, u32[]{:S(2)}) collective-permute-start(bf16[128,768]{1,0:T(8,128)(2,1)S(1)} %fusion.1), channel_id=1, source_target_pairs={{0,2},{1,15},{2,4},{3,1},{4,6},{5,3},{6,8},{7,5},{8,10},{9,7},{10,... | collective-permute-start | bytes 589832 | tf_op jit(solution)/shard_map/ppermute | solution.py:203
  112.5 42.0 %all-to-all-start.1 = ((bf16[64,16,384]{2,1,0:T(8,128)(2,1)}), bf16[64,16,384]{2,1,0:T(8,128)(2,1)S(1)}, u32[]{:S(2)}, u32[]{:S(2)}) async-start(bf16[64,16,384]{2,1,0:T(8,128)(2,1)} %get-tuple-element.5), calls=%async_computation.1 | async-start | bytes 1572864 | tf_op jit(solution)/shard_map/all_to_all | solution.py:268
  122.2 32.3 %copy-start = (s32[128,1]{0,1:T(1,128)S(1)}, s32[128,1]{0,1:T(1,128)}, u32[]{:S(2)}) copy-start(s32[128,1]{0,1:T(1,128)} %param.9) | copy-start | bytes 1540
  123.2 8.8 %collective-permute-start.4 = (bf16[128,768]{1,0:T(8,128)(2,1)S(1)}, bf16[128,768]{1,0:T(8,128)(2,1)S(1)}, u32[]{:S(2)}, u32[]{:S(2)}) collective-permute-start(bf16[128,768]{1,0:T(8,128)(2,1)S(1)} %fusion.2), channel_id=1, source_target_pairs={{0,2},{1,15},{2,4},{3,1},{4,6},{5,3},{6,8},{7,5},{8,10},{9,7},{10,... | collective-permute-start | bytes 589832 | tf_op jit(solution)/shard_map/ppermute | solution.py:203
  133.0 8.8 %collective-permute-start.5 = (bf16[128,768]{1,0:T(8,128)(2,1)S(1)}, bf16[128,768]{1,0:T(8,128)(2,1)S(1)}, u32[]{:S(2)}, u32[]{:S(2)}) collective-permute-start(bf16[128,768]{1,0:T(8,128)(2,1)S(1)} %fusion.3), channel_id=1, source_target_pairs={{0,2},{1,15},{2,4},{3,1},{4,6},{5,3},{6,8},{7,5},{8,10},{9,7},{10,... | collective-permute-start | bytes 589832 | tf_op jit(solution)/shard_map/ppermute | solution.py:203
  142.8 8.8 %collective-permute-start.6 = (bf16[128,768]{1,0:T(8,128)(2,1)S(1)}, bf16[128,768]{1,0:T(8,128)(2,1)S(1)}, u32[]{:S(2)}, u32[]{:S(2)}) collective-permute-start(bf16[128,768]{1,0:T(8,128)(2,1)S(1)} %fusion.4), channel_id=1, source_target_pairs={{0,2},{1,15},{2,4},{3,1},{4,6},{5,3},{6,8},{7,5},{8,10},{9,7},{10,... | collective-permute-start | bytes 589832 | tf_op jit(solution)/shard_map/ppermute | solution.py:203
  152.6 8.8 %collective-permute-start.7 = (bf16[128,768]{1,0:T(8,128)(2,1)S(1)}, bf16[128,768]{1,0:T(8,128)(2,1)S(1)}, u32[]{:S(2)}, u32[]{:S(2)}) collective-permute-start(bf16[128,768]{1,0:T(8,128)(2,1)S(1)} %fusion.5), channel_id=1, source_target_pairs={{0,2},{1,15},{2,4},{3,1},{4,6},{5,3},{6,8},{7,5},{8,10},{9,7},{10,... | collective-permute-start | bytes 589832 | tf_op jit(solution)/shard_map/ppermute | solution.py:203
Sparse Core Ops, SparseCore 0:
  10.7 59.5 all-gather.2

commit v2 on v1

--- a/solution.py
+++ b/solution.py
@@ -5,7 +5,7 @@
 from jax import lax
 from jax.experimental import pallas as pl
 from jax.experimental.pallas import tpu as pltpu
-from jax.sharding import PartitionSpec as P
+from jax.sharding import Mesh, PartitionSpec as P
 
 CAP = 3
 LANE = 128
@@ -91,56 +91,85 @@
             yield slice(s * peers, (s + 1) * peers), c, scr[s, pl.ds(c, peers, stride=chunks), :]
 
 
-def expert_kernel(
-    core_ref, got_hbm, wg_hbm, wu_hbm, down_hbm,
-    part_hbm, keep_hbm, send_hbm,
-    got, wg, wu, down, scr, rows, cot, own, other, keep, send, part, sems,
-):
-    sources = [
-        (got_hbm.at[:, :, pl.ds(0, CAP * LANE)], got.at[0]),
-        (got_hbm.at[:, :, pl.ds(CAP * LANE, CAP * LANE)], got.at[1]),
-        (wg_hbm, wg),
-        (wu_hbm, wu),
-        (down_hbm, down),
-    ]
+def start_all(pairs, sems, base=0):
     copies = [
-        pltpu.make_async_copy(a, b, sems.at[i]) for i, (a, b) in enumerate(sources)
+        pltpu.make_async_copy(source, target, sems.at[base + i])
+        for i, (source, target) in enumerate(pairs)
     ]
     for copy in copies:
         copy.start()
-    peers, chunks, _ = part.shape
-    first = core_ref[0] == 0
+    return copies
+
+
+def forward_kernel(
+    got_hbm, wg_hbm, wu_hbm,
+    terms_hbm, gate_hbm, up_hbm, cot_hbm,
+    got, wg, wu, scr, rows, cot, gate, up, terms, sems,
+):
+    copies = start_all(
+        [
+            (got_hbm.at[:, :, pl.ds(0, CAP * LANE)], got.at[0]),
+            (wg_hbm, wg),
+            (wu_hbm, wu),
+            (got_hbm.at[:, :, pl.ds(CAP * LANE, CAP * LANE)], got.at[1]),
+        ],
+        sems,
+    )
+    chunks = got.shape[2]
     copies[0].wait()
     for lines, c, value in to_rows(got.at[0], scr):
         rows[lines, lanes(c)] = value.astype(BF16)
+    copies[1].wait()
+    gate_value = mm(rows[...], wg[...])
+    gate[...] = gate_value
     copies[2].wait()
-    gate = mm(rows[...], wg[...])
-    sig = jax.nn.sigmoid(gate)
+    up_value = mm(rows[...], wu[...])
+    up[...] = up_value
+    hidden = (gate_value * jax.nn.sigmoid(gate_value) * up_value).astype(BF16)
+    sent = start_all([(gate, gate_hbm), (up, up_hbm)], sems, 4)
     copies[3].wait()
-    up = mm(rows[...], wu[...])
-    hidden = (gate * sig * up).astype(BF16)
-    copies[1].wait()
-    even = None
     for lines, c, value in to_rows(got.at[1], scr):
         cot[lines, lanes(c)] = value.astype(BF16)
-        if c % 2 == 0:
-            even = value
-        else:
-            own[lines, lanes(c // 2)] = jnp.where(first, even, value).astype(BF16)
-            other[lines, lanes(c // 2)] = jnp.where(first, value, even).astype(BF16)
-    sent = []
-    for i, (source, target, target_hbm) in enumerate(
-        ((other, send, send_hbm), (own, keep, keep_hbm))
-    ):
-        for b in range(chunks // 2):
-            target[b] = mm(source[:, lanes(b)], hidden, 0, 0).astype(BF16)
-        copy = pltpu.make_async_copy(target, target_hbm, sems.at[5 + i])
-        copy.start()
-        sent.append(copy)
+    sent += start_all([(cot, cot_hbm)], sems, 6)
+    half = chunks // 2 * LANE
+    for part in range(2):
+        for b in range(part * chunks // 2, (part + 1) * chunks // 2, 2):
+            at = lanes(b, 2)
+            terms[at, :] = mm(cot[:, at], hidden, 0, 0).astype(BF16)
+        at = pl.ds(part * half, half)
+        sent += start_all([(terms.at[at, :], terms_hbm.at[at, :])], sems, 7 + part)
+    for copy in sent:
+        copy.wait()
+
+
+def backward_kernel(
+    gate_hbm, up_hbm, cot_hbm, down_hbm, wg_hbm, wu_hbm,
+    part_hbm,
+    gate, up, cot, down, wg, wu, scr, part, sems,
+):
+    copies = start_all(
+        [
+            (cot_hbm, cot),
+            (down_hbm, down),
+            (gate_hbm, gate),
+            (up_hbm, up),
+            (wg_hbm, wg),
+            (wu_hbm, wu),
+        ],
+        sems,
+    )
+    peers, chunks, _ = part.shape
+    copies[0].wait()
+    copies[1].wait()
+    grad = mm(cot[...], down[...])
+    copies[2].wait()
+    copies[3].wait()
+    v = gate[...]
+    sig = jax.nn.sigmoid(v)
+    gate_grad = (grad * up[...] * sig * (1.0 + v * (1.0 - sig))).astype(BF16)
+    up_grad = (grad * (v * sig)).astype(BF16)
     copies[4].wait()
-    grad = mm(cot[...], down[...])
-    gate_grad = (grad * up * sig * (1.0 + gate * (1.0 - sig))).astype(BF16)
-    up_grad = (grad * (gate * sig)).astype(BF16)
+    copies[5].wait()
     for c in range(0, chunks, 2):
         at = lanes(c, 2)
         value = mm(gate_grad, wg[at, :], 1, 1) + mm(up_grad, wu[at, :], 1, 1)
@@ -151,10 +180,7 @@
                 ]
     for s in range(CAP):
         part[:, :, lanes(s)] = scr[s].reshape(peers, chunks, LANE).astype(BF16)
-    copy = pltpu.make_async_copy(part, part_hbm, sems.at[7])
-    copy.start()
-    sent.append(copy)
-    for copy in sent:
+    for copy in start_all([(part, part_hbm)], sems, 6):
         copy.wait()
 
 
@@ -181,44 +207,29 @@
     )
 
 
-def reduce_features(keep, send):
-    ranks = lax.axis_size("dp")
-    chips = ranks // 2
-    me = lax.axis_index("dp")
-    z = me // 2
-    step = 1 - 2 * (me % 2)
-    swapped = lax.ppermute(send, "dp", [(d, d ^ 1) for d in range(ranks)])
-    onward = [
-        (d, (d // 2 + 1 - 2 * (d % 2)) % chips * 2 + d % 2) for d in range(ranks)
-    ]
-
-    def term(k):
-        at = lax.rem(z - k * step + 2 * chips, chips)
-        mine = lax.dynamic_index_in_dim(keep, at, 0, keepdims=False)
-        theirs = lax.dynamic_index_in_dim(swapped, at, 0, keepdims=False)
-        return mine.astype(F32) + theirs.astype(F32)
-
-    total = term(1)
-    for k in range(1, chips):
-        arrived = lax.ppermute(total.astype(BF16), "dp", onward)
-        total = term(k + 1) + arrived.astype(F32)
-    return total
+def reduce_features(terms):
+    over_z = lax.psum_scatter(terms, "z", scatter_dimension=0, tiled=True)
+    both = over_z.reshape(2, LANE, terms.shape[1])
+    core = lax.axis_index("core")
+    mine = lax.dynamic_index_in_dim(both, core, 0, keepdims=False)
+    other = lax.dynamic_index_in_dim(both, 1 - core, 0, keepdims=False)
+    arrived = lax.ppermute(other, "core", [(0, 1), (1, 0)])
+    return mine.astype(F32) + arrived.astype(F32)
 
 
 def on_device(tokens, cotangent, expert_ids, route_weight, w_gate, w_up, w_down):
     n, width = tokens.shape
     peers = lax.axis_size("expert")
-    ranks = lax.axis_size("dp")
+    ranks = lax.axis_size("z") * 2
     hidden = w_gate.shape[2]
     chunks = width // LANE
     slots = CAP * peers
     product = 2 * slots * width * hidden
-    core = (lax.axis_index("dp") % 2).astype(jnp.int32).reshape(1)
     ids = expert_ids.reshape(1, n)
     weight = route_weight.reshape(1, n)
     wg = w_gate.reshape(width, hidden)
     wu = w_up.reshape(width, hidden)
-    full_down = lax.all_gather(w_down.reshape(width // ranks, hidden), "dp", axis=0, tiled=True)
+    full_down = lax.all_gather(w_down.reshape(width // ranks, hidden), ("z", "core"), axis=0, tiled=True)
 
     shape = jax.ShapeDtypeStruct
     packed = call(
@@ -237,34 +248,53 @@
     )(ids, weight, tokens, cotangent)
     got = lax.all_to_all(packed, "expert", split_axis=0, concat_axis=0, tiled=True)
 
-    part, keep, send = call(
-        expert_kernel,
+    weights = pltpu.VMEM((width, hidden), BF16)
+    inner = pltpu.VMEM((slots, hidden), F32)
+    terms, gate, up, cot = call(
+        forward_kernel,
         (
-            shape((peers, chunks, CAP * LANE), BF16),
-            shape((chunks // 2, LANE, hidden), BF16),
-            shape((chunks // 2, LANE, hidden), BF16),
+            shape((width, hidden), BF16),
+            shape((slots, hidden), F32),
+            shape((slots, hidden), F32),
+            shape((slots, width), BF16),
         ),
-        [SMEM, HBM, HBM, HBM, HBM],
-        (HBM, HBM, HBM),
+        [HBM] * 3,
+        (HBM,) * 4,
         [
             pltpu.VMEM((2, peers, chunks, CAP * LANE), BF16),
-            pltpu.VMEM((width, hidden), BF16),
-            pltpu.VMEM((width, hidden), BF16),
-            pltpu.VMEM((width, hidden), BF16),
+            weights,
+            weights,
             pltpu.VMEM((CAP, peers * chunks, LANE), F32),
             pltpu.VMEM((slots, width), BF16),
             pltpu.VMEM((slots, width), BF16),
-            pltpu.VMEM((slots, width // 2), BF16),
-            pltpu.VMEM((slots, width // 2), BF16),
-            pltpu.VMEM((chunks // 2, LANE, hidden), BF16),
-            pltpu.VMEM((chunks // 2, LANE, hidden), BF16),
+            inner,
+            inner,
+            weights,
+            pltpu.SemaphoreType.DMA((9,)),
+        ],
+        48, 3 * product, 14 << 20, "forward",
+    )(got, wg, wu)
+
+    part = call(
+        backward_kernel,
+        shape((peers, chunks, CAP * LANE), BF16),
+        [HBM] * 6,
+        HBM,
+        [
+            inner,
+            inner,
+            pltpu.VMEM((slots, width), BF16),
+            weights,
+            weights,
+            weights,
+            pltpu.VMEM((CAP, peers * chunks, LANE), F32),
             pltpu.VMEM((peers, chunks, CAP * LANE), BF16),
-            pltpu.SemaphoreType.DMA((8,)),
-        ],
-        48, 6 * product, 16 << 20, "expert",
-    )(core, got, wg, wu, full_down)
-
-    down_part = reduce_features(keep, send)
+            pltpu.SemaphoreType.DMA((7,)),
+        ],
+        58, 3 * product, 14 << 20, "backward",
+    )(gate, up, cot, full_down, wg, wu)
+
+    down_part = reduce_features(terms)
     returned = lax.all_to_all(part, "expert", split_axis=0, concat_axis=0, tiled=True)
 
     token_grad = call(
@@ -284,16 +314,17 @@
 
 
 def solution(mesh):
-    in_specs = (
-        P(("expert", "dp"), None),
-        P(("expert", "dp"), None),
-        P(("expert", "dp"), None),
-        P(("expert", "dp"), None),
-        P("expert", None, None),
-        P("expert", None, None),
-        P("dp", "expert", None),
-    )
-    out_specs = (P(("expert", "dp"), None), P("dp", "expert", None))
+    ranks = mesh.shape["dp"]
+    split = Mesh(
+        mesh.devices.reshape(mesh.shape["expert"], ranks // 2, 2), ("expert", "z", "core")
+    )
+    tokens = P(("expert", "z", "core"), None)
+    experts = P("expert", None, None)
+    features = P(("z", "core"), "expert", None)
     return jax.shard_map(
-        on_device, mesh=mesh, in_specs=in_specs, out_specs=out_specs, check_vma=False
-    )
+        on_device,
+        mesh=split,
+        in_specs=(tokens, tokens, tokens, tokens, experts, experts, features),
+        out_specs=(tokens, features),
+        check_vma=False,
+    )

time: 171 us -> 153 us (0.89)
  blocking collectives: 0 us -> 53.4 us
  waiting for transfers between devices: 90.8 us -> 45.9 us
  starting transfers between devices: 42.9 us -> 9.85 us
  Pallas kernels: 15.8 us -> 21.1 us
  other arithmetic: 5.22 us -> 0.98 us
  local copies, waits for them, and re-layouts: 1.16 us -> 4.59 us
    all_to_all x0 -> x1, blocking collectives: none -> 53.4 us  [on_device(): lax.all_to_all(packed, 'expert', split_axis=0, concat_axis=0, tiled=True)]
    ppermute x8 -> x1, waiting for transfers between devices: 49.4 us -> 0.01 us  [reduce_features(): arrived = lax.ppermute(other, 'core', [(0, 1), (1, 0)])]
    reduce_scatter x0 -> x1, waiting for transfers between devices: none -> 45.2 us  [reduce_features(): over_z = lax.psum_scatter(terms, 'z', scatter_dimension=0, tiled=True)]
    all_to_all x1 -> x0, waiting for transfers between devices: 35.9 us -> none  [on_device(): lax.all_to_all(packed, 'expert', split_axis=0, concat_axis=0, tiled=True)]
    all_to_all x1 -> x0, starting transfers between devices: 17.5 us -> none  [on_device(): lax.all_to_all(packed, 'expert', split_axis=0, concat_axis=0, tiled=True)]
    ppermute x8 -> x1, starting transfers between devices: 15.8 us -> 1.92 us  [reduce_features(): arrived = lax.ppermute(other, 'core', [(0, 1), (1, 0)])]
    pallas_call x1 -> x2, Pallas kernels: 9.81 us -> 15 us  [the longest x1 7.81 us: on_device(): call(backward_kernel, shape((peers, chunks, CAP * LANE), BF16), [HBM] * 6...]
    all_gather x1, waiting for transfers between devices: 4.83 us -> 0.02 us  [on_device(): lax.all_gather(w_down.reshape(width // ranks, hidden), ('z', 'core'), axi...]
  transfers between devices with their start and end apart: 11 -> 4, of which waited for: 9 -> 1; matrix products, arithmetic and copies ran while one was open for 2% -> 1% of each run, Pallas kernels for 4% -> 14%
where the time goes in v2:
time: 153 us; the launch traced here: 151 us
  blocking collectives  53.4 us (35%)
  waiting for transfers between devices  45.9 us (30%)
  Pallas kernels  21.1 us (14%)
  between operations  15.6 us (10%)
  starting transfers between devices  9.85 us (6%)
  local copies, waits for them, and re-layouts  4.59 us (3%)
    all_to_all x1, blocking collectives, on_device(): lax.all_to_all(packed, 'expert', split_axis=0, concat_axis=0, tiled=True)  53.4 us
    reduce_scatter x1, waiting for transfers between devices, reduce_features(): over_z = lax.psum_scatter(terms, 'z', scatter_dimension=0, tiled=True)  45.2 us
    all_to_all x1, starting transfers between devices, on_device(): lax.all_to_all(part, 'expert', split_axis=0, concat_axis=0, tiled=True)  7.84 us
    pallas_call x1, Pallas kernels, on_device(): call(backward_kernel, shape((peers, chunks, CAP * LANE), BF16), [HBM] * 6...  7.81 us
    pallas_call x1, Pallas kernels, on_device(): call(forward_kernel, (shape((width, hidden), BF16), shape((slots, hidden)...  7.15 us
    pallas_call x1, Pallas kernels, on_device(): call(functools.partial(pack_kernel, peers), shape((peers, chunks, 2 * CAP...  4.22 us
  transfers between devices with their start and end apart: 4, of which 1 were waited for; matrix products, arithmetic and copies ran while one was open for 1% of the time, Pallas kernels for 14%

profile of v2, /device:TPU:14, one launch (start us, length us, event | category | flops | bytes accessed | tf_op | source)
XLA Modules:
  0.0 151.4 jit_solution(12551890129889304083)
XLA Ops:
  8.0 0.0 all-gather.3.cloned.1.call-start
  8.0 0.7 all-gather.3.cloned.1.call-update
  8.7 0.0 reduce-scatter.2.cloned.1.call-start
  8.8 4.2 %pack.1 = bf16[64,16,768]{2,1,0:T(8,128)(2,1)} custom-call(s32[1,128]{1,0:T(1,128)} %bitcast.11, f32[1,128]{1,0:T(1,128)} %bitcast.20, bf16[128,2048]{1,0:T(8,128)(2,1)} %tok_hbm.1, bf16[128,2048]{1,0:T(8,128)(2,1)} %cot_hbm.1), custom_call_target="tpu_custom_call" | custom-call | flops 201326592 | bytes 4194304 | tf_op jit(solution)/shard_map/pack/pallas_call | solution.py:235
  13.0 53.4 %all_to_all.10.got_hbm = bf16[64,16,768]{2,1,0:T(8,128)(2,1)S(1)} all-to-all(bf16[64,16,768]{2,1,0:T(8,128)(2,1)} %pack.1), channel_id=1, replica_groups=mesh['expert'=64,'z'=8,'core'=2] {'expert'}, dimensions={0} | all-to-all | bytes 3145728 | tf_op jit(solution)/shard_map/all_to_all | solution.py:249
  66.4 7.1 %forward.1 = (bf16[2048,768]{1,0:T(8,128)(2,1)}, f32[192,768]{1,0:T(8,128)S(1)}, f32[192,768]{1,0:T(8,128)S(1)}, bf16[192,2048]{1,0:T(8,128)(2,1)S(1)}) custom-call(bf16[64,16,768]{2,1,0:T(8,128)(2,1)S(1)} %all_to_all.10.got_hbm, bf16[2048,768]{1,0:T(8,128)(2,1)} %bitcast.13, bf16[2048,768]{1,0:T(8,128)(2,1)} %bitcast.15), custom_call_target="tpu_custom_call" | custom-call | flops 1811939328 | bytes 14680064 | tf_op jit(solution)/shard_map/forward/pallas_call | solution.py:253
  73.6 0.0 copy-start
  73.6 0.9 copy-done
  74.5 0.9 copy-done.1
  75.4 0.9 copy-done.2
  76.2 0.0 reduce-scatter.2.cloned.1.call-update
  76.3 0.0 all-gather.3.cloned.1.call-done
  76.3 0.0 copy-start.3
  76.3 7.8 %backward.1 = bf16[64,16,384]{2,1,0:T(8,128)(2,1)} custom-call(f32[192,768]{1,0:T(8,128)} %copy-done.1, f32[192,768]{1,0:T(8,128)} %copy-done.2, bf16[192,2048]{1,0:T(8,128)(2,1)} %copy-done, bf16[2048,768]{1,0:T(8,128)(2,1)} %bitcast.17, bf16[2048,768]{1,0:T(8,128)(2,1)} %bitcast.14, bf16[2048,768]{1,0:T(8,128)(2,1)} %bitcast.16), custom_call_target="tpu_custom_call" | custom-call | flops 1811939328 | bytes 14680064 | tf_op jit(solution)/shard_map/backward/pallas_call | solution.py:278
  84.1 7.8 %all-to-all-start.1 = ((bf16[64,16,384]{2,1,0:T(8,128)(2,1)}), bf16[64,16,384]{2,1,0:T(8,128)(2,1)S(1)}, u32[]{:S(2)}, u32[]{:S(2)}) async-start(bf16[64,16,384]{2,1,0:T(8,128)(2,1)} %backward.1), calls=%async_computation.1 | async-start | bytes 1572864 | tf_op jit(solution)/shard_map/all_to_all | solution.py:298
  92.0 45.2 %reduce-scatter.2.cloned.1.call-done = bf16[256,768]{1,0:T(8,128)(2,1)} async-done(((bf16[2048,768]{1,0:T(8,128)(2,1)}), bf16[256,768]{1,0:T(8,128)(2,1)}) %reduce-scatter.2.cloned.1.call-update) | async-done | bytes 393232 | tf_op jit(solution)/shard_map/reduce_scatter | solution.py:211
  137.1 0.9 dynamic-slice_bitcast_fusion
  138.1 1.9 %collective-permute-start = (bf16[128,768]{1,0:T(8,128)(2,1)S(1)}, bf16[128,768]{1,0:T(8,128)(2,1)S(1)}, u32[]{:S(2)}, u32[]{:S(2)}) collective-permute-start(bf16[128,768]{1,0:T(8,128)(2,1)S(1)} %dynamic-slice_bitcast_fusion), channel_id=1, source_target_pairs={{0,1},{1,0},{2,3},{3,2},{4,5},{5,4},{6,7},{7,6},{8,9},{9,8},{10,11... | collective-permute-start | bytes 589832 | tf_op jit(solution)/shard_map/ppermute | solution.py:216
  140.0 0.0 all-to-all-done.1.got_hbm
  140.0 0.0 copy-done.3
  140.0 1.9 %collect.1 = bf16[128,2048]{1,0:T(8,128)(2,1)} custom-call(s32[1,128]{1,0:T(1,128)S(1)} %bitcast.12, bf16[64,16,384]{2,1,0:T(8,128)(2,1)S(1)} %all-to-all-done.1.got_hbm), custom_call_target="tpu_custom_call" | custom-call | flops 100663296 | bytes 2097152 | tf_op jit(solution)/shard_map/collect/pallas_call | solution.py:300
  141.9 0.0 collective-permute-done
  141.9 1.0 convert_add_fusion
  142.9 1.0 reshape.33
  (2 shorter events, 0.0 us)
Async XLA Ops:
  8.0 68.3 %all-gather.3.cloned.1.call-start = ((), (), s32[]{:S(2)}) async-start(), calls=%async_computation.4 | async-start | bytes 3342336 | tf_op jit(solution)/shard_map/all_gather | solution.py:232
  8.7 128.4 %reduce-scatter.2.cloned.1.call-start = ((), (), s32[]{:S(2)}) async-start(), calls=%async_computation.3 | async-start | bytes 3538944 | tf_op jit(solution)/shard_map/reduce_scatter | solution.py:211
  73.6 0.9 copy-start
  74.5 0.9 copy-start.1
  75.4 0.9 copy-start.2
  76.3 63.7 %copy-start.3 = (s32[128,1]{0,1:T(1,128)S(1)}, s32[128,1]{0,1:T(1,128)}, u32[]{:S(2)}) copy-start(s32[128,1]{0,1:T(1,128)} %param.9) | copy-start | bytes 1540
  84.1 55.9 %all-to-all-start.1 = ((bf16[64,16,384]{2,1,0:T(8,128)(2,1)}), bf16[64,16,384]{2,1,0:T(8,128)(2,1)S(1)}, u32[]{:S(2)}, u32[]{:S(2)}) async-start(bf16[64,16,384]{2,1,0:T(8,128)(2,1)} %backward.1), calls=%async_computation.1 | async-start | bytes 1572864 | tf_op jit(solution)/shard_map/all_to_all | solution.py:298
  138.1 3.9 %collective-permute-start = (bf16[128,768]{1,0:T(8,128)(2,1)S(1)}, bf16[128,768]{1,0:T(8,128)(2,1)S(1)}, u32[]{:S(2)}, u32[]{:S(2)}) collective-permute-start(bf16[128,768]{1,0:T(8,128)(2,1)S(1)} %dynamic-slice_bitcast_fusion), channel_id=1, source_target_pairs={{0,1},{1,0},{2,3},{3,2},{4,5},{5,4},{6,7},{7,6},{8,9},{9,8},{10,11... | collective-permute-start | bytes 589832 | tf_op jit(solution)/shard_map/ppermute | solution.py:216
Sparse Core Ops, SparseCore 0:
  11.5 59.5 all-gather.2
Sparse Core Ops, SparseCore 1:
  76.3 60.7 reduce-scatter.1

commit v3 on v1

v3 whole, which is shorter than its diff:
```python
import functools

import jax
import jax.numpy as jnp
from jax import lax
from jax.experimental import pallas as pl
from jax.experimental.pallas import tpu as pltpu
from jax.sharding import Mesh, PartitionSpec as P

CAP = 3
LANE = 128
NEAR = (0, -1, 1, -3, 3, -2, -4, 2)
FOLD = (-2, -4, 2, 3, -3, -1, 1, 0)
BF16 = jnp.bfloat16
F32 = jnp.float32

VMEM = pl.BlockSpec(memory_space=pltpu.VMEM)
SMEM = pl.BlockSpec(memory_space=pltpu.SMEM)
HBM = pl.BlockSpec(memory_space=pltpu.HBM)


def mm(a, b, ca=1, cb=0):
    return lax.dot_general(a, b, (((ca,), (cb,)), ((), ())), preferred_element_type=F32)


def slots_of(ids_row, peers):
    n = ids_row.shape[1]
    across = jnp.broadcast_to(ids_row, (n, n))
    down = across.T
    row = lax.broadcasted_iota(jnp.int32, (n, n), 0)
    col = lax.broadcasted_iota(jnp.int32, (n, n), 1)
    earlier = jnp.where((across == down) & (row < col), 1.0, 0.0).astype(F32)
    rank = jnp.sum(earlier, axis=0, keepdims=True).astype(jnp.int32)
    return rank * peers + ids_row


def placing_of(ids_row, peers):
    n = ids_row.shape[1]
    lines = lax.broadcasted_iota(jnp.int32, (CAP * peers, n), 0)
    return jnp.where(lines == slots_of(ids_row, peers), 1.0, 0.0).astype(BF16)


def lanes(q, count=1):
    return slice(q * LANE, (q + count) * LANE)


def start_all(pairs, sems, base=0):
    copies = [
        pltpu.make_async_copy(source, target, sems.at[base + i])
        for i, (source, target) in enumerate(pairs)
    ]
    for copy in copies:
        copy.start()
    return copies


def pack_kernel(
    peers, ids_ref, weight_ref, tok_hbm, cot_hbm, own_hbm,
    out_hbm, passed_hbm,
    tok, cot, out, scr, sems,
):
    copies = start_all([(tok_hbm, tok), (cot_hbm, cot), (own_hbm, passed_hbm)], sems)
    n, width = tok.shape
    chunks = width // LANE
    placing = placing_of(ids_ref[...], peers)
    weight = jnp.broadcast_to(weight_ref[...], (n, n)).T[:, :1]
    sent = copies[2:]
    for which in range(2):
        copies[which].wait()
        for c in range(0, chunks, 2):
            if which == 0:
                rows = tok[:, lanes(c, 2)]
            else:
                rows = (weight * cot[:, lanes(c, 2)].astype(F32)).astype(BF16)
            placed = mm(placing, rows)
            for s in range(CAP):
                for h in range(2):
                    scr[CAP * which + s, pl.ds(c + h, peers, stride=chunks), :] = placed[
                        s * peers : (s + 1) * peers, lanes(h)
                    ]
        for q in range(CAP * which, CAP * which + CAP):
            out[which, :, :, lanes(q % CAP)] = (
                scr[q].reshape(peers, chunks, LANE).astype(BF16)
            )
        copy = pltpu.make_async_copy(
            out.at[which], out_hbm.at[:, :, pl.ds(which * CAP * LANE, CAP * LANE)], sems.at[3 + which]
        )
        copy.start()
        sent.append(copy)
    for copy in sent:
        copy.wait()


def to_rows(got, scr):
    peers, chunks, _ = got.shape
    for s in range(CAP):
        scr[s] = got[:, :, lanes(s)].astype(F32).reshape(peers * chunks, LANE)
    for s in range(CAP):
        for c in range(chunks):
            yield slice(s * peers, (s + 1) * peers), c, scr[s, pl.ds(c, peers, stride=chunks), :]


def expert_kernel(
    place_ref, got_hbm, wg_hbm, wu_hbm, first_hbm, rest_hbm, first_other_hbm, rest_other_hbm,
    part_hbm, send_hbm, keep_hbm,
    got, wg, wu, down, scr, rows, cot, own, other, send, keep, part, sems,
):
    z, core = place_ref[0], place_ref[1]
    copies = start_all(
        [
            (got_hbm.at[:, :, pl.ds(0, CAP * LANE)], got.at[0]),
            (wg_hbm, wg),
            (wu_hbm, wu),
            (got_hbm.at[:, :, pl.ds(CAP * LANE, CAP * LANE)], got.at[1]),
        ],
        sems,
    )
    near = first_hbm.shape[0]
    chips = near + rest_hbm.shape[0]
    gathered = []
    for i, step in enumerate(NEAR):
        chip = lax.rem(z + (step + chips), chips)
        mine, theirs = (first_hbm, first_other_hbm) if i < near else (rest_hbm, rest_other_hbm)
        at = i if i < near else i - near
        gathered.append((mine.at[at], down.at[chip * 2 + core]))
        gathered.append((theirs.at[at], down.at[chip * 2 + 1 - core]))
    arriving = start_all(gathered, sems, 7)
    peers, chunks, _ = part.shape
    first = core == 0
    copies[0].wait()
    for lines, c, value in to_rows(got.at[0], scr):
        rows[lines, lanes(c)] = value.astype(BF16)
    copies[1].wait()
    gate = mm(rows[...], wg[...])
    sig = jax.nn.sigmoid(gate)
    copies[2].wait()
    up = mm(rows[...], wu[...])
    hidden = (gate * sig * up).astype(BF16)
    copies[3].wait()
    even = None
    for lines, c, value in to_rows(got.at[1], scr):
        cot[lines, lanes(c)] = value.astype(BF16)
        if c % 2 == 0:
            even = value
        else:
            own[lines, lanes(c // 2)] = jnp.where(first, even, value).astype(BF16)
            other[lines, lanes(c // 2)] = jnp.where(first, value, even).astype(BF16)
    sent = []
    for i, (source, target, target_hbm) in enumerate(
        ((other, send, send_hbm), (own, keep, keep_hbm))
    ):
        for b in range(0, chunks // 2, 2):
            value = mm(source[:, lanes(b, 2)], hidden, 0, 0).astype(BF16)
            target[b] = value[:LANE]
            target[b + 1] = value[LANE:]
        sent += start_all([(target, target_hbm)], sems, 4 + i)
    for copy in arriving:
        copy.wait()
    grad = mm(cot[...], down[...].reshape(wg.shape))
    gate_grad = (grad * up * sig * (1.0 + gate * (1.0 - sig))).astype(BF16)
    up_grad = (grad * (gate * sig)).astype(BF16)
    for c in range(0, chunks, 2):
        at = lanes(c, 2)
        value = mm(gate_grad, wg[at, :], 1, 1) + mm(up_grad, wu[at, :], 1, 1)
        for s in range(CAP):
            for h in range(2):
                scr[s, pl.ds(c + h, peers, stride=chunks), :] = value[
                    s * peers : (s + 1) * peers, lanes(h)
                ]
    for s in range(CAP):
        part[:, :, lanes(s)] = scr[s].reshape(peers, chunks, LANE).astype(BF16)
    sent += start_all([(part, part_hbm)], sems, 6)
    for copy in sent:
        copy.wait()


def fold_kernel(
    place_ref, keep_hbm, swapped_hbm,
    above_ref, below_ref, far_ref, outer_ref, inner_ref, under_ref, last_ref,
    kept, came, sems,
):
    z = place_ref[0]
    chips = keep_hbm.shape[0]
    copies = []
    for i, step in enumerate(FOLD):
        chip = lax.rem(z + (step + chips), chips)
        copies.append(
            start_all(
                [(keep_hbm.at[chip], kept.at[i]), (swapped_hbm.at[chip], came.at[i])], sems, 2 * i
            )
        )
    targets = (
        above_ref.at[0], above_ref.at[1], below_ref, far_ref,
        outer_ref, inner_ref, under_ref, last_ref,
    )
    for i, target in enumerate(targets):
        for copy in copies[i]:
            copy.wait()
        target[...] = (kept[i].astype(F32) + came[i].astype(F32)).astype(target.dtype)


def collect_kernel(peers, ids_ref, got_hbm, out_ref, got, scr, rows, sem):
    copy = pltpu.make_async_copy(got_hbm, got, sem)
    copy.start()
    placing = placing_of(ids_ref[...], peers)
    copy.wait()
    for lines, c, value in to_rows(got, scr):
        rows[lines, lanes(c)] = value.astype(BF16)
    out_ref[...] = mm(placing, rows[...], 0, 0).astype(BF16)


def call(kernel, out_shape, in_specs, out_specs, scratch, limit, flops, moved, name):
    return pl.pallas_call(
        kernel,
        out_shape=out_shape,
        in_specs=in_specs,
        out_specs=out_specs,
        scratch_shapes=scratch,
        compiler_params=pltpu.CompilerParams(vmem_limit_bytes=limit << 20),
        cost_estimate=pl.CostEstimate(flops=flops, bytes_accessed=moved, transcendentals=0),
        name=name,
    )


def over_core(x):
    return lax.ppermute(x, "core", [(0, 1), (1, 0)])


def round_z(x, step):
    chips = lax.axis_size("z")
    return lax.ppermute(x, "z", [(j, (j + step) % chips) for j in range(chips)])


def gather_features(own):
    m1, p1, m3, p3 = round_z(own, 1), round_z(own, -1), round_z(own, 3), round_z(own, -3)
    m2, m4 = jnp.split(round_z(jnp.concatenate([m1, m3]), 1), 2)
    p2 = round_z(p1, -1)
    first = jnp.stack([own, m1, p1, m3, p3])
    rest = jnp.stack([m2, m4, p2])
    return first, rest, over_core(first), over_core(rest)


def reduce_features(place, keep, swapped):
    blocks, lines, hidden = keep.shape
    narrow = jax.ShapeDtypeStruct((lines, hidden), BF16)
    wide = jax.ShapeDtypeStruct((lines, hidden), F32)
    both = jax.ShapeDtypeStruct((2, lines, hidden), BF16)
    pair, low, far_low, outer, inner, under, total = call(
        fold_kernel,
        (both, narrow, narrow, wide, wide, wide, wide),
        [SMEM, HBM, HBM],
        (VMEM,) * 7,
        [
            pltpu.VMEM(keep.shape, BF16),
            pltpu.VMEM(keep.shape, BF16),
            pltpu.SemaphoreType.DMA((2 * blocks,)),
        ],
        24, keep.size, 6 * keep.size, "fold",
    )(place, keep, swapped)
    above = round_z(pair, -1)
    below = round_z(low, 1)
    far_below = round_z(far_low, 3)
    far_above = round_z((outer + above[1].astype(F32)).astype(BF16), -3)
    near_above = round_z((inner + above[0].astype(F32)).astype(BF16), -1)
    near_below = round_z((under + below.astype(F32)).astype(BF16), 1)
    for arrived in (near_above, far_above, near_below, far_below):
        total = total + arrived.astype(F32)
    return total


def on_device(tokens, cotangent, expert_ids, route_weight, w_gate, w_up, w_down):
    n, width = tokens.shape
    peers = lax.axis_size("expert")
    ranks = lax.axis_size("z") * 2
    hidden = w_gate.shape[2]
    chunks = width // LANE
    slots = CAP * peers
    product = 2 * slots * width * hidden
    ids = expert_ids.reshape(1, n)
    weight = route_weight.reshape(1, n)
    wg = w_gate.reshape(width, hidden)
    wu = w_up.reshape(width, hidden)
    place = jnp.stack([lax.axis_index("z"), lax.axis_index("core")]).astype(jnp.int32)
    own = w_down.reshape(width // ranks, hidden)

    shape = jax.ShapeDtypeStruct
    packed, own = call(
        functools.partial(pack_kernel, peers),
        (shape((peers, chunks, 2 * CAP * LANE), BF16), shape(own.shape, BF16)),
        [VMEM, VMEM, HBM, HBM, HBM],
        (HBM, HBM),
        [
            pltpu.VMEM((n, width), BF16),
            pltpu.VMEM((n, width), BF16),
            pltpu.VMEM((2, peers, chunks, CAP * LANE), BF16),
            pltpu.VMEM((2 * CAP, peers * chunks, LANE), F32),
            pltpu.SemaphoreType.DMA((5,)),
        ],
        58, 4 * slots * n * width, 4 << 20, "pack",
    )(ids, weight, tokens, cotangent, own)
    got = lax.all_to_all(packed, "expert", split_axis=0, concat_axis=0, tiled=True)
    gathered = gather_features(own)

    weights = pltpu.VMEM((width, hidden), BF16)
    features = pltpu.VMEM((chunks // 2, LANE, hidden), BF16)
    part, send, keep = call(
        expert_kernel,
        (
            shape((peers, chunks, CAP * LANE), BF16),
            shape((chunks // 2, LANE, hidden), BF16),
            shape((chunks // 2, LANE, hidden), BF16),
        ),
        [SMEM] + [HBM] * 7,
        (HBM,) * 3,
        [
            pltpu.VMEM((2, peers, chunks, CAP * LANE), BF16),
            weights,
            weights,
            pltpu.VMEM((chunks, LANE, hidden), BF16),
            pltpu.VMEM((CAP, peers * chunks, LANE), F32),
            pltpu.VMEM((slots, width), BF16),
            pltpu.VMEM((slots, width), BF16),
            pltpu.VMEM((slots, width // 2), BF16),
            pltpu.VMEM((slots, width // 2), BF16),
            features,
            features,
            pltpu.VMEM((peers, chunks, CAP * LANE), BF16),
            pltpu.SemaphoreType.DMA((7 + chunks,)),
        ],
        58, 6 * product, 18 << 20, "expert",
    )(place, got, wg, wu, *gathered)
    swapped = over_core(send)
    down_part = reduce_features(place, keep, swapped)
    returned = lax.all_to_all(part, "expert", split_axis=0, concat_axis=0, tiled=True)

    token_grad = call(
        functools.partial(collect_kernel, peers),
        shape((n, width), BF16),
        [VMEM, HBM],
        VMEM,
        [
            pltpu.VMEM((peers, chunks, CAP * LANE), BF16),
            pltpu.VMEM((CAP, peers * chunks, LANE), F32),
            pltpu.VMEM((slots, width), BF16),
            pltpu.SemaphoreType.DMA,
        ],
        16, 2 * slots * n * width, 2 << 20, "collect",
    )(ids, returned)
    return (token_grad, down_part.reshape(w_down.shape))


def solution(mesh):
    ranks = mesh.shape["dp"]
    split = Mesh(
        mesh.devices.reshape(mesh.shape["expert"], ranks // 2, 2), ("expert", "z", "core")
    )
    tokens = P(("expert", "z", "core"), None)
    experts = P("expert", None, None)
    features = P(("z", "core"), "expert", None)
    return jax.shard_map(
        on_device,
        mesh=split,
        in_specs=(tokens, tokens, tokens, tokens, experts, experts, features),
        out_specs=(tokens, features),
        check_vma=False,
    )
```

time: 171 us -> 150 us (0.88)
  waiting for transfers between devices: 90.8 us -> 33.7 us
  starting transfers between devices: 42.9 us -> 86.7 us
  between operations: 14.4 us -> 1.01 us
  Pallas kernels: 15.8 us -> 24 us
  other arithmetic: 5.22 us -> 0.92 us
    ppermute x8 -> x15, starting transfers between devices: 15.8 us -> 56.3 us  [the longest x12 50.3 us: round_z(): return lax.ppermute(x, 'z', [(j, (j + step) % chips) for j in range(chips)])]
    all_to_all x1, waiting for transfers between devices: 35.9 us -> 0.01 us  [on_device(): lax.all_to_all(packed, 'expert', split_axis=0, concat_axis=0, tiled=True)]
    ppermute x8 -> x15, waiting for transfers between devices: 49.4 us -> 33.7 us  [the longest x12 32.2 us: round_z(): return lax.ppermute(x, 'z', [(j, (j + step) % chips) for j in range(chips)])]
    pallas_call x1 -> x2, Pallas kernels: 4.15 us -> 11.5 us  [the longest x1 7.78 us: on_device(): call(functools.partial(pack_kernel, peers), (shape((peers, chunks, 2 * CA...]
    all_gather x1 -> x0, waiting for transfers between devices: 4.83 us -> none  [on_device(): lax.all_gather(w_down.reshape(width // ranks, hidden), 'dp', axis=0, tile...]
    convert_element_type x7 -> x2, other arithmetic: 4.23 us -> 0.11 us  [the longest x1 0.07 us: reduce_features(): near_above = round_z((inner + above[0].astype(F32)).astype(BF16), -1)]
    all_to_all x1, starting transfers between devices: 9.66 us -> 12.7 us  [on_device(): lax.all_to_all(part, 'expert', split_axis=0, concat_axis=0, tiled=True)]
  transfers between devices with their start and end apart: 11 -> 17, of which waited for: 9 -> 10; matrix products, arithmetic and copies ran while one was open for 2% -> 1% of each run, Pallas kernels for 4% -> 4%
where the time goes in v3:
time: 150 us; the launch traced here: 149 us
  starting transfers between devices  86.7 us (58%)
  waiting for transfers between devices  33.7 us (22%)
  Pallas kernels  24 us (16%)
  local copies, waits for them, and re-layouts  2.43 us (2%)
    ppermute x12, starting transfers between devices, round_z(): return lax.ppermute(x, 'z', [(j, (j + step) % chips) for j in range(chips)])  50.3 us
    ppermute x12, waiting for transfers between devices, round_z(): return lax.ppermute(x, 'z', [(j, (j + step) % chips) for j in range(chips)])  32.2 us
    all_to_all x1, starting transfers between devices, on_device(): lax.all_to_all(packed, 'expert', split_axis=0, concat_axis=0, tiled=True)  17.6 us
    all_to_all x1, starting transfers between devices, on_device(): lax.all_to_all(part, 'expert', split_axis=0, concat_axis=0, tiled=True)  12.7 us
    pallas_call x1, Pallas kernels, on_device(): call(expert_kernel, (shape((peers, chunks, CAP * LANE), BF16), shape((chu...  10.5 us
    pallas_call x1, Pallas kernels, on_device(): call(functools.partial(pack_kernel, peers), (shape((peers, chunks, 2 * CA...  7.78 us
    ppermute x3, starting transfers between devices, over_core(): return lax.ppermute(x, 'core', [(0, 1), (1, 0)])  6.03 us
    pallas_call x1, Pallas kernels, reduce_features(): call(fold_kernel, (both, narrow, narrow, wide, wide, wide, wide), [SMEM,...  3.77 us
  transfers between devices with their start and end apart: 17, of which 10 were waited for; matrix products, arithmetic and copies ran while one was open for 1% of the time, Pallas kernels for 4%

profile of v3, /device:TPU:14, one launch (start us, length us, event | category | flops | bytes accessed | tf_op | source)
XLA Modules:
  0.0 148.8 jit_solution(15792822490479013764)
XLA Ops:
  0.6 7.8 %pack.1 = (bf16[64,16,768]{2,1,0:T(8,128)(2,1)}, bf16[128,768]{1,0:T(8,128)(2,1)}) custom-call(s32[1,128]{1,0:T(1,128)} %bitcast.34, f32[1,128]{1,0:T(1,128)} %bitcast.38, bf16[128,2048]{1,0:T(8,128)(2,1)} %tok_hbm.1, bf16[128,2048]{1,0:T(8,128)(2,1)} %cot_hbm.1, bf16[128,768]{1,0:T(8,128)(2,1)} %bitcast.37), custom_call_target="tpu_custom_call" | custom-call | flops 201326592 | bytes 4194304 | tf_op jit(solution)/shard_map/pack/pallas_call | solution.py:287
  8.4 17.6 %all-to-all-start = ((bf16[64,16,768]{2,1,0:T(8,128)(2,1)}), bf16[64,16,768]{2,1,0:T(8,128)(2,1)S(1)}, u32[]{:S(2)}, u32[]{:S(2)}) async-start(bf16[64,16,768]{2,1,0:T(8,128)(2,1)} %get-tuple-element.14), calls=%async_computation | async-start | bytes 3145728 | tf_op jit(solution)/shard_map/all_to_all | solution.py:301
  26.1 11.6 %collective-permute-start.3 = (bf16[128,768]{1,0:T(8,128)(2,1)S(1)}, bf16[128,768]{1,0:T(8,128)(2,1)S(1)}, u32[]{:S(2)}, u32[]{:S(2)}) collective-permute-start(bf16[128,768]{1,0:T(8,128)(2,1)S(1)} %copy-done.5), channel_id=1, source_target_pairs={{0,10},{2,12},{4,14},{6,0},{8,2},{10,4},{12,6},{14,8},{1,11},{3,13... | collective-permute-start | bytes 589832 | tf_op jit(solution)/shard_map/ppermute | solution.py:231
  39.7 8.8 %collective-permute-start.1 = (bf16[128,768]{1,0:T(8,128)(2,1)S(1)}, bf16[128,768]{1,0:T(8,128)(2,1)S(1)}, u32[]{:S(2)}, u32[]{:S(2)}) collective-permute-start(bf16[128,768]{1,0:T(8,128)(2,1)S(1)} %copy-done.5), channel_id=1, source_target_pairs={{0,14},{2,0},{4,2},{6,4},{8,6},{10,8},{12,10},{14,12},{1,15},{3,1}... | collective-permute-start | bytes 589832 | tf_op jit(solution)/shard_map/ppermute | solution.py:231
  50.4 7.0 %collective-permute-done.2 = bf16[128,768]{1,0:T(8,128)(2,1)S(1)} collective-permute-done((bf16[128,768]{1,0:T(8,128)(2,1)S(1)}, bf16[128,768]{1,0:T(8,128)(2,1)S(1)}, u32[]{:S(2)}, u32[]{:S(2)}) %collective-permute-start.2) | collective-permute-done | bytes 196640 | tf_op jit(solution)/shard_map/ppermute | solution.py:231
  57.4 4.1 %collective-permute-done = bf16[128,768]{1,0:T(8,128)(2,1)S(1)} collective-permute-done((bf16[128,768]{1,0:T(8,128)(2,1)S(1)}, bf16[128,768]{1,0:T(8,128)(2,1)S(1)}, u32[]{:S(2)}, u32[]{:S(2)}) %collective-permute-start) | collective-permute-done | bytes 196640 | tf_op jit(solution)/shard_map/ppermute | solution.py:231
  61.6 1.9 %collective-permute-start.4 = (bf16[256,768]{1,0:T(8,128)(2,1)S(1)}, bf16[256,768]{1,0:T(8,128)(2,1)S(1)}, u32[]{:S(2)}, u32[]{:S(2)}) collective-permute-start(bf16[256,768]{1,0:T(8,128)(2,1)S(1)} %pad_maximum_fusion.1), channel_id=1, source_target_pairs={{0,2},{2,4},{4,6},{6,8},{8,10},{10,12},{12,14},{14,0},{1,3},{3,5},... | collective-permute-start | bytes 1179656 | tf_op jit(solution)/shard_map/ppermute | solution.py:231
  63.6 1.9 %collective-permute-start.6 = (bf16[5,128,768]{2,1,0:T(8,128)(2,1)S(1)}, bf16[5,128,768]{2,1,0:T(8,128)(2,1)}, u32[]{:S(2)}, u32[]{:S(2)}) collective-permute-start(bf16[5,128,768]{2,1,0:T(8,128)(2,1)S(1)} %bitcast_dynamic-update-slice_fusion.first_hbm), channel_id=1, source_target_pairs={{0,1},{1,0},{2,3},{3,2},{4,5},{5,4},{6,7},{7,6},{8,9},{9,8},{10,11... | collective-permute-start | bytes 2949128 | tf_op jit(solution)/shard_map/ppermute | solution.py:226
  65.6 5.1 %collective-permute-start.5 = (bf16[128,768]{1,0:T(8,128)(2,1)S(1)}, bf16[128,768]{1,0:T(8,128)(2,1)S(1)}, u32[]{:S(2)}, u32[]{:S(2)}) collective-permute-start(bf16[128,768]{1,0:T(8,128)(2,1)S(1)} %collective-permute-done.1), channel_id=1, source_target_pairs={{0,14},{2,0},{4,2},{6,4},{8,6},{10,8},{12,10},{14,12},{1,15},{3,1}... | collective-permute-start | bytes 589832 | tf_op jit(solution)/shard_map/ppermute | solution.py:231
  70.7 5.0 %collective-permute-done.4 = bf16[256,768]{1,0:T(8,128)(2,1)S(1)} collective-permute-done((bf16[256,768]{1,0:T(8,128)(2,1)S(1)}, bf16[256,768]{1,0:T(8,128)(2,1)S(1)}, u32[]{:S(2)}, u32[]{:S(2)}) %collective-permute-start.4) | collective-permute-done | bytes 393248 | tf_op jit(solution)/shard_map/ppermute | solution.py:231
  75.8 1.9 %collective-permute-start.7 = (bf16[3,128,768]{2,1,0:T(8,128)(2,1)S(1)}, bf16[3,128,768]{2,1,0:T(8,128)(2,1)}, u32[]{:S(2)}, u32[]{:S(2)}) collective-permute-start(bf16[3,128,768]{2,1,0:T(8,128)(2,1)S(1)} %pad_maximum_fusion.rest_hbm), channel_id=1, source_target_pairs={{0,1},{1,0},{2,3},{3,2},{4,5},{5,4},{6,7},{7,6},{8,9},{9,8},{10,11... | collective-permute-start | bytes 1769480 | tf_op jit(solution)/shard_map/ppermute | solution.py:226
  81.0 10.5 %expert.1 = (bf16[64,16,384]{2,1,0:T(8,128)(2,1)}, bf16[8,128,768]{2,1,0:T(8,128)(2,1)}, bf16[8,128,768]{2,1,0:T(8,128)(2,1)}) custom-call(s32[2]{0:T(128)} %pad_add_fusion.place_ref, bf16[64,16,768]{2,1,0:T(8,128)(2,1)} %copy-done.3, bf16[2048,768]{1,0:T(8,128)(2,1)} %bitcast.39, bf16[2048,768]{1,0:T(8,128)(2,1)} %bitcast.40, ...), custom_call_target="tpu_custom_call" | custom-call | flops 3623878656 | bytes 18874368 | tf_op jit(solution)/shard_map/expert/pallas_call | solution.py:306
  91.6 2.2 %collective-permute-start.8 = (bf16[8,128,768]{2,1,0:T(8,128)(2,1)}, bf16[8,128,768]{2,1,0:T(8,128)(2,1)}, u32[]{:S(2)}, u32[]{:S(2)}) collective-permute-start(bf16[8,128,768]{2,1,0:T(8,128)(2,1)} %get-tuple-element.18), channel_id=1, source_target_pairs={{0,1},{1,0},{2,3},{3,2},{4,5},{5,4},{6,7},{7,6},{8,9},{9,8},{10,11... | collective-permute-start | bytes 4718600 | tf_op jit(solution)/shard_map/ppermute | solution.py:226
  93.8 12.7 %all-to-all-start.1 = ((bf16[64,16,384]{2,1,0:T(8,128)(2,1)}), bf16[64,16,384]{2,1,0:T(8,128)(2,1)S(1)}, u32[]{:S(2)}, u32[]{:S(2)}) async-start(bf16[64,16,384]{2,1,0:T(8,128)(2,1)} %get-tuple-element.16), calls=%async_computation.1 | async-start | bytes 1572864 | tf_op jit(solution)/shard_map/all_to_all | solution.py:334
  106.6 3.8 %fold.1 = (bf16[2,128,768]{2,1,0:T(8,128)(2,1)S(1)}, bf16[128,768]{1,0:T(8,128)(2,1)S(1)}, bf16[128,768]{1,0:T(8,128)(2,1)S(1)}, f32[128,768]{1,0:T(8,128)S(1)},...) custom-call(s32[2]{0:T(128)S(1)} %copy-done.2, bf16[8,128,768]{2,1,0:T(8,128)(2,1)S(1)} %copy-done, ...), custom_call_target="tpu_custom_call" | custom-call | flops 786432 | bytes 4718592 | tf_op jit(solution)/shard_map/fold/pallas_call | solution.py:248
  110.3 1.9 %collective-permute-start.12 = (bf16[128,768]{1,0:T(8,128)(2,1)S(1)}, bf16[128,768]{1,0:T(8,128)(2,1)S(1)}, u32[]{:S(2)}, u32[]{:S(2)}) collective-permute-start(bf16[128,768]{1,0:T(8,128)(2,1)S(1)} %get-tuple-element.24), channel_id=1, source_target_pairs={{0,2},{2,4},{4,6},{6,8},{8,10},{10,12},{12,14},{14,0},{1,3},{3,5},... | collective-permute-start | bytes 589832 | tf_op jit(solution)/shard_map/ppermute | solution.py:231
  112.3 5.3 %collective-permute-start.9 = (bf16[2,128,768]{2,1,0:T(8,128)(2,1)S(1)}, bf16[2,128,768]{2,1,0:T(8,128)(2,1)S(1)}, u32[]{:S(2)}, u32[]{:S(2)}) collective-permute-start(bf16[2,128,768]{2,1,0:T(8,128)(2,1)S(1)} %get-tuple-element.21), channel_id=1, source_target_pairs={{0,14},{2,0},{4,2},{6,4},{8,6},{10,8},{12,10},{14,12},{1,15},{3,1}... | collective-permute-start | bytes 1179656 | tf_op jit(solution)/shard_map/ppermute | solution.py:231
  117.6 2.0 %collective-permute-start.14 = (bf16[128,768]{1,0:T(8,128)(2,1)S(1)}, bf16[128,768]{1,0:T(8,128)(2,1)S(1)}, u32[]{:S(2)}, u32[]{:S(2)}) collective-permute-start(bf16[128,768]{1,0:T(8,128)(2,1)S(1)} %get-tuple-element.25), channel_id=1, source_target_pairs={{0,6},{2,8},{4,10},{6,12},{8,14},{10,0},{12,2},{14,4},{1,7},{3,9},... | collective-permute-start | bytes 589832 | tf_op jit(solution)/shard_map/ppermute | solution.py:231
  120.6 2.2 %collective-permute-start.13 = (bf16[128,768]{1,0:T(8,128)(2,1)S(1)}, bf16[128,768]{1,0:T(8,128)(2,1)S(1)}, u32[]{:S(2)}, u32[]{:S(2)}) collective-permute-start(bf16[128,768]{1,0:T(8,128)(2,1)S(1)} %add_convert_fusion), channel_id=1, source_target_pairs={{0,2},{2,4},{4,6},{6,8},{8,10},{10,12},{12,14},{14,0},{1,3},{3,5},... | collective-permute-start | bytes 589832 | tf_op jit(solution)/shard_map/ppermute | solution.py:231
  122.8 3.1 %collective-permute-done.9 = bf16[2,128,768]{2,1,0:T(8,128)(2,1)S(1)} collective-permute-done((bf16[2,128,768]{2,1,0:T(8,128)(2,1)S(1)}, bf16[2,128,768]{2,1,0:T(8,128)(2,1)S(1)}, u32[]{:S(2)}, u32[]{:S(2)}) %collective-permute-start.9) | collective-permute-done | bytes 393248 | tf_op jit(solution)/shard_map/ppermute | solution.py:231
  126.0 5.6 %collective-permute-start.10 = (bf16[128,768]{1,0:T(8,128)(2,1)S(1)}, bf16[128,768]{1,0:T(8,128)(2,1)S(1)}, u32[]{:S(2)}, u32[]{:S(2)}) collective-permute-start(bf16[128,768]{1,0:T(8,128)(2,1)S(1)} %get-tuple-element.28), channel_id=1, source_target_pairs={{0,14},{2,0},{4,2},{6,4},{8,6},{10,8},{12,10},{14,12},{1,15},{3,1}... | collective-permute-start | bytes 589832 | tf_op jit(solution)/shard_map/ppermute | solution.py:231
  135.5 2.0 %collective-permute-done.14 = bf16[128,768]{1,0:T(8,128)(2,1)S(1)} collective-permute-done((bf16[128,768]{1,0:T(8,128)(2,1)S(1)}, bf16[128,768]{1,0:T(8,128)(2,1)S(1)}, u32[]{:S(2)}, u32[]{:S(2)}) %collective-permute-start.14) | collective-permute-done | bytes 196640 | tf_op jit(solution)/shard_map/ppermute | solution.py:231
  138.5 4.8 %collective-permute-done.10 = bf16[128,768]{1,0:T(8,128)(2,1)S(1)} collective-permute-done((bf16[128,768]{1,0:T(8,128)(2,1)S(1)}, bf16[128,768]{1,0:T(8,128)(2,1)S(1)}, u32[]{:S(2)}, u32[]{:S(2)}) %collective-permute-start.10) | collective-permute-done | bytes 196640 | tf_op jit(solution)/shard_map/ppermute | solution.py:231
  143.4 4.1 %collective-permute-done.11 = bf16[128,768]{1,0:T(8,128)(2,1)S(1)} collective-permute-done((bf16[128,768]{1,0:T(8,128)(2,1)S(1)}, bf16[128,768]{1,0:T(8,128)(2,1)S(1)}, u32[]{:S(2)}, u32[]{:S(2)}) %collective-permute-start.11) | collective-permute-done | bytes 196640 | tf_op jit(solution)/shard_map/ppermute | solution.py:231
  (41 shorter events, 14.6 us)
Async XLA Ops:
  8.4 17.7 %copy-start.5 = (bf16[128,768]{1,0:T(8,128)(2,1)S(1)}, bf16[128,768]{1,0:T(8,128)(2,1)}, u32[]{:S(2)}) copy-start(bf16[128,768]{1,0:T(8,128)(2,1)} %get-tuple-element.15) | copy-start | bytes 589828
  8.4 71.4 %all-to-all-start = ((bf16[64,16,768]{2,1,0:T(8,128)(2,1)}), bf16[64,16,768]{2,1,0:T(8,128)(2,1)S(1)}, u32[]{:S(2)}, u32[]{:S(2)}) async-start(bf16[64,16,768]{2,1,0:T(8,128)(2,1)} %get-tuple-element.14), calls=%async_computation | async-start | bytes 3145728 | tf_op jit(solution)/shard_map/all_to_all | solution.py:301
  26.1 37.5 %collective-permute-start.3 = (bf16[128,768]{1,0:T(8,128)(2,1)S(1)}, bf16[128,768]{1,0:T(8,128)(2,1)S(1)}, u32[]{:S(2)}, u32[]{:S(2)}) collective-permute-start(bf16[128,768]{1,0:T(8,128)(2,1)S(1)} %copy-done.5), channel_id=1, source_target_pairs={{0,10},{2,12},{4,14},{6,0},{8,2},{10,4},{12,6},{14,8},{1,11},{3,13... | collective-permute-start | bytes 589832 | tf_op jit(solution)/shard_map/ppermute | solution.py:231
  37.7 19.7 %collective-permute-start.2 = (bf16[128,768]{1,0:T(8,128)(2,1)S(1)}, bf16[128,768]{1,0:T(8,128)(2,1)S(1)}, u32[]{:S(2)}, u32[]{:S(2)}) collective-permute-start(bf16[128,768]{1,0:T(8,128)(2,1)S(1)} %copy-done.5), channel_id=1, source_target_pairs={{0,6},{2,8},{4,10},{6,12},{8,14},{10,0},{12,2},{14,4},{1,7},{3,9},... | collective-permute-start | bytes 589832 | tf_op jit(solution)/shard_map/ppermute | solution.py:231
  39.7 23.9 %collective-permute-start.1 = (bf16[128,768]{1,0:T(8,128)(2,1)S(1)}, bf16[128,768]{1,0:T(8,128)(2,1)S(1)}, u32[]{:S(2)}, u32[]{:S(2)}) collective-permute-start(bf16[128,768]{1,0:T(8,128)(2,1)S(1)} %copy-done.5), channel_id=1, source_target_pairs={{0,14},{2,0},{4,2},{6,4},{8,6},{10,8},{12,10},{14,12},{1,15},{3,1}... | collective-permute-start | bytes 589832 | tf_op jit(solution)/shard_map/ppermute | solution.py:231
  48.4 13.1 %collective-permute-start = (bf16[128,768]{1,0:T(8,128)(2,1)S(1)}, bf16[128,768]{1,0:T(8,128)(2,1)S(1)}, u32[]{:S(2)}, u32[]{:S(2)}) collective-permute-start(bf16[128,768]{1,0:T(8,128)(2,1)S(1)} %copy-done.5), channel_id=1, source_target_pairs={{0,2},{2,4},{4,6},{6,8},{8,10},{10,12},{12,14},{14,0},{1,3},{3,5},... | collective-permute-start | bytes 589832 | tf_op jit(solution)/shard_map/ppermute | solution.py:231
  61.6 14.1 %collective-permute-start.4 = (bf16[256,768]{1,0:T(8,128)(2,1)S(1)}, bf16[256,768]{1,0:T(8,128)(2,1)S(1)}, u32[]{:S(2)}, u32[]{:S(2)}) collective-permute-start(bf16[256,768]{1,0:T(8,128)(2,1)S(1)} %pad_maximum_fusion.1), channel_id=1, source_target_pairs={{0,2},{2,4},{4,6},{6,8},{8,10},{10,12},{12,14},{14,0},{1,3},{3,5},... | collective-permute-start | bytes 1179656 | tf_op jit(solution)/shard_map/ppermute | solution.py:231
  63.6 16.3 %copy-start.6 = (bf16[5,128,768]{2,1,0:T(8,128)(2,1)}, bf16[5,128,768]{2,1,0:T(8,128)(2,1)S(1)}, u32[]{:S(2)}) copy-start(bf16[5,128,768]{2,1,0:T(8,128)(2,1)S(1)} %bitcast_dynamic-update-slice_fusion.first_hbm) | copy-start | bytes 2949124
  63.6 16.2 %collective-permute-start.6 = (bf16[5,128,768]{2,1,0:T(8,128)(2,1)S(1)}, bf16[5,128,768]{2,1,0:T(8,128)(2,1)}, u32[]{:S(2)}, u32[]{:S(2)}) collective-permute-start(bf16[5,128,768]{2,1,0:T(8,128)(2,1)S(1)} %bitcast_dynamic-update-slice_fusion.first_hbm), channel_id=1, source_target_pairs={{0,1},{1,0},{2,3},{3,2},{4,5},{5,4},{6,7},{7,6},{8,9},{9,8},{10,11... | collective-permute-start | bytes 2949128 | tf_op jit(solution)/shard_map/ppermute | solution.py:226
  65.6 10.2 %collective-permute-start.5 = (bf16[128,768]{1,0:T(8,128)(2,1)S(1)}, bf16[128,768]{1,0:T(8,128)(2,1)S(1)}, u32[]{:S(2)}, u32[]{:S(2)}) collective-permute-start(bf16[128,768]{1,0:T(8,128)(2,1)S(1)} %collective-permute-done.1), channel_id=1, source_target_pairs={{0,14},{2,0},{4,2},{6,4},{8,6},{10,8},{12,10},{14,12},{1,15},{3,1}... | collective-permute-start | bytes 589832 | tf_op jit(solution)/shard_map/ppermute | solution.py:231
  75.8 4.1 %copy-start.4 = (bf16[3,128,768]{2,1,0:T(8,128)(2,1)}, bf16[3,128,768]{2,1,0:T(8,128)(2,1)S(1)}, u32[]{:S(2)}) copy-start(bf16[3,128,768]{2,1,0:T(8,128)(2,1)S(1)} %pad_maximum_fusion.rest_hbm) | copy-start | bytes 1769476
  75.8 4.0 %collective-permute-start.7 = (bf16[3,128,768]{2,1,0:T(8,128)(2,1)S(1)}, bf16[3,128,768]{2,1,0:T(8,128)(2,1)}, u32[]{:S(2)}, u32[]{:S(2)}) collective-permute-start(bf16[3,128,768]{2,1,0:T(8,128)(2,1)S(1)} %pad_maximum_fusion.rest_hbm), channel_id=1, source_target_pairs={{0,1},{1,0},{2,3},{3,2},{4,5},{5,4},{6,7},{7,6},{8,9},{9,8},{10,11... | collective-permute-start | bytes 1769480 | tf_op jit(solution)/shard_map/ppermute | solution.py:226
  79.9 1.2 copy-start.3
  91.6 15.0 %copy-start = (bf16[8,128,768]{2,1,0:T(8,128)(2,1)S(1)}, bf16[8,128,768]{2,1,0:T(8,128)(2,1)}, u32[]{:S(2)}) copy-start(bf16[8,128,768]{2,1,0:T(8,128)(2,1)} %get-tuple-element.17.keep_hbm) | copy-start | bytes 4718596
  91.6 15.0 %copy-start.2 = (s32[2]{0:T(128)S(1)}, s32[2]{0:T(128)}, u32[]{:S(2)}) copy-start(s32[2]{0:T(128)} %pad_add_fusion.place_ref) | copy-start | bytes 28
  91.6 14.9 %collective-permute-start.8 = (bf16[8,128,768]{2,1,0:T(8,128)(2,1)}, bf16[8,128,768]{2,1,0:T(8,128)(2,1)}, u32[]{:S(2)}, u32[]{:S(2)}) collective-permute-start(bf16[8,128,768]{2,1,0:T(8,128)(2,1)} %get-tuple-element.18), channel_id=1, source_target_pairs={{0,1},{1,0},{2,3},{3,2},{4,5},{5,4},{6,7},{7,6},{8,9},{9,8},{10,11... | collective-permute-start | bytes 4718600 | tf_op jit(solution)/shard_map/ppermute | solution.py:226
  93.8 39.8 %all-to-all-start.1 = ((bf16[64,16,384]{2,1,0:T(8,128)(2,1)}), bf16[64,16,384]{2,1,0:T(8,128)(2,1)S(1)}, u32[]{:S(2)}, u32[]{:S(2)}) async-start(bf16[64,16,384]{2,1,0:T(8,128)(2,1)} %get-tuple-element.16), calls=%async_computation.1 | async-start | bytes 1572864 | tf_op jit(solution)/shard_map/all_to_all | solution.py:334
  110.3 23.2 %copy-start.1 = (s32[128,1]{0,1:T(1,128)S(1)}, s32[128,1]{0,1:T(1,128)}, u32[]{:S(2)}) copy-start(s32[128,1]{0,1:T(1,128)} %param.9) | copy-start | bytes 1540
  110.3 10.2 %collective-permute-start.12 = (bf16[128,768]{1,0:T(8,128)(2,1)S(1)}, bf16[128,768]{1,0:T(8,128)(2,1)S(1)}, u32[]{:S(2)}, u32[]{:S(2)}) collective-permute-start(bf16[128,768]{1,0:T(8,128)(2,1)S(1)} %get-tuple-element.24), channel_id=1, source_target_pairs={{0,2},{2,4},{4,6},{6,8},{8,10},{10,12},{12,14},{14,0},{1,3},{3,5},... | collective-permute-start | bytes 589832 | tf_op jit(solution)/shard_map/ppermute | solution.py:231
  112.3 13.7 %collective-permute-start.9 = (bf16[2,128,768]{2,1,0:T(8,128)(2,1)S(1)}, bf16[2,128,768]{2,1,0:T(8,128)(2,1)S(1)}, u32[]{:S(2)}, u32[]{:S(2)}) collective-permute-start(bf16[2,128,768]{2,1,0:T(8,128)(2,1)S(1)} %get-tuple-element.21), channel_id=1, source_target_pairs={{0,14},{2,0},{4,2},{6,4},{8,6},{10,8},{12,10},{14,12},{1,15},{3,1}... | collective-permute-start | bytes 1179656 | tf_op jit(solution)/shard_map/ppermute | solution.py:231
  117.6 19.8 %collective-permute-start.14 = (bf16[128,768]{1,0:T(8,128)(2,1)S(1)}, bf16[128,768]{1,0:T(8,128)(2,1)S(1)}, u32[]{:S(2)}, u32[]{:S(2)}) collective-permute-start(bf16[128,768]{1,0:T(8,128)(2,1)S(1)} %get-tuple-element.25), channel_id=1, source_target_pairs={{0,6},{2,8},{4,10},{6,12},{8,14},{10,0},{12,2},{14,4},{1,7},{3,9},... | collective-permute-start | bytes 589832 | tf_op jit(solution)/shard_map/ppermute | solution.py:231
  120.6 18.0 %collective-permute-start.13 = (bf16[128,768]{1,0:T(8,128)(2,1)S(1)}, bf16[128,768]{1,0:T(8,128)(2,1)S(1)}, u32[]{:S(2)}, u32[]{:S(2)}) collective-permute-start(bf16[128,768]{1,0:T(8,128)(2,1)S(1)} %add_convert_fusion), channel_id=1, source_target_pairs={{0,2},{2,4},{4,6},{6,8},{8,10},{10,12},{12,14},{14,0},{1,3},{3,5},... | collective-permute-start | bytes 589832 | tf_op jit(solution)/shard_map/ppermute | solution.py:231
  126.0 17.4 %collective-permute-start.10 = (bf16[128,768]{1,0:T(8,128)(2,1)S(1)}, bf16[128,768]{1,0:T(8,128)(2,1)S(1)}, u32[]{:S(2)}, u32[]{:S(2)}) collective-permute-start(bf16[128,768]{1,0:T(8,128)(2,1)S(1)} %get-tuple-element.28), channel_id=1, source_target_pairs={{0,14},{2,0},{4,2},{6,4},{8,6},{10,8},{12,10},{14,12},{1,15},{3,1}... | collective-permute-start | bytes 589832 | tf_op jit(solution)/shard_map/ppermute | solution.py:231
  131.6 15.9 %collective-permute-start.11 = (bf16[128,768]{1,0:T(8,128)(2,1)S(1)}, bf16[128,768]{1,0:T(8,128)(2,1)S(1)}, u32[]{:S(2)}, u32[]{:S(2)}) collective-permute-start(bf16[128,768]{1,0:T(8,128)(2,1)S(1)} %get-tuple-element.29), channel_id=1, source_target_pairs={{0,10},{2,12},{4,14},{6,0},{8,2},{10,4},{12,6},{14,8},{1,11},{3,13... | collective-permute-start | bytes 589832 | tf_op jit(solution)/shard_map/ppermute | solution.py:231

commit v4 on v3

--- a/solution.py
+++ b/solution.py
@@ -10,7 +10,6 @@
 CAP = 3
 LANE = 128
 NEAR = (0, -1, 1, -3, 3, -2, -4, 2)
-FOLD = (-2, -4, 2, 3, -3, -1, 1, 0)
 BF16 = jnp.bfloat16
 F32 = jnp.float32
 
@@ -57,14 +56,15 @@
 def pack_kernel(
     peers, ids_ref, weight_ref, tok_hbm, cot_hbm, own_hbm,
     out_hbm, passed_hbm,
-    tok, cot, out, scr, sems,
+    tok, cot, own, out, scr, sems,
 ):
-    copies = start_all([(tok_hbm, tok), (cot_hbm, cot), (own_hbm, passed_hbm)], sems)
+    copies = start_all([(tok_hbm, tok), (cot_hbm, cot), (own_hbm, own)], sems)
     n, width = tok.shape
     chunks = width // LANE
     placing = placing_of(ids_ref[...], peers)
     weight = jnp.broadcast_to(weight_ref[...], (n, n)).T[:, :1]
-    sent = copies[2:]
+    copies[2].wait()
+    sent = start_all([(own, passed_hbm)], sems, 5)
     for which in range(2):
         copies[which].wait()
         for c in range(0, chunks, 2):
@@ -100,12 +100,11 @@
             yield slice(s * peers, (s + 1) * peers), c, scr[s, pl.ds(c, peers, stride=chunks), :]
 
 
-def expert_kernel(
-    place_ref, got_hbm, wg_hbm, wu_hbm, first_hbm, rest_hbm, first_other_hbm, rest_other_hbm,
-    part_hbm, send_hbm, keep_hbm,
-    got, wg, wu, down, scr, rows, cot, own, other, send, keep, part, sems,
+def forward_kernel(
+    place_ref, got_hbm, wg_hbm, wu_hbm, after_hbm,
+    send_hbm, keep_hbm, gate_hbm, up_hbm, cot_hbm,
+    got, wg, wu, scr, rows, cot, own, other, gate, up, send, keep, sems,
 ):
-    z, core = place_ref[0], place_ref[1]
     copies = start_all(
         [
             (got_hbm.at[:, :, pl.ds(0, CAP * LANE)], got.at[0]),
@@ -115,27 +114,19 @@
         ],
         sems,
     )
-    near = first_hbm.shape[0]
-    chips = near + rest_hbm.shape[0]
-    gathered = []
-    for i, step in enumerate(NEAR):
-        chip = lax.rem(z + (step + chips), chips)
-        mine, theirs = (first_hbm, first_other_hbm) if i < near else (rest_hbm, rest_other_hbm)
-        at = i if i < near else i - near
-        gathered.append((mine.at[at], down.at[chip * 2 + core]))
-        gathered.append((theirs.at[at], down.at[chip * 2 + 1 - core]))
-    arriving = start_all(gathered, sems, 7)
-    peers, chunks, _ = part.shape
-    first = core == 0
+    chunks = got.shape[2]
+    first = place_ref[1] == 0
     copies[0].wait()
     for lines, c, value in to_rows(got.at[0], scr):
         rows[lines, lanes(c)] = value.astype(BF16)
     copies[1].wait()
-    gate = mm(rows[...], wg[...])
-    sig = jax.nn.sigmoid(gate)
+    gate_value = mm(rows[...], wg[...])
+    gate[...] = gate_value
     copies[2].wait()
-    up = mm(rows[...], wu[...])
-    hidden = (gate * sig * up).astype(BF16)
+    up_value = mm(rows[...], wu[...])
+    up[...] = up_value
+    hidden = (gate_value * jax.nn.sigmoid(gate_value) * up_value).astype(BF16)
+    sent = start_all([(gate, gate_hbm), (up, up_hbm)], sems, 4)
     copies[3].wait()
     even = None
     for lines, c, value in to_rows(got.at[1], scr):
@@ -145,7 +136,7 @@
         else:
             own[lines, lanes(c // 2)] = jnp.where(first, even, value).astype(BF16)
             other[lines, lanes(c // 2)] = jnp.where(first, value, even).astype(BF16)
-    sent = []
+    sent += start_all([(cot, cot_hbm)], sems, 6)
     for i, (source, target, target_hbm) in enumerate(
         ((other, send, send_hbm), (own, keep, keep_hbm))
     ):
@@ -153,12 +144,47 @@
             value = mm(source[:, lanes(b, 2)], hidden, 0, 0).astype(BF16)
             target[b] = value[:LANE]
             target[b + 1] = value[LANE:]
-        sent += start_all([(target, target_hbm)], sems, 4 + i)
+        sent += start_all([(target, target_hbm)], sems, 7 + i)
+    for copy in sent:
+        copy.wait()
+
+
+def backward_kernel(
+    place_ref, gate_hbm, up_hbm, cot_hbm,
+    first_hbm, rest_hbm, first_other_hbm, rest_other_hbm, wg_hbm, wu_hbm,
+    part_hbm,
+    gate, up, cot, down, wg, wu, scr, part, sems,
+):
+    z, core = place_ref[0], place_ref[1]
+    near = first_hbm.shape[0]
+    chips = near + rest_hbm.shape[0]
+    gathered = []
+    for i, step in enumerate(NEAR):
+        ahead = step * (1 - 2 * core)
+        mine, theirs = (first_hbm, first_other_hbm) if i < near else (rest_hbm, rest_other_hbm)
+        at = i if i < near else i - near
+        chip = lax.rem(z + ahead + chips, chips)
+        gathered.append((mine.at[at], down.at[chip * 2 + core]))
+        chip = lax.rem(z - ahead + chips, chips)
+        gathered.append((theirs.at[at], down.at[chip * 2 + 1 - core]))
+    copies = start_all([(cot_hbm, cot)], sems)
+    arriving = start_all(gathered, sems, 7)
+    copies += start_all(
+        [(gate_hbm, gate), (up_hbm, up), (wg_hbm, wg), (wu_hbm, wu)], sems, 1
+    )
+    peers, chunks, _ = part.shape
+    copies[0].wait()
     for copy in arriving:
         copy.wait()
     grad = mm(cot[...], down[...].reshape(wg.shape))
-    gate_grad = (grad * up * sig * (1.0 + gate * (1.0 - sig))).astype(BF16)
-    up_grad = (grad * (gate * sig)).astype(BF16)
+    copies[1].wait()
+    copies[2].wait()
+    v = gate[...]
+    sig = jax.nn.sigmoid(v)
+    gate_grad = (grad * up[...] * sig * (1.0 + v * (1.0 - sig))).astype(BF16)
+    up_grad = (grad * (v * sig)).astype(BF16)
+    copies[3].wait()
+    copies[4].wait()
     for c in range(0, chunks, 2):
         at = lanes(c, 2)
         value = mm(gate_grad, wg[at, :], 1, 1) + mm(up_grad, wu[at, :], 1, 1)
@@ -169,30 +195,22 @@
                 ]
     for s in range(CAP):
         part[:, :, lanes(s)] = scr[s].reshape(peers, chunks, LANE).astype(BF16)
-    sent += start_all([(part, part_hbm)], sems, 6)
-    for copy in sent:
+    for copy in start_all([(part, part_hbm)], sems, 5):
         copy.wait()
 
 
-def fold_kernel(
-    place_ref, keep_hbm, swapped_hbm,
-    above_ref, below_ref, far_ref, outer_ref, inner_ref, under_ref, last_ref,
-    kept, came, sems,
-):
-    z = place_ref[0]
+def fold_kernel(steps, place_ref, keep_hbm, swapped_hbm, *refs):
+    targets, (kept, came, sems) = refs[: len(steps)], refs[len(steps) :]
+    z, core = place_ref[0], place_ref[1]
     chips = keep_hbm.shape[0]
     copies = []
-    for i, step in enumerate(FOLD):
-        chip = lax.rem(z + (step + chips), chips)
+    for i, step in enumerate(steps):
+        chip = lax.rem(z + step * (1 - 2 * core) + chips, chips)
         copies.append(
             start_all(
                 [(keep_hbm.at[chip], kept.at[i]), (swapped_hbm.at[chip], came.at[i])], sems, 2 * i
             )
         )
-    targets = (
-        above_ref.at[0], above_ref.at[1], below_ref, far_ref,
-        outer_ref, inner_ref, under_ref, last_ref,
-    )
     for i, target in enumerate(targets):
         for copy in copies[i]:
             copy.wait()
@@ -228,7 +246,12 @@
 
 def round_z(x, step):
     chips = lax.axis_size("z")
-    return lax.ppermute(x, "z", [(j, (j + step) % chips) for j in range(chips)])
+    pairs = [
+        (2 * j + core, (j + step * (1 - 2 * core)) % chips * 2 + core)
+        for j in range(chips)
+        for core in range(2)
+    ]
+    return lax.ppermute(x, ("z", "core"), pairs)
 
 
 def gather_features(own):
@@ -240,28 +263,32 @@
     return first, rest, over_core(first), over_core(rest)
 
 
-def reduce_features(place, keep, swapped):
-    blocks, lines, hidden = keep.shape
-    narrow = jax.ShapeDtypeStruct((lines, hidden), BF16)
-    wide = jax.ShapeDtypeStruct((lines, hidden), F32)
-    both = jax.ShapeDtypeStruct((2, lines, hidden), BF16)
-    pair, low, far_low, outer, inner, under, total = call(
-        fold_kernel,
-        (both, narrow, narrow, wide, wide, wide, wide),
+def fold(steps, dtypes, place, keep, swapped):
+    block = keep.shape[1:]
+    count = len(steps)
+    return call(
+        functools.partial(fold_kernel, steps),
+        tuple(jax.ShapeDtypeStruct(block, dtype) for dtype in dtypes),
         [SMEM, HBM, HBM],
-        (VMEM,) * 7,
-        [
-            pltpu.VMEM(keep.shape, BF16),
-            pltpu.VMEM(keep.shape, BF16),
-            pltpu.SemaphoreType.DMA((2 * blocks,)),
+        (VMEM,) * count,
+        [
+            pltpu.VMEM((count,) + block, BF16),
+            pltpu.VMEM((count,) + block, BF16),
+            pltpu.SemaphoreType.DMA((2 * count,)),
         ],
         24, keep.size, 6 * keep.size, "fold",
     )(place, keep, swapped)
-    above = round_z(pair, -1)
-    below = round_z(low, 1)
-    far_below = round_z(far_low, 3)
-    far_above = round_z((outer + above[1].astype(F32)).astype(BF16), -3)
-    near_above = round_z((inner + above[0].astype(F32)).astype(BF16), -1)
+
+
+def reduce_features(place, keep, swapped):
+    below, above, above_far, far_below = fold((2, -2, -4, 3), (BF16,) * 4, place, keep, swapped)
+    above = round_z(above, -1)
+    above_far = round_z(above_far, -1)
+    below = round_z(below, 1)
+    far_below = round_z(far_below, 3)
+    inner, outer, under, total = fold((-1, -3, 1, 0), (F32,) * 4, place, keep, swapped)
+    far_above = round_z((outer + above_far.astype(F32)).astype(BF16), -3)
+    near_above = round_z((inner + above.astype(F32)).astype(BF16), -1)
     near_below = round_z((under + below.astype(F32)).astype(BF16), 1)
     for arrived in (near_above, far_above, near_below, far_below):
         total = total + arrived.astype(F32)
@@ -292,9 +319,10 @@
         [
             pltpu.VMEM((n, width), BF16),
             pltpu.VMEM((n, width), BF16),
+            pltpu.VMEM(own.shape, BF16),
             pltpu.VMEM((2, peers, chunks, CAP * LANE), BF16),
             pltpu.VMEM((2 * CAP, peers * chunks, LANE), F32),
-            pltpu.SemaphoreType.DMA((5,)),
+            pltpu.SemaphoreType.DMA((6,)),
         ],
         58, 4 * slots * n * width, 4 << 20, "pack",
     )(ids, weight, tokens, cotangent, own)
@@ -303,33 +331,56 @@
 
     weights = pltpu.VMEM((width, hidden), BF16)
     features = pltpu.VMEM((chunks // 2, LANE, hidden), BF16)
-    part, send, keep = call(
-        expert_kernel,
+    inner = pltpu.VMEM((slots, hidden), F32)
+    send, keep, gate, up, cot = call(
+        forward_kernel,
         (
-            shape((peers, chunks, CAP * LANE), BF16),
             shape((chunks // 2, LANE, hidden), BF16),
             shape((chunks // 2, LANE, hidden), BF16),
+            shape((slots, hidden), F32),
+            shape((slots, hidden), F32),
+            shape((slots, width), BF16),
         ),
-        [SMEM] + [HBM] * 7,
-        (HBM,) * 3,
+        [SMEM] + [HBM] * 4,
+        (HBM,) * 5,
         [
             pltpu.VMEM((2, peers, chunks, CAP * LANE), BF16),
             weights,
             weights,
-            pltpu.VMEM((chunks, LANE, hidden), BF16),
             pltpu.VMEM((CAP, peers * chunks, LANE), F32),
             pltpu.VMEM((slots, width), BF16),
             pltpu.VMEM((slots, width), BF16),
             pltpu.VMEM((slots, width // 2), BF16),
             pltpu.VMEM((slots, width // 2), BF16),
+            inner,
+            inner,
             features,
             features,
+            pltpu.SemaphoreType.DMA((9,)),
+        ],
+        62, 3 * product, 14 << 20, "forward",
+    )(place, got, wg, wu, gathered[1])
+    swapped = over_core(send)
+
+    part = call(
+        backward_kernel,
+        shape((peers, chunks, CAP * LANE), BF16),
+        [SMEM] + [HBM] * 9,
+        HBM,
+        [
+            inner,
+            inner,
+            pltpu.VMEM((slots, width), BF16),
+            pltpu.VMEM((chunks, LANE, hidden), BF16),
+            weights,
+            weights,
+            pltpu.VMEM((CAP, peers * chunks, LANE), F32),
             pltpu.VMEM((peers, chunks, CAP * LANE), BF16),
             pltpu.SemaphoreType.DMA((7 + chunks,)),
         ],
-        58, 6 * product, 18 << 20, "expert",
-    )(place, got, wg, wu, *gathered)
-    swapped = over_core(send)
+        62, 3 * product, 14 << 20, "backward",
+    )(place, gate, up, cot, *gathered, wg, wu)
+
     down_part = reduce_features(place, keep, swapped)
     returned = lax.all_to_all(part, "expert", split_axis=0, concat_axis=0, tiled=True)
 

time: 150 us -> 149 us (level)
  waiting for transfers between devices: 33.7 us -> 12.7 us
  starting transfers between devices: 86.7 us -> 96.1 us
  Pallas kernels: 24 us -> 29.9 us
  local copies, waits for them, and re-layouts: 2.43 us -> 5.81 us
  other arithmetic: 0.92 us -> 2.68 us
    ppermute x12 -> x13, waiting for transfers between devices: 32.2 us -> 10.4 us  [round_z(): return lax.ppermute(x, ('z', 'core'), pairs)]
    ppermute x12 -> x13, starting transfers between devices: 50.3 us -> 59.2 us  [round_z(): return lax.ppermute(x, ('z', 'core'), pairs)]
    pallas_call x2 -> x4, Pallas kernels: 14.3 us -> 22.6 us  [the longest x1 8.63 us: on_device(): call(backward_kernel, shape((peers, chunks, CAP * LANE), BF16), [SMEM] +...]
    pallas_call x1, Pallas kernels: 7.78 us -> 4.42 us  [on_device(): call(functools.partial(pack_kernel, peers), (shape((peers, chunks, 2 * CA...]
    unnamed x19 -> x15, local copies, waits for them, and re-layouts: 2.39 us -> 5.1 us
  transfers between devices with their start and end apart: 17 -> 18, of which waited for: 10 -> 3; matrix products, arithmetic and copies ran while one was open for 1% -> 3% of each run, Pallas kernels for 4% -> 17%
where the time goes in v4:
time: 149 us; the launch traced here: 148 us
  starting transfers between devices  96.1 us (64%)
  Pallas kernels  29.9 us (20%)
  waiting for transfers between devices  12.7 us (9%)
  local copies, waits for them, and re-layouts  5.81 us (4%)
  other arithmetic  2.68 us (2%)
    ppermute x13, starting transfers between devices, round_z(): return lax.ppermute(x, ('z', 'core'), pairs)  59.2 us
    all_to_all x1, starting transfers between devices, on_device(): lax.all_to_all(packed, 'expert', split_axis=0, concat_axis=0, tiled=True)  17.6 us
    all_to_all x1, starting transfers between devices, on_device(): lax.all_to_all(part, 'expert', split_axis=0, concat_axis=0, tiled=True)  13 us
    ppermute x13, waiting for transfers between devices, round_z(): return lax.ppermute(x, ('z', 'core'), pairs)  10.4 us
    pallas_call x1, Pallas kernels, on_device(): call(backward_kernel, shape((peers, chunks, CAP * LANE), BF16), [SMEM] +...  8.63 us
    pallas_call x1, Pallas kernels, on_device(): call(forward_kernel, (shape((chunks // 2, LANE, hidden), BF16), shape((ch...  7.62 us
    pallas_call x2, Pallas kernels, fold(): call(functools.partial(fold_kernel, steps), tuple((jax.ShapeDtypeStruct(b...  6.37 us
    ppermute x3, starting transfers between devices, over_core(): return lax.ppermute(x, 'core', [(0, 1), (1, 0)])  6.29 us
  transfers between devices with their start and end apart: 18, of which 3 were waited for; matrix products, arithmetic and copies ran while one was open for 3% of the time, Pallas kernels for 17%

profile of v4, /device:TPU:14, one launch (start us, length us, event | category | flops | bytes accessed | tf_op | source)
XLA Modules:
  0.0 148.2 jit_solution(14643120146910376589)
XLA Ops:
  0.6 4.4 %pack.1 = (bf16[64,16,768]{2,1,0:T(8,128)(2,1)}, bf16[128,768]{1,0:T(8,128)(2,1)}) custom-call(s32[1,128]{1,0:T(1,128)} %bitcast.24, f32[1,128]{1,0:T(1,128)} %bitcast.32, bf16[128,2048]{1,0:T(8,128)(2,1)} %tok_hbm.1, bf16[128,2048]{1,0:T(8,128)(2,1)} %cot_hbm.1, bf16[128,768]{1,0:T(8,128)(2,1)} %bitcast.31), custom_call_target="tpu_custom_call" | custom-call | flops 201326592 | bytes 4194304 | tf_op jit(solution)/shard_map/pack/pallas_call | solution.py:314
  5.1 17.6 %all-to-all-start = ((bf16[64,16,768]{2,1,0:T(8,128)(2,1)}), bf16[64,16,768]{2,1,0:T(8,128)(2,1)S(1)}, u32[]{:S(2)}, u32[]{:S(2)}) async-start(bf16[64,16,768]{2,1,0:T(8,128)(2,1)} %get-tuple-element.17), calls=%async_computation | async-start | bytes 3145728 | tf_op jit(solution)/shard_map/all_to_all | solution.py:329
  24.6 11.3 %collective-permute-start.1 = (bf16[128,768]{1,0:T(8,128)(2,1)S(1)}, bf16[128,768]{1,0:T(8,128)(2,1)S(1)}, u32[]{:S(2)}, u32[]{:S(2)}) collective-permute-start(bf16[128,768]{1,0:T(8,128)(2,1)S(1)} %copy-done.4), channel_id=1, source_target_pairs={{0,6},{1,11},{2,8},{3,13},{4,10},{5,15},{6,12},{7,1},{8,14},{9,3},... | collective-permute-start | bytes 589832 | tf_op jit(solution)/shard_map/ppermute | solution.py:254
  35.9 4.1 %collective-permute-start.3 = (bf16[128,768]{1,0:T(8,128)(2,1)S(1)}, bf16[128,768]{1,0:T(8,128)(2,1)S(1)}, u32[]{:S(2)}, u32[]{:S(2)}) collective-permute-start(bf16[128,768]{1,0:T(8,128)(2,1)S(1)} %copy-done.4), channel_id=1, source_target_pairs={{0,14},{1,3},{2,0},{3,5},{4,2},{5,7},{6,4},{7,9},{8,6},{9,11},{10,... | collective-permute-start | bytes 589832 | tf_op jit(solution)/shard_map/ppermute | solution.py:254
  40.1 5.7 %collective-permute-start.5 = (bf16[128,768]{1,0:T(8,128)(2,1)S(1)}, bf16[128,768]{1,0:T(8,128)(2,1)S(1)}, u32[]{:S(2)}, u32[]{:S(2)}) collective-permute-start(bf16[128,768]{1,0:T(8,128)(2,1)S(1)} %copy-done.4), channel_id=1, source_target_pairs={{0,10},{1,7},{2,12},{3,9},{4,14},{5,11},{6,0},{7,13},{8,2},{9,15},... | collective-permute-start | bytes 589832 | tf_op jit(solution)/shard_map/ppermute | solution.py:254
  47.1 10.8 %collective-permute-start.2 = (bf16[256,768]{1,0:T(8,128)(2,1)S(1)}, bf16[256,768]{1,0:T(8,128)(2,1)S(1)}, u32[]{:S(2)}, u32[]{:S(2)}) collective-permute-start(bf16[256,768]{1,0:T(8,128)(2,1)S(1)} %pad_maximum_fusion.1), channel_id=1, source_target_pairs={{0,2},{1,15},{2,4},{3,1},{4,6},{5,3},{6,8},{7,5},{8,10},{9,7},{10,... | collective-permute-start | bytes 1179656 | tf_op jit(solution)/shard_map/ppermute | solution.py:254
  64.5 5.6 %collective-permute-done.4 = bf16[128,768]{1,0:T(8,128)(2,1)S(1)} collective-permute-done((bf16[128,768]{1,0:T(8,128)(2,1)S(1)}, bf16[128,768]{1,0:T(8,128)(2,1)S(1)}, u32[]{:S(2)}, u32[]{:S(2)}) %collective-permute-start.4) | collective-permute-done | bytes 196640 | tf_op jit(solution)/shard_map/ppermute | solution.py:254
  72.2 7.6 %forward.1 = (bf16[8,128,768]{2,1,0:T(8,128)(2,1)}, bf16[8,128,768]{2,1,0:T(8,128)(2,1)}, f32[192,768]{1,0:T(8,128)}, f32[192,768]{1,0:T(8,128)}, bf16[192,2048]{1,0:T(8,128)(2,1)}) custom-call(s32[2]{0:T(128)} %pad_add_fusion.place_ref, bf16[64,16,768]{2,1,0:T(8,128)(2,1)} %copy-done.3, bf16[2048,768]{1,0:T(8,128)(2,1)} %bitcast.26, ...), custom_call_target="tpu_custom_call" | custom-call | flops 1811939328 | bytes 14680064 | tf_op jit(solution)/shard_map/forward/pallas_call | solution.py:335
  79.9 2.5 %collective-permute-start.8 = (bf16[8,128,768]{2,1,0:T(8,128)(2,1)}, bf16[8,128,768]{2,1,0:T(8,128)(2,1)S(1)}, u32[]{:S(2)}, u32[]{:S(2)}) collective-permute-start(bf16[8,128,768]{2,1,0:T(8,128)(2,1)} %get-tuple-element.23), channel_id=1, source_target_pairs={{0,1},{1,0},{2,3},{3,2},{4,5},{5,4},{6,7},{7,6},{8,9},{9,8},{10,11... | collective-permute-start | bytes 4718600 | tf_op jit(solution)/shard_map/ppermute | solution.py:244
  82.3 1.9 %collective-permute-start.7 = (bf16[3,128,768]{2,1,0:T(8,128)(2,1)}, bf16[3,128,768]{2,1,0:T(8,128)(2,1)}, u32[]{:S(2)}, u32[]{:S(2)}) collective-permute-start(bf16[3,128,768]{2,1,0:T(8,128)(2,1)} %pad_maximum_fusion.after_hbm.rest_hbm), channel_id=1, source_target_pairs={{0,1},{1,0},{2,3},{3,2},{4,5},{5,4},{6,7},{7,6},{8,9},{9,8},{10,11... | collective-permute-start | bytes 1769480 | tf_op jit(solution)/shard_map/ppermute | solution.py:244
  84.3 2.3 %collective-permute-done.7.rest_other_hbm = bf16[3,128,768]{2,1,0:T(8,128)(2,1)} collective-permute-done((bf16[3,128,768]{2,1,0:T(8,128)(2,1)}, bf16[3,128,768]{2,1,0:T(8,128)(2,1)}, u32[]{:S(2)}, u32[]{:S(2)}) %collective-permute-start.7) | collective-permute-done | bytes 589856 | tf_op jit(solution)/shard_map/ppermute | solution.py:244
  86.6 8.6 %backward.1 = bf16[64,16,384]{2,1,0:T(8,128)(2,1)} custom-call(s32[2]{0:T(128)} %pad_add_fusion.place_ref, f32[192,768]{1,0:T(8,128)} %get-tuple-element.19.gate_hbm, f32[192,768]{1,0:T(8,128)} %get-tuple-element.20.up_hbm, bf16[192,2048]{1,0:T(8,128)(2,1)} %get-tuple-element.21.cot_hbm, bf16[5,128,768]{2,1,0:T(8,128)(2,1)} %bitcast_dynamic-update-slice_fusion.first_hbm, ...), custom_call_target="tpu_custom_call" | custom-call | flops 1811939328 | bytes 14680064 | tf_op jit(solution)/shard_map/backward/pallas_call | solution.py:365
  95.2 13.0 %all-to-all-start.1 = ((bf16[64,16,384]{2,1,0:T(8,128)(2,1)}), bf16[64,16,384]{2,1,0:T(8,128)(2,1)}, u32[]{:S(2)}, u32[]{:S(2)}) async-start(bf16[64,16,384]{2,1,0:T(8,128)(2,1)} %backward.1), calls=%async_computation.1 | async-start | bytes 1572864 | tf_op jit(solution)/shard_map/all_to_all | solution.py:385
  108.3 3.5 %fold.3 = (bf16[128,768]{1,0:T(8,128)(2,1)S(1)}, bf16[128,768]{1,0:T(8,128)(2,1)S(1)}, bf16[128,768]{1,0:T(8,128)(2,1)S(1)}, bf16[128,768]{1,0:T(8,128)(2,1)}) custom-call(s32[2]{0:T(128)S(1)} %copy-done.1, bf16[8,128,768]{2,1,0:T(8,128)(2,1)S(1)} %copy-done, bf16[8,128,768]{2,1,0:T(8,128)(2,1)S(1)} %collective-permute-done.8.swapped_hbm), custom_call_target="tpu_custom_call" | custom-call | flops 786432 | bytes 4718592 | tf_op jit(solution)/shard_map/fold/pallas_call | solution.py:269
  111.8 2.9 %collective-permute-start.9 = (bf16[128,768]{1,0:T(8,128)(2,1)S(1)}, bf16[128,768]{1,0:T(8,128)(2,1)S(1)}, u32[]{:S(2)}, u32[]{:S(2)}) collective-permute-start(bf16[128,768]{1,0:T(8,128)(2,1)S(1)} %get-tuple-element.26), channel_id=1, source_target_pairs={{0,14},{1,3},{2,0},{3,5},{4,2},{5,7},{6,4},{7,9},{8,6},{9,11},{10,... | collective-permute-start | bytes 589832 | tf_op jit(solution)/shard_map/ppermute | solution.py:254
  114.7 2.6 %collective-permute-start.11 = (bf16[128,768]{1,0:T(8,128)(2,1)S(1)}, bf16[128,768]{1,0:T(8,128)(2,1)S(1)}, u32[]{:S(2)}, u32[]{:S(2)}) collective-permute-start(bf16[128,768]{1,0:T(8,128)(2,1)S(1)} %get-tuple-element.28), channel_id=1, source_target_pairs={{0,14},{1,3},{2,0},{3,5},{4,2},{5,7},{6,4},{7,9},{8,6},{9,11},{10,... | collective-permute-start | bytes 589832 | tf_op jit(solution)/shard_map/ppermute | solution.py:254
  117.3 3.2 %collective-permute-start.13 = (bf16[128,768]{1,0:T(8,128)(2,1)S(1)}, bf16[128,768]{1,0:T(8,128)(2,1)S(1)}, u32[]{:S(2)}, u32[]{:S(2)}) collective-permute-start(bf16[128,768]{1,0:T(8,128)(2,1)S(1)} %get-tuple-element.30), channel_id=1, source_target_pairs={{0,2},{1,15},{2,4},{3,1},{4,6},{5,3},{6,8},{7,5},{8,10},{9,7},{10,... | collective-permute-start | bytes 589832 | tf_op jit(solution)/shard_map/ppermute | solution.py:254
  120.6 2.4 %collective-permute-start.15 = (bf16[128,768]{1,0:T(8,128)(2,1)}, bf16[128,768]{1,0:T(8,128)(2,1)}, u32[]{:S(2)}, u32[]{:S(2)}) collective-permute-start(bf16[128,768]{1,0:T(8,128)(2,1)} %get-tuple-element.31), channel_id=1, source_target_pairs={{0,6},{1,11},{2,8},{3,13},{4,10},{5,15},{6,12},{7,1},{8,14},{9,3},... | collective-permute-start | bytes 589832 | tf_op jit(solution)/shard_map/ppermute | solution.py:254
  123.0 2.8 %fold.2 = (f32[128,768]{1,0:T(8,128)S(1)}, f32[128,768]{1,0:T(8,128)S(1)}, f32[128,768]{1,0:T(8,128)S(1)}, f32[128,768]{1,0:T(8,128)S(1)}) custom-call(s32[2]{0:T(128)S(1)} %copy-done.1, bf16[8,128,768]{2,1,0:T(8,128)(2,1)S(1)} %copy-done, bf16[8,128,768]{2,1,0:T(8,128)(2,1)S(1)} %collective-permute-done.8.swapped_hbm), custom_call_target="tpu_custom_call" | custom-call | flops 786432 | bytes 4718592 | tf_op jit(solution)/shard_map/fold/pallas_call | solution.py:269
  125.9 4.6 %collective-permute-start.10 = (bf16[128,768]{1,0:T(8,128)(2,1)S(1)}, bf16[128,768]{1,0:T(8,128)(2,1)S(1)}, u32[]{:S(2)}, u32[]{:S(2)}) collective-permute-start(bf16[128,768]{1,0:T(8,128)(2,1)S(1)} %add_convert_fusion.2), channel_id=1, source_target_pairs={{0,14},{1,3},{2,0},{3,5},{4,2},{5,7},{6,4},{7,9},{8,6},{9,11},{10,... | collective-permute-start | bytes 589832 | tf_op jit(solution)/shard_map/ppermute | solution.py:254
  130.5 4.5 %collective-permute-start.12 = (bf16[128,768]{1,0:T(8,128)(2,1)S(1)}, bf16[128,768]{1,0:T(8,128)(2,1)S(1)}, u32[]{:S(2)}, u32[]{:S(2)}) collective-permute-start(bf16[128,768]{1,0:T(8,128)(2,1)S(1)} %add_convert_fusion.1), channel_id=1, source_target_pairs={{0,10},{1,7},{2,12},{3,9},{4,14},{5,11},{6,0},{7,13},{8,2},{9,15},... | collective-permute-start | bytes 589832 | tf_op jit(solution)/shard_map/ppermute | solution.py:254
  135.1 3.2 %collective-permute-start.14 = (bf16[128,768]{1,0:T(8,128)(2,1)S(1)}, bf16[128,768]{1,0:T(8,128)(2,1)S(1)}, u32[]{:S(2)}, u32[]{:S(2)}) collective-permute-start(bf16[128,768]{1,0:T(8,128)(2,1)S(1)} %add_convert_fusion), channel_id=1, source_target_pairs={{0,2},{1,15},{2,4},{3,1},{4,6},{5,3},{6,8},{7,5},{8,10},{9,7},{10,... | collective-permute-start | bytes 589832 | tf_op jit(solution)/shard_map/ppermute | solution.py:254
  138.4 2.8 %collect.1 = bf16[128,2048]{1,0:T(8,128)(2,1)} custom-call(s32[1,128]{1,0:T(1,128)S(1)} %bitcast.25, bf16[64,16,384]{2,1,0:T(8,128)(2,1)} %all-to-all-done.1.got_hbm), custom_call_target="tpu_custom_call" | custom-call | flops 100663296 | bytes 2097152 | tf_op jit(solution)/shard_map/collect/pallas_call | solution.py:387
  141.2 4.8 %collective-permute-done.12 = bf16[128,768]{1,0:T(8,128)(2,1)S(1)} collective-permute-done((bf16[128,768]{1,0:T(8,128)(2,1)S(1)}, bf16[128,768]{1,0:T(8,128)(2,1)S(1)}, u32[]{:S(2)}, u32[]{:S(2)}) %collective-permute-start.12) | collective-permute-done | bytes 196640 | tf_op jit(solution)/shard_map/ppermute | solution.py:254
  (42 shorter events, 14.3 us)
Async XLA Ops:
  5.1 17.6 %copy-start.4 = (bf16[128,768]{1,0:T(8,128)(2,1)S(1)}, bf16[128,768]{1,0:T(8,128)(2,1)}, u32[]{:S(2)}) copy-start(bf16[128,768]{1,0:T(8,128)(2,1)} %get-tuple-element.18) | copy-start | bytes 589828
  5.1 66.0 %all-to-all-start = ((bf16[64,16,768]{2,1,0:T(8,128)(2,1)}), bf16[64,16,768]{2,1,0:T(8,128)(2,1)S(1)}, u32[]{:S(2)}, u32[]{:S(2)}) async-start(bf16[64,16,768]{2,1,0:T(8,128)(2,1)} %get-tuple-element.17), calls=%async_computation | async-start | bytes 3145728 | tf_op jit(solution)/shard_map/all_to_all | solution.py:329
  22.7 24.3 %collective-permute-start = (bf16[128,768]{1,0:T(8,128)(2,1)S(1)}, bf16[128,768]{1,0:T(8,128)(2,1)S(1)}, u32[]{:S(2)}, u32[]{:S(2)}) collective-permute-start(bf16[128,768]{1,0:T(8,128)(2,1)S(1)} %copy-done.4), channel_id=1, source_target_pairs={{0,2},{1,15},{2,4},{3,1},{4,6},{5,3},{6,8},{7,5},{8,10},{9,7},{10,... | collective-permute-start | bytes 589832 | tf_op jit(solution)/shard_map/ppermute | solution.py:254
  24.6 22.4 %collective-permute-start.1 = (bf16[128,768]{1,0:T(8,128)(2,1)S(1)}, bf16[128,768]{1,0:T(8,128)(2,1)S(1)}, u32[]{:S(2)}, u32[]{:S(2)}) collective-permute-start(bf16[128,768]{1,0:T(8,128)(2,1)S(1)} %copy-done.4), channel_id=1, source_target_pairs={{0,6},{1,11},{2,8},{3,13},{4,10},{5,15},{6,12},{7,1},{8,14},{9,3},... | collective-permute-start | bytes 589832 | tf_op jit(solution)/shard_map/ppermute | solution.py:254
  35.9 22.6 %collective-permute-start.3 = (bf16[128,768]{1,0:T(8,128)(2,1)S(1)}, bf16[128,768]{1,0:T(8,128)(2,1)S(1)}, u32[]{:S(2)}, u32[]{:S(2)}) collective-permute-start(bf16[128,768]{1,0:T(8,128)(2,1)S(1)} %copy-done.4), channel_id=1, source_target_pairs={{0,14},{1,3},{2,0},{3,5},{4,2},{5,7},{6,4},{7,9},{8,6},{9,11},{10,... | collective-permute-start | bytes 589832 | tf_op jit(solution)/shard_map/ppermute | solution.py:254
  40.1 19.9 %collective-permute-start.5 = (bf16[128,768]{1,0:T(8,128)(2,1)S(1)}, bf16[128,768]{1,0:T(8,128)(2,1)S(1)}, u32[]{:S(2)}, u32[]{:S(2)}) collective-permute-start(bf16[128,768]{1,0:T(8,128)(2,1)S(1)} %copy-done.4), channel_id=1, source_target_pairs={{0,10},{1,7},{2,12},{3,9},{4,14},{5,11},{6,0},{7,13},{8,2},{9,15},... | collective-permute-start | bytes 589832 | tf_op jit(solution)/shard_map/ppermute | solution.py:254
  47.1 17.4 %collective-permute-start.2 = (bf16[256,768]{1,0:T(8,128)(2,1)S(1)}, bf16[256,768]{1,0:T(8,128)(2,1)S(1)}, u32[]{:S(2)}, u32[]{:S(2)}) collective-permute-start(bf16[256,768]{1,0:T(8,128)(2,1)S(1)} %pad_maximum_fusion.1), channel_id=1, source_target_pairs={{0,2},{1,15},{2,4},{3,1},{4,6},{5,3},{6,8},{7,5},{8,10},{9,7},{10,... | collective-permute-start | bytes 1179656 | tf_op jit(solution)/shard_map/ppermute | solution.py:254
  60.6 25.9 %collective-permute-start.6 = (bf16[5,128,768]{2,1,0:T(8,128)(2,1)}, bf16[5,128,768]{2,1,0:T(8,128)(2,1)}, u32[]{:S(2)}, u32[]{:S(2)}) collective-permute-start(bf16[5,128,768]{2,1,0:T(8,128)(2,1)} %bitcast_dynamic-update-slice_fusion.first_hbm), channel_id=1, source_target_pairs={{0,1},{1,0},{2,3},{3,2},{4,5},{5,4},{6,7},{7,6},{8,9},{9,8},{10,11... | collective-permute-start | bytes 2949128 | tf_op jit(solution)/shard_map/ppermute | solution.py:244
  62.5 7.6 %collective-permute-start.4 = (bf16[128,768]{1,0:T(8,128)(2,1)S(1)}, bf16[128,768]{1,0:T(8,128)(2,1)S(1)}, u32[]{:S(2)}, u32[]{:S(2)}) collective-permute-start(bf16[128,768]{1,0:T(8,128)(2,1)S(1)} %collective-permute-done.3), channel_id=1, source_target_pairs={{0,14},{1,3},{2,0},{3,5},{4,2},{5,7},{6,4},{7,9},{8,6},{9,11},{10,... | collective-permute-start | bytes 589832 | tf_op jit(solution)/shard_map/ppermute | solution.py:254
  71.1 1.2 copy-start.3
  79.9 28.4 %collective-permute-start.8 = (bf16[8,128,768]{2,1,0:T(8,128)(2,1)}, bf16[8,128,768]{2,1,0:T(8,128)(2,1)S(1)}, u32[]{:S(2)}, u32[]{:S(2)}) collective-permute-start(bf16[8,128,768]{2,1,0:T(8,128)(2,1)} %get-tuple-element.23), channel_id=1, source_target_pairs={{0,1},{1,0},{2,3},{3,2},{4,5},{5,4},{6,7},{7,6},{8,9},{9,8},{10,11... | collective-permute-start | bytes 4718600 | tf_op jit(solution)/shard_map/ppermute | solution.py:244
  82.3 4.2 %collective-permute-start.7 = (bf16[3,128,768]{2,1,0:T(8,128)(2,1)}, bf16[3,128,768]{2,1,0:T(8,128)(2,1)}, u32[]{:S(2)}, u32[]{:S(2)}) collective-permute-start(bf16[3,128,768]{2,1,0:T(8,128)(2,1)} %pad_maximum_fusion.after_hbm.rest_hbm), channel_id=1, source_target_pairs={{0,1},{1,0},{2,3},{3,2},{4,5},{5,4},{6,7},{7,6},{8,9},{9,8},{10,11... | collective-permute-start | bytes 1769480 | tf_op jit(solution)/shard_map/ppermute | solution.py:244
  95.2 13.1 %copy-start = (bf16[8,128,768]{2,1,0:T(8,128)(2,1)S(1)}, bf16[8,128,768]{2,1,0:T(8,128)(2,1)}, u32[]{:S(2)}) copy-start(bf16[8,128,768]{2,1,0:T(8,128)(2,1)} %get-tuple-element.22.keep_hbm) | copy-start | bytes 4718596
  95.2 13.1 %copy-start.1 = (s32[2]{0:T(128)S(1)}, s32[2]{0:T(128)}, u32[]{:S(2)}) copy-start(s32[2]{0:T(128)} %pad_add_fusion.place_ref) | copy-start | bytes 28
  95.2 43.1 %all-to-all-start.1 = ((bf16[64,16,384]{2,1,0:T(8,128)(2,1)}), bf16[64,16,384]{2,1,0:T(8,128)(2,1)}, u32[]{:S(2)}, u32[]{:S(2)}) async-start(bf16[64,16,384]{2,1,0:T(8,128)(2,1)} %backward.1), calls=%async_computation.1 | async-start | bytes 1572864 | tf_op jit(solution)/shard_map/all_to_all | solution.py:385
  111.8 14.0 %collective-permute-start.9 = (bf16[128,768]{1,0:T(8,128)(2,1)S(1)}, bf16[128,768]{1,0:T(8,128)(2,1)S(1)}, u32[]{:S(2)}, u32[]{:S(2)}) collective-permute-start(bf16[128,768]{1,0:T(8,128)(2,1)S(1)} %get-tuple-element.26), channel_id=1, source_target_pairs={{0,14},{1,3},{2,0},{3,5},{4,2},{5,7},{6,4},{7,9},{8,6},{9,11},{10,... | collective-permute-start | bytes 589832 | tf_op jit(solution)/shard_map/ppermute | solution.py:254
  114.7 15.8 %collective-permute-start.11 = (bf16[128,768]{1,0:T(8,128)(2,1)S(1)}, bf16[128,768]{1,0:T(8,128)(2,1)S(1)}, u32[]{:S(2)}, u32[]{:S(2)}) collective-permute-start(bf16[128,768]{1,0:T(8,128)(2,1)S(1)} %get-tuple-element.28), channel_id=1, source_target_pairs={{0,14},{1,3},{2,0},{3,5},{4,2},{5,7},{6,4},{7,9},{8,6},{9,11},{10,... | collective-permute-start | bytes 589832 | tf_op jit(solution)/shard_map/ppermute | solution.py:254
  117.3 17.7 %collective-permute-start.13 = (bf16[128,768]{1,0:T(8,128)(2,1)S(1)}, bf16[128,768]{1,0:T(8,128)(2,1)S(1)}, u32[]{:S(2)}, u32[]{:S(2)}) collective-permute-start(bf16[128,768]{1,0:T(8,128)(2,1)S(1)} %get-tuple-element.30), channel_id=1, source_target_pairs={{0,2},{1,15},{2,4},{3,1},{4,6},{5,3},{6,8},{7,5},{8,10},{9,7},{10,... | collective-permute-start | bytes 589832 | tf_op jit(solution)/shard_map/ppermute | solution.py:254
  120.6 20.6 %collective-permute-start.15 = (bf16[128,768]{1,0:T(8,128)(2,1)}, bf16[128,768]{1,0:T(8,128)(2,1)}, u32[]{:S(2)}, u32[]{:S(2)}) collective-permute-start(bf16[128,768]{1,0:T(8,128)(2,1)} %get-tuple-element.31), channel_id=1, source_target_pairs={{0,6},{1,11},{2,8},{3,13},{4,10},{5,15},{6,12},{7,1},{8,14},{9,3},... | collective-permute-start | bytes 589832 | tf_op jit(solution)/shard_map/ppermute | solution.py:254
  125.8 12.6 %copy-start.2 = (s32[128,1]{0,1:T(1,128)S(1)}, s32[128,1]{0,1:T(1,128)}, u32[]{:S(2)}) copy-start(s32[128,1]{0,1:T(1,128)} %param.9) | copy-start | bytes 1540
  125.9 15.4 %collective-permute-start.10 = (bf16[128,768]{1,0:T(8,128)(2,1)S(1)}, bf16[128,768]{1,0:T(8,128)(2,1)S(1)}, u32[]{:S(2)}, u32[]{:S(2)}) collective-permute-start(bf16[128,768]{1,0:T(8,128)(2,1)S(1)} %add_convert_fusion.2), channel_id=1, source_target_pairs={{0,14},{1,3},{2,0},{3,5},{4,2},{5,7},{6,4},{7,9},{8,6},{9,11},{10,... | collective-permute-start | bytes 589832 | tf_op jit(solution)/shard_map/ppermute | solution.py:254
  130.5 15.5 %collective-permute-start.12 = (bf16[128,768]{1,0:T(8,128)(2,1)S(1)}, bf16[128,768]{1,0:T(8,128)(2,1)S(1)}, u32[]{:S(2)}, u32[]{:S(2)}) collective-permute-start(bf16[128,768]{1,0:T(8,128)(2,1)S(1)} %add_convert_fusion.1), channel_id=1, source_target_pairs={{0,10},{1,7},{2,12},{3,9},{4,14},{5,11},{6,0},{7,13},{8,2},{9,15},... | collective-permute-start | bytes 589832 | tf_op jit(solution)/shard_map/ppermute | solution.py:254
  135.1 10.9 %collective-permute-start.14 = (bf16[128,768]{1,0:T(8,128)(2,1)S(1)}, bf16[128,768]{1,0:T(8,128)(2,1)S(1)}, u32[]{:S(2)}, u32[]{:S(2)}) collective-permute-start(bf16[128,768]{1,0:T(8,128)(2,1)S(1)} %add_convert_fusion), channel_id=1, source_target_pairs={{0,2},{1,15},{2,4},{3,1},{4,6},{5,3},{6,8},{7,5},{8,10},{9,7},{10,... | collective-permute-start | bytes 589832 | tf_op jit(solution)/shard_map/ppermute | solution.py:254

commit v5 on v4

--- a/solution.py
+++ b/solution.py
@@ -10,6 +10,7 @@
 CAP = 3
 LANE = 128
 NEAR = (0, -1, 1, -3, 3, -2, -4, 2)
+FOLD = (-2, -4, 2, 3, -3, -1, 1, 0)
 BF16 = jnp.bfloat16
 F32 = jnp.float32
 
@@ -102,7 +103,7 @@
 
 def forward_kernel(
     place_ref, got_hbm, wg_hbm, wu_hbm, after_hbm,
-    send_hbm, keep_hbm, gate_hbm, up_hbm, cot_hbm,
+    send_a_hbm, send_b_hbm, keep_a_hbm, keep_b_hbm, gate_hbm, up_hbm, cot_hbm,
     got, wg, wu, scr, rows, cot, own, other, gate, up, send, keep, sems,
 ):
     copies = start_all(
@@ -115,7 +116,8 @@
         sems,
     )
     chunks = got.shape[2]
-    first = place_ref[1] == 0
+    z, core = place_ref[0], place_ref[1]
+    first = core == 0
     copies[0].wait()
     for lines, c, value in to_rows(got.at[0], scr):
         rows[lines, lanes(c)] = value.astype(BF16)
@@ -137,21 +139,30 @@
             own[lines, lanes(c // 2)] = jnp.where(first, even, value).astype(BF16)
             other[lines, lanes(c // 2)] = jnp.where(first, value, even).astype(BF16)
     sent += start_all([(cot, cot_hbm)], sems, 6)
-    for i, (source, target, target_hbm) in enumerate(
-        ((other, send, send_hbm), (own, keep, keep_hbm))
+    chips = chunks // 2
+    half = chips // 2
+    for i, (source, target, a_hbm, b_hbm, ahead) in enumerate(
+        (
+            (other, send, send_a_hbm, send_b_hbm, 2 * core - 1),
+            (own, keep, keep_a_hbm, keep_b_hbm, 1 - 2 * core),
+        )
     ):
-        for b in range(0, chunks // 2, 2):
+        for b in range(0, chips, 2):
             value = mm(source[:, lanes(b, 2)], hidden, 0, 0).astype(BF16)
             target[b] = value[:LANE]
             target[b + 1] = value[LANE:]
-        sent += start_all([(target, target_hbm)], sems, 7 + i)
+        moves = []
+        for at, step in enumerate(FOLD):
+            chip = lax.rem(z + step * ahead + chips, chips)
+            moves.append((target.at[chip], (a_hbm if at < half else b_hbm).at[at % half]))
+        sent += start_all(moves, sems, 7 + i * chips)
     for copy in sent:
         copy.wait()
 
 
 def backward_kernel(
     place_ref, gate_hbm, up_hbm, cot_hbm,
-    first_hbm, rest_hbm, first_other_hbm, rest_other_hbm, wg_hbm, wu_hbm,
+    first_hbm, rest_hbm, first_other_hbm, rest_other_hbm, wg_hbm, wu_hbm, after_hbm,
     part_hbm,
     gate, up, cot, down, wg, wu, scr, part, sems,
 ):
@@ -199,24 +210,6 @@
         copy.wait()
 
 
-def fold_kernel(steps, place_ref, keep_hbm, swapped_hbm, *refs):
-    targets, (kept, came, sems) = refs[: len(steps)], refs[len(steps) :]
-    z, core = place_ref[0], place_ref[1]
-    chips = keep_hbm.shape[0]
-    copies = []
-    for i, step in enumerate(steps):
-        chip = lax.rem(z + step * (1 - 2 * core) + chips, chips)
-        copies.append(
-            start_all(
-                [(keep_hbm.at[chip], kept.at[i]), (swapped_hbm.at[chip], came.at[i])], sems, 2 * i
-            )
-        )
-    for i, target in enumerate(targets):
-        for copy in copies[i]:
-            copy.wait()
-        target[...] = (kept[i].astype(F32) + came[i].astype(F32)).astype(target.dtype)
-
-
 def collect_kernel(peers, ids_ref, got_hbm, out_ref, got, scr, rows, sem):
     copy = pltpu.make_async_copy(got_hbm, got, sem)
     copy.start()
@@ -263,32 +256,12 @@
     return first, rest, over_core(first), over_core(rest)
 
 
-def fold(steps, dtypes, place, keep, swapped):
-    block = keep.shape[1:]
-    count = len(steps)
-    return call(
-        functools.partial(fold_kernel, steps),
-        tuple(jax.ShapeDtypeStruct(block, dtype) for dtype in dtypes),
-        [SMEM, HBM, HBM],
-        (VMEM,) * count,
-        [
-            pltpu.VMEM((count,) + block, BF16),
-            pltpu.VMEM((count,) + block, BF16),
-            pltpu.SemaphoreType.DMA((2 * count,)),
-        ],
-        24, keep.size, 6 * keep.size, "fold",
-    )(place, keep, swapped)
-
-
-def reduce_features(place, keep, swapped):
-    below, above, above_far, far_below = fold((2, -2, -4, 3), (BF16,) * 4, place, keep, swapped)
-    above = round_z(above, -1)
-    above_far = round_z(above_far, -1)
-    below = round_z(below, 1)
-    far_below = round_z(far_below, 3)
-    inner, outer, under, total = fold((-1, -3, 1, 0), (F32,) * 4, place, keep, swapped)
-    far_above = round_z((outer + above_far.astype(F32)).astype(BF16), -3)
-    near_above = round_z((inner + above.astype(F32)).astype(BF16), -1)
+def reduce_features(above, below, far_below, keep, swapped):
+    outer, inner, under, total = [
+        keep[i].astype(F32) + swapped[i].astype(F32) for i in range(keep.shape[0])
+    ]
+    far_above = round_z((outer + above[1].astype(F32)).astype(BF16), -3)
+    near_above = round_z((inner + above[0].astype(F32)).astype(BF16), -1)
     near_below = round_z((under + below.astype(F32)).astype(BF16), 1)
     for arrived in (near_above, far_above, near_below, far_below):
         total = total + arrived.astype(F32)
@@ -332,17 +305,20 @@
     weights = pltpu.VMEM((width, hidden), BF16)
     features = pltpu.VMEM((chunks // 2, LANE, hidden), BF16)
     inner = pltpu.VMEM((slots, hidden), F32)
-    send, keep, gate, up, cot = call(
+    quarter = shape((chunks // 4, LANE, hidden), BF16)
+    send_a, send_b, keep_a, keep_b, gate, up, cot = call(
         forward_kernel,
         (
-            shape((chunks // 2, LANE, hidden), BF16),
-            shape((chunks // 2, LANE, hidden), BF16),
+            quarter,
+            quarter,
+            quarter,
+            quarter,
             shape((slots, hidden), F32),
             shape((slots, hidden), F32),
             shape((slots, width), BF16),
         ),
         [SMEM] + [HBM] * 4,
-        (HBM,) * 5,
+        (HBM,) * 7,
         [
             pltpu.VMEM((2, peers, chunks, CAP * LANE), BF16),
             weights,
@@ -356,16 +332,21 @@
             inner,
             features,
             features,
-            pltpu.SemaphoreType.DMA((9,)),
+            pltpu.SemaphoreType.DMA((7 + chunks,)),
         ],
         62, 3 * product, 14 << 20, "forward",
     )(place, got, wg, wu, gathered[1])
-    swapped = over_core(send)
+    swapped_a = over_core(send_a)
+    swapped_b = over_core(send_b)
+    outward = (keep_a.astype(F32) + swapped_a.astype(F32)).astype(BF16)
+    above = round_z(outward[:2], -1)
+    below = round_z(outward[2], 1)
+    far_below = round_z(outward[3], 3)
 
     part = call(
         backward_kernel,
         shape((peers, chunks, CAP * LANE), BF16),
-        [SMEM] + [HBM] * 9,
+        [SMEM] + [HBM] * 10,
         HBM,
         [
             inner,
@@ -379,9 +360,9 @@
             pltpu.SemaphoreType.DMA((7 + chunks,)),
         ],
         62, 3 * product, 14 << 20, "backward",
-    )(place, gate, up, cot, *gathered, wg, wu)
-
-    down_part = reduce_features(place, keep, swapped)
+    )(place, gate, up, cot, *gathered, wg, wu, above)
+
+    down_part = reduce_features(above, below, far_below, keep_b, swapped_b)
     returned = lax.all_to_all(part, "expert", split_axis=0, concat_axis=0, tiled=True)
 
     token_grad = call(

time: 149 us -> 156 us (1.047)
  waiting for transfers between devices: 12.7 us -> 24.1 us
  Pallas kernels: 29.9 us -> 22.6 us
  other arithmetic: 2.68 us -> 5.65 us
  starting transfers between devices: 96.1 us -> 93.3 us
  local copies, waits for them, and re-layouts: 5.81 us -> 8.2 us
    ppermute x13 -> x12, waiting for transfers between devices: 10.4 us -> 24 us  [round_z(): return lax.ppermute(x, ('z', 'core'), pairs)]
    pallas_call x3 -> x1, Pallas kernels: 14 us -> 7.77 us  [on_device(): call(forward_kernel, (quarter, quarter, quarter, quarter, shape((slots, h...]
    all_to_all x1, starting transfers between devices: 13 us -> 9.75 us  [on_device(): lax.all_to_all(part, 'expert', split_axis=0, concat_axis=0, tiled=True)]
    ppermute x3 -> x4, waiting for transfers between devices: 2.32 us -> 0.01 us  [over_core(): return lax.ppermute(x, 'core', [(0, 1), (1, 0)])]
    ppermute x3 -> x4, starting transfers between devices: 6.29 us -> 8.29 us  [over_core(): return lax.ppermute(x, 'core', [(0, 1), (1, 0)])]
    ppermute x13 -> x12, starting transfers between devices: 59.2 us -> 57.6 us  [round_z(): return lax.ppermute(x, ('z', 'core'), pairs)]
    unnamed x15 -> x25, local copies, waits for them, and re-layouts: 5.1 us -> 5.47 us
  transfers between devices with their start and end apart: 18 -> 18, of which waited for: 3 -> 7; matrix products, arithmetic and copies ran while one was open for 3% -> 8% of each run, Pallas kernels for 17% -> 11%
where the time goes in v5:
time: 156 us; the launch traced here: 155 us
  starting transfers between devices  93.3 us (60%)
  waiting for transfers between devices  24.1 us (15%)
  Pallas kernels  22.6 us (14%)
  local copies, waits for them, and re-layouts  8.2 us (5%)
  other arithmetic  5.65 us (4%)
    ppermute x12, starting transfers between devices, round_z(): return lax.ppermute(x, ('z', 'core'), pairs)  57.6 us
    ppermute x12, waiting for transfers between devices, round_z(): return lax.ppermute(x, ('z', 'core'), pairs)  24 us
    all_to_all x1, starting transfers between devices, on_device(): lax.all_to_all(packed, 'expert', split_axis=0, concat_axis=0, tiled=True)  17.6 us
    all_to_all x1, starting transfers between devices, on_device(): lax.all_to_all(part, 'expert', split_axis=0, concat_axis=0, tiled=True)  9.75 us
    pallas_call x1, Pallas kernels, on_device(): call(backward_kernel, shape((peers, chunks, CAP * LANE), BF16), [SMEM] +...  8.61 us
    ppermute x4, starting transfers between devices, over_core(): return lax.ppermute(x, 'core', [(0, 1), (1, 0)])  8.29 us
    pallas_call x1, Pallas kernels, on_device(): call(forward_kernel, (quarter, quarter, quarter, quarter, shape((slots, h...  7.77 us
    unnamed x25, local copies, waits for them, and re-layouts  5.47 us
  transfers between devices with their start and end apart: 18, of which 7 were waited for; matrix products, arithmetic and copies ran while one was open for 8% of the time, Pallas kernels for 11%

profile of v5, /device:TPU:14, one launch (start us, length us, event | category | flops | bytes accessed | tf_op | source)
XLA Modules:
  0.0 154.8 jit_solution(12861125481545416106)
XLA Ops:
  0.6 4.4 %pack.1 = (bf16[64,16,768]{2,1,0:T(8,128)(2,1)}, bf16[128,768]{1,0:T(8,128)(2,1)}) custom-call(s32[1,128]{1,0:T(1,128)} %bitcast.46, f32[1,128]{1,0:T(1,128)} %bitcast.54, bf16[128,2048]{1,0:T(8,128)(2,1)} %tok_hbm.1, bf16[128,2048]{1,0:T(8,128)(2,1)} %cot_hbm.1, bf16[128,768]{1,0:T(8,128)(2,1)} %bitcast.53), custom_call_target="tpu_custom_call" | custom-call | flops 201326592 | bytes 4194304 | tf_op jit(solution)/shard_map/pack/pallas_call | solution.py:287
  5.0 17.6 %all-to-all-start = ((bf16[64,16,768]{2,1,0:T(8,128)(2,1)}), bf16[64,16,768]{2,1,0:T(8,128)(2,1)S(1)}, u32[]{:S(2)}, u32[]{:S(2)}) async-start(bf16[64,16,768]{2,1,0:T(8,128)(2,1)} %get-tuple-element.11), calls=%async_computation | async-start | bytes 3145728 | tf_op jit(solution)/shard_map/all_to_all | solution.py:302
  22.6 1.9 %collective-permute-start = (bf16[128,768]{1,0:T(8,128)(2,1)S(1)}, bf16[128,768]{1,0:T(8,128)(2,1)S(1)}, u32[]{:S(2)}, u32[]{:S(2)}) collective-permute-start(bf16[128,768]{1,0:T(8,128)(2,1)S(1)} %copy-done.9), channel_id=1, source_target_pairs={{0,2},{1,15},{2,4},{3,1},{4,6},{5,3},{6,8},{7,5},{8,10},{9,7},{10,... | collective-permute-start | bytes 589832 | tf_op jit(solution)/shard_map/ppermute | solution.py:247
  24.6 11.3 %collective-permute-start.1 = (bf16[128,768]{1,0:T(8,128)(2,1)S(1)}, bf16[128,768]{1,0:T(8,128)(2,1)S(1)}, u32[]{:S(2)}, u32[]{:S(2)}) collective-permute-start(bf16[128,768]{1,0:T(8,128)(2,1)S(1)} %copy-done.9), channel_id=1, source_target_pairs={{0,6},{1,11},{2,8},{3,13},{4,10},{5,15},{6,12},{7,1},{8,14},{9,3},... | collective-permute-start | bytes 589832 | tf_op jit(solution)/shard_map/ppermute | solution.py:247
  35.9 4.1 %collective-permute-start.3 = (bf16[128,768]{1,0:T(8,128)(2,1)S(1)}, bf16[128,768]{1,0:T(8,128)(2,1)}, u32[]{:S(2)}, u32[]{:S(2)}) collective-permute-start(bf16[128,768]{1,0:T(8,128)(2,1)S(1)} %copy-done.9), channel_id=1, source_target_pairs={{0,14},{1,3},{2,0},{3,5},{4,2},{5,7},{6,4},{7,9},{8,6},{9,11},{10,... | collective-permute-start | bytes 589832 | tf_op jit(solution)/shard_map/ppermute | solution.py:247
  40.0 5.7 %collective-permute-start.5 = (bf16[128,768]{1,0:T(8,128)(2,1)S(1)}, bf16[128,768]{1,0:T(8,128)(2,1)}, u32[]{:S(2)}, u32[]{:S(2)}) collective-permute-start(bf16[128,768]{1,0:T(8,128)(2,1)S(1)} %copy-done.9), channel_id=1, source_target_pairs={{0,10},{1,7},{2,12},{3,9},{4,14},{5,11},{6,0},{7,13},{8,2},{9,15},... | collective-permute-start | bytes 589832 | tf_op jit(solution)/shard_map/ppermute | solution.py:247
  47.3 11.1 %collective-permute-start.2 = (bf16[256,768]{1,0:T(8,128)(2,1)}, bf16[256,768]{1,0:T(8,128)(2,1)}, u32[]{:S(2)}, u32[]{:S(2)}) collective-permute-start(bf16[256,768]{1,0:T(8,128)(2,1)} %pad_maximum_fusion.1), channel_id=1, source_target_pairs={{0,2},{1,15},{2,4},{3,1},{4,6},{5,3},{6,8},{7,5},{8,10},{9,7},{10,... | collective-permute-start | bytes 1179656 | tf_op jit(solution)/shard_map/ppermute | solution.py:247
  61.0 3.0 %collective-permute-done.2 = bf16[256,768]{1,0:T(8,128)(2,1)} collective-permute-done((bf16[256,768]{1,0:T(8,128)(2,1)}, bf16[256,768]{1,0:T(8,128)(2,1)}, u32[]{:S(2)}, u32[]{:S(2)}) %collective-permute-start.2) | collective-permute-done | bytes 393248 | tf_op jit(solution)/shard_map/ppermute | solution.py:247
  68.9 7.8 %forward.1 = (bf16[4,128,768]{2,1,0:T(8,128)(2,1)}, bf16[4,128,768]{2,1,0:T(8,128)(2,1)}, bf16[4,128,768]{2,1,0:T(8,128)(2,1)}, bf16[4,128,768]{2,1,0:T(8,128)(2...) custom-call(s32[2]{0:T(128)} %pad_add_fusion.place_ref, bf16[64,16,768]{2,1,0:T(8,128)(2,1)} %copy-done.1, ...), custom_call_target="tpu_custom_call" | custom-call | flops 1811939328 | bytes 14680064 | tf_op jit(solution)/shard_map/forward/pallas_call | solution.py:309
  76.7 2.1 %collective-permute-start.8 = (bf16[4,128,768]{2,1,0:T(8,128)(2,1)}, bf16[4,128,768]{2,1,0:T(8,128)(2,1)S(1)}, u32[]{:S(2)}, u32[]{:S(2)}) collective-permute-start(bf16[4,128,768]{2,1,0:T(8,128)(2,1)} %get-tuple-element.17), channel_id=1, source_target_pairs={{0,1},{1,0},{2,3},{3,2},{4,5},{5,4},{6,7},{7,6},{8,9},{9,8},{10,11... | collective-permute-start | bytes 2359304 | tf_op jit(solution)/shard_map/ppermute | solution.py:237
  82.7 2.4 %collective-permute-start.6 = (bf16[5,128,768]{2,1,0:T(8,128)(2,1)}, bf16[5,128,768]{2,1,0:T(8,128)(2,1)S(1)}, u32[]{:S(2)}, u32[]{:S(2)}) collective-permute-start(bf16[5,128,768]{2,1,0:T(8,128)(2,1)} %bitcast_dynamic-update-slice_fusion.first_hbm), channel_id=1, source_target_pairs={{0,1},{1,0},{2,3},{3,2},{4,5},{5,4},{6,7},{7,6},{8,9},{9,8},{10,11... | collective-permute-start | bytes 2949128 | tf_op jit(solution)/shard_map/ppermute | solution.py:237
  85.1 1.9 %collective-permute-start.7 = (bf16[3,128,768]{2,1,0:T(8,128)(2,1)}, bf16[3,128,768]{2,1,0:T(8,128)(2,1)S(1)}, u32[]{:S(2)}, u32[]{:S(2)}) collective-permute-start(bf16[3,128,768]{2,1,0:T(8,128)(2,1)} %pad_maximum_fusion.after_hbm.rest_hbm), channel_id=1, source_target_pairs={{0,1},{1,0},{2,3},{3,2},{4,5},{5,4},{6,7},{7,6},{8,9},{9,8},{10,11... | collective-permute-start | bytes 1769480 | tf_op jit(solution)/shard_map/ppermute | solution.py:237
  87.3 7.9 %collective-permute-start.9 = (bf16[2,128,768]{2,1,0:T(8,128)(2,1)S(1)}, bf16[2,128,768]{2,1,0:T(8,128)(2,1)S(1)}, u32[]{:S(2)}, u32[]{:S(2)}) collective-permute-start(bf16[2,128,768]{2,1,0:T(8,128)(2,1)S(1)} %slice.52), channel_id=1, source_target_pairs={{0,14},{1,3},{2,0},{3,5},{4,2},{5,7},{6,4},{7,9},{8,6},{9,11},{10,... | collective-permute-start | bytes 1179656 | tf_op jit(solution)/shard_map/ppermute | solution.py:247
  95.2 1.9 %collective-permute-start.10 = (bf16[4,128,768]{2,1,0:T(8,128)(2,1)}, bf16[4,128,768]{2,1,0:T(8,128)(2,1)}, u32[]{:S(2)}, u32[]{:S(2)}) collective-permute-start(bf16[4,128,768]{2,1,0:T(8,128)(2,1)} %get-tuple-element.19), channel_id=1, source_target_pairs={{0,1},{1,0},{2,3},{3,2},{4,5},{5,4},{6,7},{7,6},{8,9},{9,8},{10,11... | collective-permute-start | bytes 2359304 | tf_op jit(solution)/shard_map/ppermute | solution.py:237
  97.2 3.3 %collective-permute-done.9.after_hbm = bf16[2,128,768]{2,1,0:T(8,128)(2,1)S(1)} collective-permute-done((bf16[2,128,768]{2,1,0:T(8,128)(2,1)S(1)}, bf16[2,128,768]{2,1,0:T(8,128)(2,1)S(1)}, u32[]{:S(2)}, u32[]{:S(2)}) %collective-permute-start.9) | collective-permute-done | bytes 393248 | tf_op jit(solution)/shard_map/ppermute | solution.py:247
  101.3 8.6 %backward.1 = bf16[64,16,384]{2,1,0:T(8,128)(2,1)} custom-call(s32[2]{0:T(128)} %pad_add_fusion.place_ref, f32[192,768]{1,0:T(8,128)} %get-tuple-element.13.gate_hbm, f32[192,768]{1,0:T(8,128)} %get-tuple-element.14.up_hbm, bf16[192,2048]{1,0:T(8,128)(2,1)} %get-tuple-element.15.cot_hbm, bf16[5,128,768]{2,1,0:T(8,128)(2,1)} %bitcast_dynamic-update-slice_fusion.first_hbm, ...), custom_call_target="tpu_custom_call" | custom-call | flops 1811939328 | bytes 14680064 | tf_op jit(solution)/shard_map/backward/pallas_call | solution.py:346
  109.9 9.8 %all-to-all-start.1 = ((bf16[64,16,384]{2,1,0:T(8,128)(2,1)}), bf16[64,16,384]{2,1,0:T(8,128)(2,1)S(1)}, u32[]{:S(2)}, u32[]{:S(2)}) async-start(bf16[64,16,384]{2,1,0:T(8,128)(2,1)} %backward.1), calls=%async_computation.1 | async-start | bytes 1572864 | tf_op jit(solution)/shard_map/all_to_all | solution.py:366
  119.7 2.2 %collective-permute-start.13 = (bf16[128,768]{1,0:T(8,128)(2,1)S(1)}, bf16[128,768]{1,0:T(8,128)(2,1)S(1)}, u32[]{:S(2)}, u32[]{:S(2)}) collective-permute-start(bf16[128,768]{1,0:T(8,128)(2,1)S(1)} %get-tuple-element.24), channel_id=1, source_target_pairs={{0,2},{1,15},{2,4},{3,1},{4,6},{5,3},{6,8},{7,5},{8,10},{9,7},{10,... | collective-permute-start | bytes 589832 | tf_op jit(solution)/shard_map/ppermute | solution.py:247
  121.9 2.4 %collective-permute-start.15 = (bf16[128,768]{1,0:T(8,128)(2,1)S(1)}, bf16[128,768]{1,0:T(8,128)(2,1)S(1)}, u32[]{:S(2)}, u32[]{:S(2)}) collective-permute-start(bf16[128,768]{1,0:T(8,128)(2,1)S(1)} %get-tuple-element.25), channel_id=1, source_target_pairs={{0,6},{1,11},{2,8},{3,13},{4,10},{5,15},{6,12},{7,1},{8,14},{9,3},... | collective-permute-start | bytes 589832 | tf_op jit(solution)/shard_map/ppermute | solution.py:247
  124.3 4.6 %collective-permute-done.13 = bf16[128,768]{1,0:T(8,128)(2,1)S(1)} collective-permute-done((bf16[128,768]{1,0:T(8,128)(2,1)S(1)}, bf16[128,768]{1,0:T(8,128)(2,1)S(1)}, u32[]{:S(2)}, u32[]{:S(2)}) %collective-permute-start.13) | collective-permute-done | bytes 196640 | tf_op jit(solution)/shard_map/ppermute | solution.py:247
  129.9 1.9 %collective-permute-start.14 = (bf16[128,768]{1,0:T(8,128)(2,1)S(1)}, bf16[128,768]{1,0:T(8,128)(2,1)S(1)}, u32[]{:S(2)}, u32[]{:S(2)}) collective-permute-start(bf16[128,768]{1,0:T(8,128)(2,1)S(1)} %fusion), channel_id=1, source_target_pairs={{0,2},{1,15},{2,4},{3,1},{4,6},{5,3},{6,8},{7,5},{8,10},{9,7},{10,... | collective-permute-start | bytes 589832 | tf_op jit(solution)/shard_map/ppermute | solution.py:247
  133.1 5.1 %collective-permute-start.11 = (bf16[128,768]{1,0:T(8,128)(2,1)S(1)}, bf16[128,768]{1,0:T(8,128)(2,1)S(1)}, u32[]{:S(2)}, u32[]{:S(2)}) collective-permute-start(bf16[128,768]{1,0:T(8,128)(2,1)S(1)} %get-tuple-element.22), channel_id=1, source_target_pairs={{0,14},{1,3},{2,0},{3,5},{4,2},{5,7},{6,4},{7,9},{8,6},{9,11},{10,... | collective-permute-start | bytes 589832 | tf_op jit(solution)/shard_map/ppermute | solution.py:247
  138.2 1.9 %collective-permute-start.12 = (bf16[128,768]{1,0:T(8,128)(2,1)S(1)}, bf16[128,768]{1,0:T(8,128)(2,1)S(1)}, u32[]{:S(2)}, u32[]{:S(2)}) collective-permute-start(bf16[128,768]{1,0:T(8,128)(2,1)S(1)} %get-tuple-element.23), channel_id=1, source_target_pairs={{0,10},{1,7},{2,12},{3,9},{4,14},{5,11},{6,0},{7,13},{8,2},{9,15},... | collective-permute-start | bytes 589832 | tf_op jit(solution)/shard_map/ppermute | solution.py:247
  141.4 9.3 %collective-permute-done.12 = bf16[128,768]{1,0:T(8,128)(2,1)S(1)} collective-permute-done((bf16[128,768]{1,0:T(8,128)(2,1)S(1)}, bf16[128,768]{1,0:T(8,128)(2,1)S(1)}, u32[]{:S(2)}, u32[]{:S(2)}) %collective-permute-start.12) | collective-permute-done | bytes 196640 | tf_op jit(solution)/shard_map/ppermute | solution.py:247
  (52 shorter events, 21.4 us)
Async XLA Ops:
  5.0 17.6 %copy-start.9 = (bf16[128,768]{1,0:T(8,128)(2,1)S(1)}, bf16[128,768]{1,0:T(8,128)(2,1)}, u32[]{:S(2)}) copy-start(bf16[128,768]{1,0:T(8,128)(2,1)} %get-tuple-element.12) | copy-start | bytes 589828
  5.0 62.7 %all-to-all-start = ((bf16[64,16,768]{2,1,0:T(8,128)(2,1)}), bf16[64,16,768]{2,1,0:T(8,128)(2,1)S(1)}, u32[]{:S(2)}, u32[]{:S(2)}) async-start(bf16[64,16,768]{2,1,0:T(8,128)(2,1)} %get-tuple-element.11), calls=%async_computation | async-start | bytes 3145728 | tf_op jit(solution)/shard_map/all_to_all | solution.py:302
  22.6 23.1 %collective-permute-start = (bf16[128,768]{1,0:T(8,128)(2,1)S(1)}, bf16[128,768]{1,0:T(8,128)(2,1)S(1)}, u32[]{:S(2)}, u32[]{:S(2)}) collective-permute-start(bf16[128,768]{1,0:T(8,128)(2,1)S(1)} %copy-done.9), channel_id=1, source_target_pairs={{0,2},{1,15},{2,4},{3,1},{4,6},{5,3},{6,8},{7,5},{8,10},{9,7},{10,... | collective-permute-start | bytes 589832 | tf_op jit(solution)/shard_map/ppermute | solution.py:247
  24.6 22.0 %collective-permute-start.1 = (bf16[128,768]{1,0:T(8,128)(2,1)S(1)}, bf16[128,768]{1,0:T(8,128)(2,1)S(1)}, u32[]{:S(2)}, u32[]{:S(2)}) collective-permute-start(bf16[128,768]{1,0:T(8,128)(2,1)S(1)} %copy-done.9), channel_id=1, source_target_pairs={{0,6},{1,11},{2,8},{3,13},{4,10},{5,15},{6,12},{7,1},{8,14},{9,3},... | collective-permute-start | bytes 589832 | tf_op jit(solution)/shard_map/ppermute | solution.py:247
  35.9 23.2 %collective-permute-start.3 = (bf16[128,768]{1,0:T(8,128)(2,1)S(1)}, bf16[128,768]{1,0:T(8,128)(2,1)}, u32[]{:S(2)}, u32[]{:S(2)}) collective-permute-start(bf16[128,768]{1,0:T(8,128)(2,1)S(1)} %copy-done.9), channel_id=1, source_target_pairs={{0,14},{1,3},{2,0},{3,5},{4,2},{5,7},{6,4},{7,9},{8,6},{9,11},{10,... | collective-permute-start | bytes 589832 | tf_op jit(solution)/shard_map/ppermute | solution.py:247
  40.0 41.1 %collective-permute-start.5 = (bf16[128,768]{1,0:T(8,128)(2,1)S(1)}, bf16[128,768]{1,0:T(8,128)(2,1)}, u32[]{:S(2)}, u32[]{:S(2)}) collective-permute-start(bf16[128,768]{1,0:T(8,128)(2,1)S(1)} %copy-done.9), channel_id=1, source_target_pairs={{0,10},{1,7},{2,12},{3,9},{4,14},{5,11},{6,0},{7,13},{8,2},{9,15},... | collective-permute-start | bytes 589832 | tf_op jit(solution)/shard_map/ppermute | solution.py:247
  47.3 16.7 %collective-permute-start.2 = (bf16[256,768]{1,0:T(8,128)(2,1)}, bf16[256,768]{1,0:T(8,128)(2,1)}, u32[]{:S(2)}, u32[]{:S(2)}) collective-permute-start(bf16[256,768]{1,0:T(8,128)(2,1)} %pad_maximum_fusion.1), channel_id=1, source_target_pairs={{0,2},{1,15},{2,4},{3,1},{4,6},{5,3},{6,8},{7,5},{8,10},{9,7},{10,... | collective-permute-start | bytes 1179656 | tf_op jit(solution)/shard_map/ppermute | solution.py:247
  59.1 7.8 %collective-permute-start.4 = (bf16[128,768]{1,0:T(8,128)(2,1)}, bf16[128,768]{1,0:T(8,128)(2,1)S(1)}, u32[]{:S(2)}, u32[]{:S(2)}) collective-permute-start(bf16[128,768]{1,0:T(8,128)(2,1)} %collective-permute-done.3), channel_id=1, source_target_pairs={{0,14},{1,3},{2,0},{3,5},{4,2},{5,7},{6,4},{7,9},{8,6},{9,11},{10,... | collective-permute-start | bytes 589832 | tf_op jit(solution)/shard_map/ppermute | solution.py:247
  61.0 6.7 %copy-start.4 = (bf16[5,128,768]{2,1,0:T(8,128)(2,1)}, bf16[5,128,768]{2,1,0:T(8,128)(2,1)S(1)}, u32[]{:S(2)}) copy-start(bf16[5,128,768]{2,1,0:T(8,128)(2,1)S(1)} %bitcast_dynamic-update-slice_fusion.3) | copy-start | bytes 2949124
  76.7 10.4 %copy-start.7 = (bf16[4,128,768]{2,1,0:T(8,128)(2,1)S(1)}, bf16[4,128,768]{2,1,0:T(8,128)(2,1)}, u32[]{:S(2)}) copy-start(bf16[4,128,768]{2,1,0:T(8,128)(2,1)} %get-tuple-element.16) | copy-start | bytes 2359300
  76.7 10.3 %collective-permute-start.8 = (bf16[4,128,768]{2,1,0:T(8,128)(2,1)}, bf16[4,128,768]{2,1,0:T(8,128)(2,1)S(1)}, u32[]{:S(2)}, u32[]{:S(2)}) collective-permute-start(bf16[4,128,768]{2,1,0:T(8,128)(2,1)} %get-tuple-element.17), channel_id=1, source_target_pairs={{0,1},{1,0},{2,3},{3,2},{4,5},{5,4},{6,7},{7,6},{8,9},{9,8},{10,11... | collective-permute-start | bytes 2359304 | tf_op jit(solution)/shard_map/ppermute | solution.py:237
  82.7 14.5 %collective-permute-start.6 = (bf16[5,128,768]{2,1,0:T(8,128)(2,1)}, bf16[5,128,768]{2,1,0:T(8,128)(2,1)S(1)}, u32[]{:S(2)}, u32[]{:S(2)}) collective-permute-start(bf16[5,128,768]{2,1,0:T(8,128)(2,1)} %bitcast_dynamic-update-slice_fusion.first_hbm), channel_id=1, source_target_pairs={{0,1},{1,0},{2,3},{3,2},{4,5},{5,4},{6,7},{7,6},{8,9},{9,8},{10,11... | collective-permute-start | bytes 2949128 | tf_op jit(solution)/shard_map/ppermute | solution.py:237
  85.1 12.0 %collective-permute-start.7 = (bf16[3,128,768]{2,1,0:T(8,128)(2,1)}, bf16[3,128,768]{2,1,0:T(8,128)(2,1)S(1)}, u32[]{:S(2)}, u32[]{:S(2)}) collective-permute-start(bf16[3,128,768]{2,1,0:T(8,128)(2,1)} %pad_maximum_fusion.after_hbm.rest_hbm), channel_id=1, source_target_pairs={{0,1},{1,0},{2,3},{3,2},{4,5},{5,4},{6,7},{7,6},{8,9},{9,8},{10,11... | collective-permute-start | bytes 1769480 | tf_op jit(solution)/shard_map/ppermute | solution.py:237
  87.3 13.2 %collective-permute-start.9 = (bf16[2,128,768]{2,1,0:T(8,128)(2,1)S(1)}, bf16[2,128,768]{2,1,0:T(8,128)(2,1)S(1)}, u32[]{:S(2)}, u32[]{:S(2)}) collective-permute-start(bf16[2,128,768]{2,1,0:T(8,128)(2,1)S(1)} %slice.52), channel_id=1, source_target_pairs={{0,14},{1,3},{2,0},{3,5},{4,2},{5,7},{6,4},{7,9},{8,6},{9,11},{10,... | collective-permute-start | bytes 1179656 | tf_op jit(solution)/shard_map/ppermute | solution.py:247
  95.2 29.1 %collective-permute-start.10 = (bf16[4,128,768]{2,1,0:T(8,128)(2,1)}, bf16[4,128,768]{2,1,0:T(8,128)(2,1)}, u32[]{:S(2)}, u32[]{:S(2)}) collective-permute-start(bf16[4,128,768]{2,1,0:T(8,128)(2,1)} %get-tuple-element.19), channel_id=1, source_target_pairs={{0,1},{1,0},{2,3},{3,2},{4,5},{5,4},{6,7},{7,6},{8,9},{9,8},{10,11... | collective-permute-start | bytes 2359304 | tf_op jit(solution)/shard_map/ppermute | solution.py:237
  109.9 19.1 %copy-start.6 = (bf16[4,128,768]{2,1,0:T(8,128)(2,1)S(1)}, bf16[4,128,768]{2,1,0:T(8,128)(2,1)}, u32[]{:S(2)}) copy-start(bf16[4,128,768]{2,1,0:T(8,128)(2,1)} %get-tuple-element.18) | copy-start | bytes 2359300
  109.9 22.0 %copy-start.3 = (bf16[2,128,768]{2,1,0:T(8,128)(2,1)S(1)}, bf16[2,128,768]{2,1,0:T(8,128)(2,1)}, u32[]{:S(2)}) copy-start(bf16[2,128,768]{2,1,0:T(8,128)(2,1)} %copy-done.2) | copy-start | bytes 1179652
  109.9 43.0 %all-to-all-start.1 = ((bf16[64,16,384]{2,1,0:T(8,128)(2,1)}), bf16[64,16,384]{2,1,0:T(8,128)(2,1)S(1)}, u32[]{:S(2)}, u32[]{:S(2)}) async-start(bf16[64,16,384]{2,1,0:T(8,128)(2,1)} %backward.1), calls=%async_computation.1 | async-start | bytes 1572864 | tf_op jit(solution)/shard_map/all_to_all | solution.py:366
  119.7 9.2 %collective-permute-start.13 = (bf16[128,768]{1,0:T(8,128)(2,1)S(1)}, bf16[128,768]{1,0:T(8,128)(2,1)S(1)}, u32[]{:S(2)}, u32[]{:S(2)}) collective-permute-start(bf16[128,768]{1,0:T(8,128)(2,1)S(1)} %get-tuple-element.24), channel_id=1, source_target_pairs={{0,2},{1,15},{2,4},{3,1},{4,6},{5,3},{6,8},{7,5},{8,10},{9,7},{10,... | collective-permute-start | bytes 589832 | tf_op jit(solution)/shard_map/ppermute | solution.py:247
  121.9 18.2 %collective-permute-start.15 = (bf16[128,768]{1,0:T(8,128)(2,1)S(1)}, bf16[128,768]{1,0:T(8,128)(2,1)S(1)}, u32[]{:S(2)}, u32[]{:S(2)}) collective-permute-start(bf16[128,768]{1,0:T(8,128)(2,1)S(1)} %get-tuple-element.25), channel_id=1, source_target_pairs={{0,6},{1,11},{2,8},{3,13},{4,10},{5,15},{6,12},{7,1},{8,14},{9,3},... | collective-permute-start | bytes 589832 | tf_op jit(solution)/shard_map/ppermute | solution.py:247
  129.9 10.2 %collective-permute-start.14 = (bf16[128,768]{1,0:T(8,128)(2,1)S(1)}, bf16[128,768]{1,0:T(8,128)(2,1)S(1)}, u32[]{:S(2)}, u32[]{:S(2)}) collective-permute-start(bf16[128,768]{1,0:T(8,128)(2,1)S(1)} %fusion), channel_id=1, source_target_pairs={{0,2},{1,15},{2,4},{3,1},{4,6},{5,3},{6,8},{7,5},{8,10},{9,7},{10,... | collective-permute-start | bytes 589832 | tf_op jit(solution)/shard_map/ppermute | solution.py:247
  133.1 19.8 %copy-start = (s32[128,1]{0,1:T(1,128)S(1)}, s32[128,1]{0,1:T(1,128)}, u32[]{:S(2)}) copy-start(s32[128,1]{0,1:T(1,128)} %param.9) | copy-start | bytes 1540
  133.1 8.3 %collective-permute-start.11 = (bf16[128,768]{1,0:T(8,128)(2,1)S(1)}, bf16[128,768]{1,0:T(8,128)(2,1)S(1)}, u32[]{:S(2)}, u32[]{:S(2)}) collective-permute-start(bf16[128,768]{1,0:T(8,128)(2,1)S(1)} %get-tuple-element.22), channel_id=1, source_target_pairs={{0,14},{1,3},{2,0},{3,5},{4,2},{5,7},{6,4},{7,9},{8,6},{9,11},{10,... | collective-permute-start | bytes 589832 | tf_op jit(solution)/shard_map/ppermute | solution.py:247
  138.2 12.5 %collective-permute-start.12 = (bf16[128,768]{1,0:T(8,128)(2,1)S(1)}, bf16[128,768]{1,0:T(8,128)(2,1)S(1)}, u32[]{:S(2)}, u32[]{:S(2)}) collective-permute-start(bf16[128,768]{1,0:T(8,128)(2,1)S(1)} %get-tuple-element.23), channel_id=1, source_target_pairs={{0,10},{1,7},{2,12},{3,9},{4,14},{5,11},{6,0},{7,13},{8,2},{9,15},... | collective-permute-start | bytes 589832 | tf_op jit(solution)/shard_map/ppermute | solution.py:247
  (4 other events, 8.6 us)

commit v6 on v5

--- a/solution.py
+++ b/solution.py
@@ -162,7 +162,7 @@
 
 def backward_kernel(
     place_ref, gate_hbm, up_hbm, cot_hbm,
-    first_hbm, rest_hbm, first_other_hbm, rest_other_hbm, wg_hbm, wu_hbm, after_hbm,
+    first_hbm, rest_hbm, first_other_hbm, rest_other_hbm, wg_hbm, wu_hbm,
     part_hbm,
     gate, up, cot, down, wg, wu, scr, part, sems,
 ):
@@ -346,7 +346,7 @@
     part = call(
         backward_kernel,
         shape((peers, chunks, CAP * LANE), BF16),
-        [SMEM] + [HBM] * 10,
+        [SMEM] + [HBM] * 9,
         HBM,
         [
             inner,
@@ -360,7 +360,7 @@
             pltpu.SemaphoreType.DMA((7 + chunks,)),
         ],
         62, 3 * product, 14 << 20, "backward",
-    )(place, gate, up, cot, *gathered, wg, wu, above)
+    )(place, gate, up, cot, *gathered, wg, wu)
 
     down_part = reduce_features(above, below, far_below, keep_b, swapped_b)
     returned = lax.all_to_all(part, "expert", split_axis=0, concat_axis=0, tiled=True)

time: 156 us -> 152 us (0.974)
  other arithmetic: 5.65 us -> 3.33 us
    all_to_all x1, starting transfers between devices: 9.75 us -> 12.8 us  [on_device(): lax.all_to_all(part, 'expert', split_axis=0, concat_axis=0, tiled=True)]
    ppermute x12, starting transfers between devices: 57.6 us -> 55.2 us  [round_z(): return lax.ppermute(x, ('z', 'core'), pairs)]
    unnamed x25 -> x17, local copies, waits for them, and re-layouts: 5.47 us -> 5.95 us
  transfers between devices with their start and end apart: 18 -> 18, of which waited for: 7 -> 5; matrix products, arithmetic and copies ran while one was open for 8% -> 5% of each run, Pallas kernels for 11% -> 11%
where the time goes in v6:
time: 152 us; the launch traced here: 151 us
  starting transfers between devices  94.4 us (62%)
  waiting for transfers between devices  22.9 us (15%)
  Pallas kernels  22.7 us (15%)
  local copies, waits for them, and re-layouts  6.72 us (4%)
  other arithmetic  3.33 us (2%)
    ppermute x12, starting transfers between devices, round_z(): return lax.ppermute(x, ('z', 'core'), pairs)  55.2 us
    ppermute x12, waiting for transfers between devices, round_z(): return lax.ppermute(x, ('z', 'core'), pairs)  22.8 us
    all_to_all x1, starting transfers between devices, on_device(): lax.all_to_all(packed, 'expert', split_axis=0, concat_axis=0, tiled=True)  17.6 us
    all_to_all x1, starting transfers between devices, on_device(): lax.all_to_all(part, 'expert', split_axis=0, concat_axis=0, tiled=True)  12.8 us
    ppermute x4, starting transfers between devices, over_core(): return lax.ppermute(x, 'core', [(0, 1), (1, 0)])  8.71 us
    pallas_call x1, Pallas kernels, on_device(): call(backward_kernel, shape((peers, chunks, CAP * LANE), BF16), [SMEM] +...  8.66 us
    pallas_call x1, Pallas kernels, on_device(): call(forward_kernel, (quarter, quarter, quarter, quarter, shape((slots, h...  7.79 us
    unnamed x17, local copies, waits for them, and re-layouts  5.95 us
  transfers between devices with their start and end apart: 18, of which 5 were waited for; matrix products, arithmetic and copies ran while one was open for 5% of the time, Pallas kernels for 11%

profile of v6, /device:TPU:14, one launch (start us, length us, event | category | flops | bytes accessed | tf_op | source)
XLA Modules:
  0.0 151.0 jit_solution(18055857325619638628)
XLA Ops:
  0.6 4.4 %pack.1 = (bf16[64,16,768]{2,1,0:T(8,128)(2,1)}, bf16[128,768]{1,0:T(8,128)(2,1)}) custom-call(s32[1,128]{1,0:T(1,128)} %bitcast.46, f32[1,128]{1,0:T(1,128)} %bitcast.54, bf16[128,2048]{1,0:T(8,128)(2,1)} %tok_hbm.1, bf16[128,2048]{1,0:T(8,128)(2,1)} %cot_hbm.1, bf16[128,768]{1,0:T(8,128)(2,1)} %bitcast.53), custom_call_target="tpu_custom_call" | custom-call | flops 201326592 | bytes 4194304 | tf_op jit(solution)/shard_map/pack/pallas_call | solution.py:287
  5.1 17.6 %all-to-all-start = ((bf16[64,16,768]{2,1,0:T(8,128)(2,1)}), bf16[64,16,768]{2,1,0:T(8,128)(2,1)S(1)}, u32[]{:S(2)}, u32[]{:S(2)}) async-start(bf16[64,16,768]{2,1,0:T(8,128)(2,1)} %get-tuple-element.11), calls=%async_computation | async-start | bytes 3145728 | tf_op jit(solution)/shard_map/all_to_all | solution.py:302
  22.7 1.9 %collective-permute-start = (bf16[128,768]{1,0:T(8,128)(2,1)S(1)}, bf16[128,768]{1,0:T(8,128)(2,1)S(1)}, u32[]{:S(2)}, u32[]{:S(2)}) collective-permute-start(bf16[128,768]{1,0:T(8,128)(2,1)S(1)} %copy-done.5), channel_id=1, source_target_pairs={{0,2},{1,15},{2,4},{3,1},{4,6},{5,3},{6,8},{7,5},{8,10},{9,7},{10,... | collective-permute-start | bytes 589832 | tf_op jit(solution)/shard_map/ppermute | solution.py:247
  24.6 11.3 %collective-permute-start.1 = (bf16[128,768]{1,0:T(8,128)(2,1)S(1)}, bf16[128,768]{1,0:T(8,128)(2,1)S(1)}, u32[]{:S(2)}, u32[]{:S(2)}) collective-permute-start(bf16[128,768]{1,0:T(8,128)(2,1)S(1)} %copy-done.5), channel_id=1, source_target_pairs={{0,6},{1,11},{2,8},{3,13},{4,10},{5,15},{6,12},{7,1},{8,14},{9,3},... | collective-permute-start | bytes 589832 | tf_op jit(solution)/shard_map/ppermute | solution.py:247
  35.9 4.1 %collective-permute-start.3 = (bf16[128,768]{1,0:T(8,128)(2,1)S(1)}, bf16[128,768]{1,0:T(8,128)(2,1)S(1)}, u32[]{:S(2)}, u32[]{:S(2)}) collective-permute-start(bf16[128,768]{1,0:T(8,128)(2,1)S(1)} %copy-done.5), channel_id=1, source_target_pairs={{0,14},{1,3},{2,0},{3,5},{4,2},{5,7},{6,4},{7,9},{8,6},{9,11},{10,... | collective-permute-start | bytes 589832 | tf_op jit(solution)/shard_map/ppermute | solution.py:247
  40.1 5.7 %collective-permute-start.5 = (bf16[128,768]{1,0:T(8,128)(2,1)S(1)}, bf16[128,768]{1,0:T(8,128)(2,1)S(1)}, u32[]{:S(2)}, u32[]{:S(2)}) collective-permute-start(bf16[128,768]{1,0:T(8,128)(2,1)S(1)} %copy-done.5), channel_id=1, source_target_pairs={{0,10},{1,7},{2,12},{3,9},{4,14},{5,11},{6,0},{7,13},{8,2},{9,15},... | collective-permute-start | bytes 589832 | tf_op jit(solution)/shard_map/ppermute | solution.py:247
  47.1 10.7 %collective-permute-start.2 = (bf16[256,768]{1,0:T(8,128)(2,1)S(1)}, bf16[256,768]{1,0:T(8,128)(2,1)S(1)}, u32[]{:S(2)}, u32[]{:S(2)}) collective-permute-start(bf16[256,768]{1,0:T(8,128)(2,1)S(1)} %pad_maximum_fusion.1), channel_id=1, source_target_pairs={{0,2},{1,15},{2,4},{3,1},{4,6},{5,3},{6,8},{7,5},{8,10},{9,7},{10,... | collective-permute-start | bytes 1179656 | tf_op jit(solution)/shard_map/ppermute | solution.py:247
  62.5 1.9 %collective-permute-start.4 = (bf16[128,768]{1,0:T(8,128)(2,1)S(1)}, bf16[128,768]{1,0:T(8,128)(2,1)S(1)}, u32[]{:S(2)}, u32[]{:S(2)}) collective-permute-start(bf16[128,768]{1,0:T(8,128)(2,1)S(1)} %collective-permute-done.3), channel_id=1, source_target_pairs={{0,14},{1,3},{2,0},{3,5},{4,2},{5,7},{6,4},{7,9},{8,6},{9,11},{10,... | collective-permute-start | bytes 589832 | tf_op jit(solution)/shard_map/ppermute | solution.py:247
  64.5 5.6 %collective-permute-done.4 = bf16[128,768]{1,0:T(8,128)(2,1)S(1)} collective-permute-done((bf16[128,768]{1,0:T(8,128)(2,1)S(1)}, bf16[128,768]{1,0:T(8,128)(2,1)S(1)}, u32[]{:S(2)}, u32[]{:S(2)}) %collective-permute-start.4) | collective-permute-done | bytes 196640 | tf_op jit(solution)/shard_map/ppermute | solution.py:247
  72.2 7.8 %forward.1 = (bf16[4,128,768]{2,1,0:T(8,128)(2,1)}, bf16[4,128,768]{2,1,0:T(8,128)(2,1)}, bf16[4,128,768]{2,1,0:T(8,128)(2,1)}, bf16[4,128,768]{2,1,0:T(8,128)(2...) custom-call(s32[2]{0:T(128)} %pad_add_fusion.place_ref, bf16[64,16,768]{2,1,0:T(8,128)(2,1)} %copy-done.1, ...), custom_call_target="tpu_custom_call" | custom-call | flops 1811939328 | bytes 14680064 | tf_op jit(solution)/shard_map/forward/pallas_call | solution.py:309
  80.0 2.5 %collective-permute-start.9 = (bf16[4,128,768]{2,1,0:T(8,128)(2,1)}, bf16[4,128,768]{2,1,0:T(8,128)(2,1)}, u32[]{:S(2)}, u32[]{:S(2)}) collective-permute-start(bf16[4,128,768]{2,1,0:T(8,128)(2,1)} %get-tuple-element.19), channel_id=1, source_target_pairs={{0,1},{1,0},{2,3},{3,2},{4,5},{5,4},{6,7},{7,6},{8,9},{9,8},{10,11... | collective-permute-start | bytes 2359304 | tf_op jit(solution)/shard_map/ppermute | solution.py:237
  82.5 1.9 %collective-permute-start.7 = (bf16[3,128,768]{2,1,0:T(8,128)(2,1)}, bf16[3,128,768]{2,1,0:T(8,128)(2,1)S(1)}, u32[]{:S(2)}, u32[]{:S(2)}) collective-permute-start(bf16[3,128,768]{2,1,0:T(8,128)(2,1)} %pad_maximum_fusion.after_hbm.rest_hbm), channel_id=1, source_target_pairs={{0,1},{1,0},{2,3},{3,2},{4,5},{5,4},{6,7},{7,6},{8,9},{9,8},{10,11... | collective-permute-start | bytes 1769480 | tf_op jit(solution)/shard_map/ppermute | solution.py:237
  84.4 2.4 %collective-permute-start.8 = (bf16[4,128,768]{2,1,0:T(8,128)(2,1)}, bf16[4,128,768]{2,1,0:T(8,128)(2,1)S(1)}, u32[]{:S(2)}, u32[]{:S(2)}) collective-permute-start(bf16[4,128,768]{2,1,0:T(8,128)(2,1)} %get-tuple-element.17), channel_id=1, source_target_pairs={{0,1},{1,0},{2,3},{3,2},{4,5},{5,4},{6,7},{7,6},{8,9},{9,8},{10,11... | collective-permute-start | bytes 2359304 | tf_op jit(solution)/shard_map/ppermute | solution.py:237
  87.7 8.7 %backward.1 = bf16[64,16,384]{2,1,0:T(8,128)(2,1)} custom-call(s32[2]{0:T(128)} %pad_add_fusion.place_ref, f32[192,768]{1,0:T(8,128)} %get-tuple-element.13.gate_hbm, f32[192,768]{1,0:T(8,128)} %get-tuple-element.14.up_hbm, bf16[192,2048]{1,0:T(8,128)(2,1)} %get-tuple-element.15.cot_hbm, bf16[5,128,768]{2,1,0:T(8,128)(2,1)} %bitcast_dynamic-update-slice_fusion.first_hbm, ...), custom_call_target="tpu_custom_call" | custom-call | flops 1811939328 | bytes 14680064 | tf_op jit(solution)/shard_map/backward/pallas_call | solution.py:346
  96.4 12.8 %all-to-all-start.1 = ((bf16[64,16,384]{2,1,0:T(8,128)(2,1)}), bf16[64,16,384]{2,1,0:T(8,128)(2,1)S(1)}, u32[]{:S(2)}, u32[]{:S(2)}) async-start(bf16[64,16,384]{2,1,0:T(8,128)(2,1)} %backward.1), calls=%async_computation.1 | async-start | bytes 1572864 | tf_op jit(solution)/shard_map/all_to_all | solution.py:366
  110.7 1.9 %collective-permute-start.13 = (bf16[128,768]{1,0:T(8,128)(2,1)S(1)}, bf16[128,768]{1,0:T(8,128)(2,1)S(1)}, u32[]{:S(2)}, u32[]{:S(2)}) collective-permute-start(bf16[128,768]{1,0:T(8,128)(2,1)S(1)} %get-tuple-element.24), channel_id=1, source_target_pairs={{0,2},{1,15},{2,4},{3,1},{4,6},{5,3},{6,8},{7,5},{8,10},{9,7},{10,... | collective-permute-start | bytes 589832 | tf_op jit(solution)/shard_map/ppermute | solution.py:247
  112.6 5.1 %collective-permute-start.10 = (bf16[2,128,768]{2,1,0:T(8,128)(2,1)S(1)}, bf16[2,128,768]{2,1,0:T(8,128)(2,1)S(1)}, u32[]{:S(2)}, u32[]{:S(2)}) collective-permute-start(bf16[2,128,768]{2,1,0:T(8,128)(2,1)S(1)} %slice.54), channel_id=1, source_target_pairs={{0,14},{1,3},{2,0},{3,5},{4,2},{5,7},{6,4},{7,9},{8,6},{9,11},{10,... | collective-permute-start | bytes 1179656 | tf_op jit(solution)/shard_map/ppermute | solution.py:247
  117.8 1.9 %collective-permute-start.15 = (bf16[128,768]{1,0:T(8,128)(2,1)S(1)}, bf16[128,768]{1,0:T(8,128)(2,1)S(1)}, u32[]{:S(2)}, u32[]{:S(2)}) collective-permute-start(bf16[128,768]{1,0:T(8,128)(2,1)S(1)} %get-tuple-element.25), channel_id=1, source_target_pairs={{0,6},{1,11},{2,8},{3,13},{4,10},{5,15},{6,12},{7,1},{8,14},{9,3},... | collective-permute-start | bytes 589832 | tf_op jit(solution)/shard_map/ppermute | solution.py:247
  120.3 3.1 %collective-permute-start.14 = (bf16[128,768]{1,0:T(8,128)(2,1)S(1)}, bf16[128,768]{1,0:T(8,128)(2,1)S(1)}, u32[]{:S(2)}, u32[]{:S(2)}) collective-permute-start(bf16[128,768]{1,0:T(8,128)(2,1)S(1)} %fusion), channel_id=1, source_target_pairs={{0,2},{1,15},{2,4},{3,1},{4,6},{5,3},{6,8},{7,5},{8,10},{9,7},{10,... | collective-permute-start | bytes 589832 | tf_op jit(solution)/shard_map/ppermute | solution.py:247
  123.4 7.7 %collective-permute-done.10 = bf16[2,128,768]{2,1,0:T(8,128)(2,1)S(1)} collective-permute-done((bf16[2,128,768]{2,1,0:T(8,128)(2,1)S(1)}, bf16[2,128,768]{2,1,0:T(8,128)(2,1)S(1)}, u32[]{:S(2)}, u32[]{:S(2)}) %collective-permute-start.10) | collective-permute-done | bytes 393248 | tf_op jit(solution)/shard_map/ppermute | solution.py:247
  131.3 5.6 %collective-permute-start.11 = (bf16[128,768]{1,0:T(8,128)(2,1)S(1)}, bf16[128,768]{1,0:T(8,128)(2,1)S(1)}, u32[]{:S(2)}, u32[]{:S(2)}) collective-permute-start(bf16[128,768]{1,0:T(8,128)(2,1)S(1)} %get-tuple-element.22), channel_id=1, source_target_pairs={{0,14},{1,3},{2,0},{3,5},{4,2},{5,7},{6,4},{7,9},{8,6},{9,11},{10,... | collective-permute-start | bytes 589832 | tf_op jit(solution)/shard_map/ppermute | solution.py:247
  136.9 1.9 %collective-permute-start.12 = (bf16[128,768]{1,0:T(8,128)(2,1)S(1)}, bf16[128,768]{1,0:T(8,128)(2,1)S(1)}, u32[]{:S(2)}, u32[]{:S(2)}) collective-permute-start(bf16[128,768]{1,0:T(8,128)(2,1)S(1)} %get-tuple-element.23), channel_id=1, source_target_pairs={{0,10},{1,7},{2,12},{3,9},{4,14},{5,11},{6,0},{7,13},{8,2},{9,15},... | collective-permute-start | bytes 589832 | tf_op jit(solution)/shard_map/ppermute | solution.py:247
  138.8 4.2 %collective-permute-done.11 = bf16[128,768]{1,0:T(8,128)(2,1)S(1)} collective-permute-done((bf16[128,768]{1,0:T(8,128)(2,1)S(1)}, bf16[128,768]{1,0:T(8,128)(2,1)S(1)}, u32[]{:S(2)}, u32[]{:S(2)}) %collective-permute-start.11) | collective-permute-done | bytes 196640 | tf_op jit(solution)/shard_map/ppermute | solution.py:247
  143.0 4.8 %collective-permute-done.12 = bf16[128,768]{1,0:T(8,128)(2,1)S(1)} collective-permute-done((bf16[128,768]{1,0:T(8,128)(2,1)S(1)}, bf16[128,768]{1,0:T(8,128)(2,1)S(1)}, u32[]{:S(2)}, u32[]{:S(2)}) %collective-permute-start.12) | collective-permute-done | bytes 196640 | tf_op jit(solution)/shard_map/ppermute | solution.py:247
  (44 shorter events, 14.4 us)
Async XLA Ops:
  5.0 17.6 %copy-start.5 = (bf16[128,768]{1,0:T(8,128)(2,1)S(1)}, bf16[128,768]{1,0:T(8,128)(2,1)}, u32[]{:S(2)}) copy-start(bf16[128,768]{1,0:T(8,128)(2,1)} %get-tuple-element.12) | copy-start | bytes 589828
  5.1 66.0 %all-to-all-start = ((bf16[64,16,768]{2,1,0:T(8,128)(2,1)}), bf16[64,16,768]{2,1,0:T(8,128)(2,1)S(1)}, u32[]{:S(2)}, u32[]{:S(2)}) async-start(bf16[64,16,768]{2,1,0:T(8,128)(2,1)} %get-tuple-element.11), calls=%async_computation | async-start | bytes 3145728 | tf_op jit(solution)/shard_map/all_to_all | solution.py:302
  22.7 24.4 %collective-permute-start = (bf16[128,768]{1,0:T(8,128)(2,1)S(1)}, bf16[128,768]{1,0:T(8,128)(2,1)S(1)}, u32[]{:S(2)}, u32[]{:S(2)}) collective-permute-start(bf16[128,768]{1,0:T(8,128)(2,1)S(1)} %copy-done.5), channel_id=1, source_target_pairs={{0,2},{1,15},{2,4},{3,1},{4,6},{5,3},{6,8},{7,5},{8,10},{9,7},{10,... | collective-permute-start | bytes 589832 | tf_op jit(solution)/shard_map/ppermute | solution.py:247
  24.6 22.5 %collective-permute-start.1 = (bf16[128,768]{1,0:T(8,128)(2,1)S(1)}, bf16[128,768]{1,0:T(8,128)(2,1)S(1)}, u32[]{:S(2)}, u32[]{:S(2)}) collective-permute-start(bf16[128,768]{1,0:T(8,128)(2,1)S(1)} %copy-done.5), channel_id=1, source_target_pairs={{0,6},{1,11},{2,8},{3,13},{4,10},{5,15},{6,12},{7,1},{8,14},{9,3},... | collective-permute-start | bytes 589832 | tf_op jit(solution)/shard_map/ppermute | solution.py:247
  35.9 22.6 %collective-permute-start.3 = (bf16[128,768]{1,0:T(8,128)(2,1)S(1)}, bf16[128,768]{1,0:T(8,128)(2,1)S(1)}, u32[]{:S(2)}, u32[]{:S(2)}) collective-permute-start(bf16[128,768]{1,0:T(8,128)(2,1)S(1)} %copy-done.5), channel_id=1, source_target_pairs={{0,14},{1,3},{2,0},{3,5},{4,2},{5,7},{6,4},{7,9},{8,6},{9,11},{10,... | collective-permute-start | bytes 589832 | tf_op jit(solution)/shard_map/ppermute | solution.py:247
  40.1 19.9 %collective-permute-start.5 = (bf16[128,768]{1,0:T(8,128)(2,1)S(1)}, bf16[128,768]{1,0:T(8,128)(2,1)S(1)}, u32[]{:S(2)}, u32[]{:S(2)}) collective-permute-start(bf16[128,768]{1,0:T(8,128)(2,1)S(1)} %copy-done.5), channel_id=1, source_target_pairs={{0,10},{1,7},{2,12},{3,9},{4,14},{5,11},{6,0},{7,13},{8,2},{9,15},... | collective-permute-start | bytes 589832 | tf_op jit(solution)/shard_map/ppermute | solution.py:247
  47.1 17.3 %collective-permute-start.2 = (bf16[256,768]{1,0:T(8,128)(2,1)S(1)}, bf16[256,768]{1,0:T(8,128)(2,1)S(1)}, u32[]{:S(2)}, u32[]{:S(2)}) collective-permute-start(bf16[256,768]{1,0:T(8,128)(2,1)S(1)} %pad_maximum_fusion.1), channel_id=1, source_target_pairs={{0,2},{1,15},{2,4},{3,1},{4,6},{5,3},{6,8},{7,5},{8,10},{9,7},{10,... | collective-permute-start | bytes 1179656 | tf_op jit(solution)/shard_map/ppermute | solution.py:247
  60.6 26.3 %collective-permute-start.6 = (bf16[5,128,768]{2,1,0:T(8,128)(2,1)}, bf16[5,128,768]{2,1,0:T(8,128)(2,1)}, u32[]{:S(2)}, u32[]{:S(2)}) collective-permute-start(bf16[5,128,768]{2,1,0:T(8,128)(2,1)} %bitcast_dynamic-update-slice_fusion.first_hbm), channel_id=1, source_target_pairs={{0,1},{1,0},{2,3},{3,2},{4,5},{5,4},{6,7},{7,6},{8,9},{9,8},{10,11... | collective-permute-start | bytes 2949128 | tf_op jit(solution)/shard_map/ppermute | solution.py:237
  62.5 7.6 %collective-permute-start.4 = (bf16[128,768]{1,0:T(8,128)(2,1)S(1)}, bf16[128,768]{1,0:T(8,128)(2,1)S(1)}, u32[]{:S(2)}, u32[]{:S(2)}) collective-permute-start(bf16[128,768]{1,0:T(8,128)(2,1)S(1)} %collective-permute-done.3), channel_id=1, source_target_pairs={{0,14},{1,3},{2,0},{3,5},{4,2},{5,7},{6,4},{7,9},{8,6},{9,11},{10,... | collective-permute-start | bytes 589832 | tf_op jit(solution)/shard_map/ppermute | solution.py:247
  71.0 1.2 copy-start.1
  80.0 29.2 %collective-permute-start.9 = (bf16[4,128,768]{2,1,0:T(8,128)(2,1)}, bf16[4,128,768]{2,1,0:T(8,128)(2,1)}, u32[]{:S(2)}, u32[]{:S(2)}) collective-permute-start(bf16[4,128,768]{2,1,0:T(8,128)(2,1)} %get-tuple-element.19), channel_id=1, source_target_pairs={{0,1},{1,0},{2,3},{3,2},{4,5},{5,4},{6,7},{7,6},{8,9},{9,8},{10,11... | collective-permute-start | bytes 2359304 | tf_op jit(solution)/shard_map/ppermute | solution.py:237
  82.5 4.3 %collective-permute-start.7 = (bf16[3,128,768]{2,1,0:T(8,128)(2,1)}, bf16[3,128,768]{2,1,0:T(8,128)(2,1)S(1)}, u32[]{:S(2)}, u32[]{:S(2)}) collective-permute-start(bf16[3,128,768]{2,1,0:T(8,128)(2,1)} %pad_maximum_fusion.after_hbm.rest_hbm), channel_id=1, source_target_pairs={{0,1},{1,0},{2,3},{3,2},{4,5},{5,4},{6,7},{7,6},{8,9},{9,8},{10,11... | collective-permute-start | bytes 1769480 | tf_op jit(solution)/shard_map/ppermute | solution.py:237
  84.4 35.3 %collective-permute-start.8 = (bf16[4,128,768]{2,1,0:T(8,128)(2,1)}, bf16[4,128,768]{2,1,0:T(8,128)(2,1)S(1)}, u32[]{:S(2)}, u32[]{:S(2)}) collective-permute-start(bf16[4,128,768]{2,1,0:T(8,128)(2,1)} %get-tuple-element.17), channel_id=1, source_target_pairs={{0,1},{1,0},{2,3},{3,2},{4,5},{5,4},{6,7},{7,6},{8,9},{9,8},{10,11... | collective-permute-start | bytes 2359304 | tf_op jit(solution)/shard_map/ppermute | solution.py:237
  86.9 0.8 copy-start.4
  96.4 12.9 %copy-start.3 = (bf16[4,128,768]{2,1,0:T(8,128)(2,1)S(1)}, bf16[4,128,768]{2,1,0:T(8,128)(2,1)}, u32[]{:S(2)}) copy-start(bf16[4,128,768]{2,1,0:T(8,128)(2,1)} %get-tuple-element.18) | copy-start | bytes 2359300
  96.4 52.8 %all-to-all-start.1 = ((bf16[64,16,384]{2,1,0:T(8,128)(2,1)}), bf16[64,16,384]{2,1,0:T(8,128)(2,1)S(1)}, u32[]{:S(2)}, u32[]{:S(2)}) async-start(bf16[64,16,384]{2,1,0:T(8,128)(2,1)} %backward.1), calls=%async_computation.1 | async-start | bytes 1572864 | tf_op jit(solution)/shard_map/all_to_all | solution.py:366
  109.2 11.0 %copy-start.2 = (bf16[4,128,768]{2,1,0:T(8,128)(2,1)S(1)}, bf16[4,128,768]{2,1,0:T(8,128)(2,1)}, u32[]{:S(2)}) copy-start(bf16[4,128,768]{2,1,0:T(8,128)(2,1)} %get-tuple-element.16) | copy-start | bytes 2359300
  110.7 9.5 %collective-permute-start.13 = (bf16[128,768]{1,0:T(8,128)(2,1)S(1)}, bf16[128,768]{1,0:T(8,128)(2,1)S(1)}, u32[]{:S(2)}, u32[]{:S(2)}) collective-permute-start(bf16[128,768]{1,0:T(8,128)(2,1)S(1)} %get-tuple-element.24), channel_id=1, source_target_pairs={{0,2},{1,15},{2,4},{3,1},{4,6},{5,3},{6,8},{7,5},{8,10},{9,7},{10,... | collective-permute-start | bytes 589832 | tf_op jit(solution)/shard_map/ppermute | solution.py:247
  112.6 18.5 %collective-permute-start.10 = (bf16[2,128,768]{2,1,0:T(8,128)(2,1)S(1)}, bf16[2,128,768]{2,1,0:T(8,128)(2,1)S(1)}, u32[]{:S(2)}, u32[]{:S(2)}) collective-permute-start(bf16[2,128,768]{2,1,0:T(8,128)(2,1)S(1)} %slice.54), channel_id=1, source_target_pairs={{0,14},{1,3},{2,0},{3,5},{4,2},{5,7},{6,4},{7,9},{8,6},{9,11},{10,... | collective-permute-start | bytes 1179656 | tf_op jit(solution)/shard_map/ppermute | solution.py:247
  117.8 21.0 %collective-permute-start.15 = (bf16[128,768]{1,0:T(8,128)(2,1)S(1)}, bf16[128,768]{1,0:T(8,128)(2,1)S(1)}, u32[]{:S(2)}, u32[]{:S(2)}) collective-permute-start(bf16[128,768]{1,0:T(8,128)(2,1)S(1)} %get-tuple-element.25), channel_id=1, source_target_pairs={{0,6},{1,11},{2,8},{3,13},{4,10},{5,15},{6,12},{7,1},{8,14},{9,3},... | collective-permute-start | bytes 589832 | tf_op jit(solution)/shard_map/ppermute | solution.py:247
  120.3 18.5 %collective-permute-start.14 = (bf16[128,768]{1,0:T(8,128)(2,1)S(1)}, bf16[128,768]{1,0:T(8,128)(2,1)S(1)}, u32[]{:S(2)}, u32[]{:S(2)}) collective-permute-start(bf16[128,768]{1,0:T(8,128)(2,1)S(1)} %fusion), channel_id=1, source_target_pairs={{0,2},{1,15},{2,4},{3,1},{4,6},{5,3},{6,8},{7,5},{8,10},{9,7},{10,... | collective-permute-start | bytes 589832 | tf_op jit(solution)/shard_map/ppermute | solution.py:247
  131.3 17.9 %copy-start = (s32[128,1]{0,1:T(1,128)S(1)}, s32[128,1]{0,1:T(1,128)}, u32[]{:S(2)}) copy-start(s32[128,1]{0,1:T(1,128)} %param.9) | copy-start | bytes 1540
  131.3 11.7 %collective-permute-start.11 = (bf16[128,768]{1,0:T(8,128)(2,1)S(1)}, bf16[128,768]{1,0:T(8,128)(2,1)S(1)}, u32[]{:S(2)}, u32[]{:S(2)}) collective-permute-start(bf16[128,768]{1,0:T(8,128)(2,1)S(1)} %get-tuple-element.22), channel_id=1, source_target_pairs={{0,14},{1,3},{2,0},{3,5},{4,2},{5,7},{6,4},{7,9},{8,6},{9,11},{10,... | collective-permute-start | bytes 589832 | tf_op jit(solution)/shard_map/ppermute | solution.py:247
  136.9 10.9 %collective-permute-start.12 = (bf16[128,768]{1,0:T(8,128)(2,1)S(1)}, bf16[128,768]{1,0:T(8,128)(2,1)S(1)}, u32[]{:S(2)}, u32[]{:S(2)}) collective-permute-start(bf16[128,768]{1,0:T(8,128)(2,1)S(1)} %get-tuple-element.23), channel_id=1, source_target_pairs={{0,10},{1,7},{2,12},{3,9},{4,14},{5,11},{6,0},{7,13},{8,2},{9,15},... | collective-permute-start | bytes 589832 | tf_op jit(solution)/shard_map/ppermute | solution.py:247

commit v7 on v6

--- a/solution.py
+++ b/solution.py
@@ -210,7 +210,7 @@
         copy.wait()
 
 
-def collect_kernel(peers, ids_ref, got_hbm, out_ref, got, scr, rows, sem):
+def collect_kernel(peers, ids_ref, got_hbm, out_ref, mark_ref, got, scr, rows, sem):
     copy = pltpu.make_async_copy(got_hbm, got, sem)
     copy.start()
     placing = placing_of(ids_ref[...], peers)
@@ -218,6 +218,7 @@
     for lines, c, value in to_rows(got, scr):
         rows[lines, lanes(c)] = value.astype(BF16)
     out_ref[...] = mm(placing, rows[...], 0, 0).astype(BF16)
+    mark_ref[...] = ids_ref[...]
 
 
 def call(kernel, out_shape, in_specs, out_specs, scratch, limit, flops, moved, name):
@@ -256,6 +257,14 @@
     return first, rest, over_core(first), over_core(rest)
 
 
+def finish_kernel(total_ref, *refs):
+    *arrived, _, out_ref = refs
+    total = total_ref[...]
+    for ref in arrived:
+        total = total + ref[...].astype(F32)
+    out_ref[...] = total.reshape(out_ref.shape)
+
+
 def reduce_features(above, below, far_below, keep, swapped):
     outer, inner, under, total = [
         keep[i].astype(F32) + swapped[i].astype(F32) for i in range(keep.shape[0])
@@ -263,9 +272,7 @@
     far_above = round_z((outer + above[1].astype(F32)).astype(BF16), -3)
     near_above = round_z((inner + above[0].astype(F32)).astype(BF16), -1)
     near_below = round_z((under + below.astype(F32)).astype(BF16), 1)
-    for arrived in (near_above, far_above, near_below, far_below):
-        total = total + arrived.astype(F32)
-    return total
+    return total, near_above, far_above, near_below, far_below
 
 
 def on_device(tokens, cotangent, expert_ids, route_weight, w_gate, w_up, w_down):
@@ -339,7 +346,7 @@
     swapped_a = over_core(send_a)
     swapped_b = over_core(send_b)
     outward = (keep_a.astype(F32) + swapped_a.astype(F32)).astype(BF16)
-    above = round_z(outward[:2], -1)
+    above = [round_z(outward[0], -1), round_z(outward[1], -1)]
     below = round_z(outward[2], 1)
     far_below = round_z(outward[3], 3)
 
@@ -362,14 +369,14 @@
         62, 3 * product, 14 << 20, "backward",
     )(place, gate, up, cot, *gathered, wg, wu)
 
-    down_part = reduce_features(above, below, far_below, keep_b, swapped_b)
+    terms = reduce_features(above, below, far_below, keep_b, swapped_b)
     returned = lax.all_to_all(part, "expert", split_axis=0, concat_axis=0, tiled=True)
 
-    token_grad = call(
+    token_grad, mark = call(
         functools.partial(collect_kernel, peers),
-        shape((n, width), BF16),
+        (shape((n, width), BF16), shape((1, n), jnp.int32)),
         [VMEM, HBM],
-        VMEM,
+        (VMEM, VMEM),
         [
             pltpu.VMEM((peers, chunks, CAP * LANE), BF16),
             pltpu.VMEM((CAP, peers * chunks, LANE), F32),
@@ -378,7 +385,15 @@
         ],
         16, 2 * slots * n * width, 2 << 20, "collect",
     )(ids, returned)
-    return (token_grad, down_part.reshape(w_down.shape))
+    down_grad = call(
+        finish_kernel,
+        shape((width // ranks, 1, hidden), F32),
+        [VMEM] * (len(terms) + 1),
+        VMEM,
+        [],
+        8, 5 * LANE * hidden, 2 << 20, "finish",
+    )(*terms, mark)
+    return (token_grad, down_grad)
 
 
 def solution(mesh):

time: 152 us -> 144 us (0.947)
  waiting for transfers between devices: 22.9 us -> 14.9 us
  local copies, waits for them, and re-layouts: 6.72 us -> 4.75 us
    ppermute x12 -> x13, waiting for transfers between devices: 22.8 us -> 14.8 us  [round_z(): return lax.ppermute(x, ('z', 'core'), pairs)]
    unnamed x17 -> x16, local copies, waits for them, and re-layouts: 5.95 us -> 3.99 us
    ppermute x12 -> x13, starting transfers between devices: 55.2 us -> 56.7 us  [round_z(): return lax.ppermute(x, ('z', 'core'), pairs)]
  transfers between devices with their start and end apart: 18 -> 19, of which waited for: 5 -> 6; matrix products, arithmetic and copies ran while one was open for 5% -> 4% of each run, Pallas kernels for 11% -> 13%
where the time goes in v7:
time: 144 us; the launch traced here: 142 us
  starting transfers between devices  95.3 us (66%)
  Pallas kernels  23.7 us (16%)
  waiting for transfers between devices  14.9 us (10%)
  local copies, waits for them, and re-layouts  4.75 us (3%)
  other arithmetic  1.98 us (1%)
    ppermute x13, starting transfers between devices, round_z(): return lax.ppermute(x, ('z', 'core'), pairs)  56.7 us
    all_to_all x1, starting transfers between devices, on_device(): lax.all_to_all(packed, 'expert', split_axis=0, concat_axis=0, tiled=True)  17.6 us
    ppermute x13, waiting for transfers between devices, round_z(): return lax.ppermute(x, ('z', 'core'), pairs)  14.8 us
    all_to_all x1, starting transfers between devices, on_device(): lax.all_to_all(part, 'expert', split_axis=0, concat_axis=0, tiled=True)  12.8 us
    pallas_call x1, Pallas kernels, on_device(): call(backward_kernel, shape((peers, chunks, CAP * LANE), BF16), [SMEM] +...  8.65 us
    ppermute x4, starting transfers between devices, over_core(): return lax.ppermute(x, 'core', [(0, 1), (1, 0)])  8.21 us
    pallas_call x1, Pallas kernels, on_device(): call(forward_kernel, (quarter, quarter, quarter, quarter, shape((slots, h...  7.78 us
    pallas_call x1, Pallas kernels, on_device(): call(functools.partial(pack_kernel, peers), (shape((peers, chunks, 2 * CA...  4.4 us
  transfers between devices with their start and end apart: 19, of which 6 were waited for; matrix products, arithmetic and copies ran while one was open for 4% of the time, Pallas kernels for 13%

profile of v7, /device:TPU:14, one launch (start us, length us, event | category | flops | bytes accessed | tf_op | source)
XLA Modules:
  0.0 141.6 jit_solution(3797172322597465533)
XLA Ops:
  0.6 4.4 %pack.1 = (bf16[64,16,768]{2,1,0:T(8,128)(2,1)}, bf16[128,768]{1,0:T(8,128)(2,1)}) custom-call(s32[1,128]{1,0:T(1,128)} %bitcast.44, f32[1,128]{1,0:T(1,128)} %bitcast.52, bf16[128,2048]{1,0:T(8,128)(2,1)} %tok_hbm.1, bf16[128,2048]{1,0:T(8,128)(2,1)} %cot_hbm.1, bf16[128,768]{1,0:T(8,128)(2,1)} %bitcast.51), custom_call_target="tpu_custom_call" | custom-call | flops 201326592 | bytes 4194304 | tf_op jit(solution)/shard_map/pack/pallas_call | solution.py:294
  5.1 17.6 %all-to-all-start = ((bf16[64,16,768]{2,1,0:T(8,128)(2,1)}), bf16[64,16,768]{2,1,0:T(8,128)(2,1)S(1)}, u32[]{:S(2)}, u32[]{:S(2)}) async-start(bf16[64,16,768]{2,1,0:T(8,128)(2,1)} %get-tuple-element.13), calls=%async_computation | async-start | bytes 3145728 | tf_op jit(solution)/shard_map/all_to_all | solution.py:309
  22.7 1.9 %collective-permute-start = (bf16[128,768]{1,0:T(8,128)(2,1)S(1)}, bf16[128,768]{1,0:T(8,128)(2,1)S(1)}, u32[]{:S(2)}, u32[]{:S(2)}) collective-permute-start(bf16[128,768]{1,0:T(8,128)(2,1)S(1)} %copy-done.4), channel_id=1, source_target_pairs={{0,2},{1,15},{2,4},{3,1},{4,6},{5,3},{6,8},{7,5},{8,10},{9,7},{10,... | collective-permute-start | bytes 589832 | tf_op jit(solution)/shard_map/ppermute | solution.py:248
  24.6 11.3 %collective-permute-start.1 = (bf16[128,768]{1,0:T(8,128)(2,1)S(1)}, bf16[128,768]{1,0:T(8,128)(2,1)S(1)}, u32[]{:S(2)}, u32[]{:S(2)}) collective-permute-start(bf16[128,768]{1,0:T(8,128)(2,1)S(1)} %copy-done.4), channel_id=1, source_target_pairs={{0,6},{1,11},{2,8},{3,13},{4,10},{5,15},{6,12},{7,1},{8,14},{9,3},... | collective-permute-start | bytes 589832 | tf_op jit(solution)/shard_map/ppermute | solution.py:248
  35.9 4.1 %collective-permute-start.3 = (bf16[128,768]{1,0:T(8,128)(2,1)S(1)}, bf16[128,768]{1,0:T(8,128)(2,1)S(1)}, u32[]{:S(2)}, u32[]{:S(2)}) collective-permute-start(bf16[128,768]{1,0:T(8,128)(2,1)S(1)} %copy-done.4), channel_id=1, source_target_pairs={{0,14},{1,3},{2,0},{3,5},{4,2},{5,7},{6,4},{7,9},{8,6},{9,11},{10,... | collective-permute-start | bytes 589832 | tf_op jit(solution)/shard_map/ppermute | solution.py:248
  40.1 5.7 %collective-permute-start.5 = (bf16[128,768]{1,0:T(8,128)(2,1)S(1)}, bf16[128,768]{1,0:T(8,128)(2,1)S(1)}, u32[]{:S(2)}, u32[]{:S(2)}) collective-permute-start(bf16[128,768]{1,0:T(8,128)(2,1)S(1)} %copy-done.4), channel_id=1, source_target_pairs={{0,10},{1,7},{2,12},{3,9},{4,14},{5,11},{6,0},{7,13},{8,2},{9,15},... | collective-permute-start | bytes 589832 | tf_op jit(solution)/shard_map/ppermute | solution.py:248
  46.6 11.2 %collective-permute-start.2 = (bf16[256,768]{1,0:T(8,128)(2,1)S(1)}, bf16[256,768]{1,0:T(8,128)(2,1)S(1)}, u32[]{:S(2)}, u32[]{:S(2)}) collective-permute-start(bf16[256,768]{1,0:T(8,128)(2,1)S(1)} %pad_maximum_fusion.1), channel_id=1, source_target_pairs={{0,2},{1,15},{2,4},{3,1},{4,6},{5,3},{6,8},{7,5},{8,10},{9,7},{10,... | collective-permute-start | bytes 1179656 | tf_op jit(solution)/shard_map/ppermute | solution.py:248
  62.5 1.9 %collective-permute-start.4 = (bf16[128,768]{1,0:T(8,128)(2,1)S(1)}, bf16[128,768]{1,0:T(8,128)(2,1)S(1)}, u32[]{:S(2)}, u32[]{:S(2)}) collective-permute-start(bf16[128,768]{1,0:T(8,128)(2,1)S(1)} %collective-permute-done.3), channel_id=1, source_target_pairs={{0,14},{1,3},{2,0},{3,5},{4,2},{5,7},{6,4},{7,9},{8,6},{9,11},{10,... | collective-permute-start | bytes 589832 | tf_op jit(solution)/shard_map/ppermute | solution.py:248
  64.5 5.6 %collective-permute-done.4 = bf16[128,768]{1,0:T(8,128)(2,1)S(1)} collective-permute-done((bf16[128,768]{1,0:T(8,128)(2,1)S(1)}, bf16[128,768]{1,0:T(8,128)(2,1)S(1)}, u32[]{:S(2)}, u32[]{:S(2)}) %collective-permute-start.4) | collective-permute-done | bytes 196640 | tf_op jit(solution)/shard_map/ppermute | solution.py:248
  71.0 2.5 %collective-permute-start.7 = (bf16[3,128,768]{2,1,0:T(8,128)(2,1)}, bf16[3,128,768]{2,1,0:T(8,128)(2,1)}, u32[]{:S(2)}, u32[]{:S(2)}) collective-permute-start(bf16[3,128,768]{2,1,0:T(8,128)(2,1)} %pad_maximum_fusion.after_hbm.rest_hbm), channel_id=1, source_target_pairs={{0,1},{1,0},{2,3},{3,2},{4,5},{5,4},{6,7},{7,6},{8,9},{9,8},{10,11... | collective-permute-start | bytes 1769480 | tf_op jit(solution)/shard_map/ppermute | solution.py:238
  75.3 7.8 %forward.1 = (bf16[4,128,768]{2,1,0:T(8,128)(2,1)}, bf16[4,128,768]{2,1,0:T(8,128)(2,1)}, bf16[4,128,768]{2,1,0:T(8,128)(2,1)}, bf16[4,128,768]{2,1,0:T(8,128)(2...) custom-call(s32[2]{0:T(128)} %pad_add_fusion.place_ref, bf16[64,16,768]{2,1,0:T(8,128)(2,1)} %copy-done.1, ...), custom_call_target="tpu_custom_call" | custom-call | flops 1811939328 | bytes 14680064 | tf_op jit(solution)/shard_map/forward/pallas_call | solution.py:316
  83.1 1.9 %collective-permute-start.9 = (bf16[4,128,768]{2,1,0:T(8,128)(2,1)}, bf16[4,128,768]{2,1,0:T(8,128)(2,1)S(1)}, u32[]{:S(2)}, u32[]{:S(2)}) collective-permute-start(bf16[4,128,768]{2,1,0:T(8,128)(2,1)} %get-tuple-element.22), channel_id=1, source_target_pairs={{0,1},{1,0},{2,3},{3,2},{4,5},{5,4},{6,7},{7,6},{8,9},{9,8},{10,11... | collective-permute-start | bytes 2359304 | tf_op jit(solution)/shard_map/ppermute | solution.py:238
  85.0 8.6 %backward.1 = bf16[64,16,384]{2,1,0:T(8,128)(2,1)} custom-call(s32[2]{0:T(128)} %pad_add_fusion.place_ref, f32[192,768]{1,0:T(8,128)} %get-tuple-element.15.gate_hbm, f32[192,768]{1,0:T(8,128)} %get-tuple-element.16.up_hbm, bf16[192,2048]{1,0:T(8,128)(2,1)} %get-tuple-element.17.cot_hbm, bf16[5,128,768]{2,1,0:T(8,128)(2,1)} %bitcast_dynamic-update-slice_fusion.first_hbm, ...), custom_call_target="tpu_custom_call" | custom-call | flops 1811939328 | bytes 14680064 | tf_op jit(solution)/shard_map/backward/pallas_call | solution.py:353
  93.7 12.8 %all-to-all-start.1 = ((bf16[64,16,384]{2,1,0:T(8,128)(2,1)}), bf16[64,16,384]{2,1,0:T(8,128)(2,1)S(1)}, u32[]{:S(2)}, u32[]{:S(2)}) async-start(bf16[64,16,384]{2,1,0:T(8,128)(2,1)} %backward.1), calls=%async_computation.1 | async-start | bytes 1572864 | tf_op jit(solution)/shard_map/all_to_all | solution.py:373
  106.5 1.9 %collective-permute-start.8 = (bf16[4,128,768]{2,1,0:T(8,128)(2,1)S(1)}, bf16[4,128,768]{2,1,0:T(8,128)(2,1)S(1)}, u32[]{:S(2)}, u32[]{:S(2)}) collective-permute-start(bf16[4,128,768]{2,1,0:T(8,128)(2,1)S(1)} %copy-done.5), channel_id=1, source_target_pairs={{0,1},{1,0},{2,3},{3,2},{4,5},{5,4},{6,7},{7,6},{8,9},{9,8},{10,11... | collective-permute-start | bytes 2359304 | tf_op jit(solution)/shard_map/ppermute | solution.py:238
  108.8 3.1 %collective-permute-start.10 = (bf16[128,768]{1,0:T(8,128)(2,1)S(1)}, bf16[128,768]{1,0:T(8,128)(2,1)S(1)}, u32[]{:S(2)}, u32[]{:S(2)}) collective-permute-start(bf16[128,768]{1,0:T(8,128)(2,1)S(1)} %get-tuple-element.30), channel_id=1, source_target_pairs={{0,14},{1,3},{2,0},{3,5},{4,2},{5,7},{6,4},{7,9},{8,6},{9,11},{10,... | collective-permute-start | bytes 589832 | tf_op jit(solution)/shard_map/ppermute | solution.py:248
  111.8 2.6 %collective-permute-start.12 = (bf16[128,768]{1,0:T(8,128)(2,1)S(1)}, bf16[128,768]{1,0:T(8,128)(2,1)S(1)}, u32[]{:S(2)}, u32[]{:S(2)}) collective-permute-start(bf16[128,768]{1,0:T(8,128)(2,1)S(1)} %get-tuple-element.29), channel_id=1, source_target_pairs={{0,14},{1,3},{2,0},{3,5},{4,2},{5,7},{6,4},{7,9},{8,6},{9,11},{10,... | collective-permute-start | bytes 589832 | tf_op jit(solution)/shard_map/ppermute | solution.py:248
  114.4 3.2 %collective-permute-start.14 = (bf16[128,768]{1,0:T(8,128)(2,1)S(1)}, bf16[128,768]{1,0:T(8,128)(2,1)S(1)}, u32[]{:S(2)}, u32[]{:S(2)}) collective-permute-start(bf16[128,768]{1,0:T(8,128)(2,1)S(1)} %get-tuple-element.28), channel_id=1, source_target_pairs={{0,2},{1,15},{2,4},{3,1},{4,6},{5,3},{6,8},{7,5},{8,10},{9,7},{10,... | collective-permute-start | bytes 589832 | tf_op jit(solution)/shard_map/ppermute | solution.py:248
  117.7 2.4 %collective-permute-start.16 = (bf16[128,768]{1,0:T(8,128)(2,1)S(1)}, bf16[128,768]{1,0:T(8,128)(2,1)S(1)}, u32[]{:S(2)}, u32[]{:S(2)}) collective-permute-start(bf16[128,768]{1,0:T(8,128)(2,1)S(1)} %get-tuple-element.27), channel_id=1, source_target_pairs={{0,6},{1,11},{2,8},{3,13},{4,10},{5,15},{6,12},{7,1},{8,14},{9,3},... | collective-permute-start | bytes 589832 | tf_op jit(solution)/shard_map/ppermute | solution.py:248
  121.2 2.0 %collective-permute-done.14 = bf16[128,768]{1,0:T(8,128)(2,1)S(1)} collective-permute-done((bf16[128,768]{1,0:T(8,128)(2,1)S(1)}, bf16[128,768]{1,0:T(8,128)(2,1)S(1)}, u32[]{:S(2)}, u32[]{:S(2)}) %collective-permute-start.14) | collective-permute-done | bytes 196640 | tf_op jit(solution)/shard_map/ppermute | solution.py:248
  123.4 1.9 %collective-permute-start.11 = (bf16[128,768]{1,0:T(8,128)(2,1)S(1)}, bf16[128,768]{1,0:T(8,128)(2,1)S(1)}, u32[]{:S(2)}, u32[]{:S(2)}) collective-permute-start(bf16[128,768]{1,0:T(8,128)(2,1)S(1)} %get-tuple-element.26), channel_id=1, source_target_pairs={{0,14},{1,3},{2,0},{3,5},{4,2},{5,7},{6,4},{7,9},{8,6},{9,11},{10,... | collective-permute-start | bytes 589832 | tf_op jit(solution)/shard_map/ppermute | solution.py:248
  125.4 4.1 %collective-permute-start.13 = (bf16[128,768]{1,0:T(8,128)(2,1)S(1)}, bf16[128,768]{1,0:T(8,128)(2,1)S(1)}, u32[]{:S(2)}, u32[]{:S(2)}) collective-permute-start(bf16[128,768]{1,0:T(8,128)(2,1)S(1)} %get-tuple-element.25), channel_id=1, source_target_pairs={{0,10},{1,7},{2,12},{3,9},{4,14},{5,11},{6,0},{7,13},{8,2},{9,15},... | collective-permute-start | bytes 589832 | tf_op jit(solution)/shard_map/ppermute | solution.py:248
  129.5 3.2 %collective-permute-start.15 = (bf16[128,768]{1,0:T(8,128)(2,1)S(1)}, bf16[128,768]{1,0:T(8,128)(2,1)S(1)}, u32[]{:S(2)}, u32[]{:S(2)}) collective-permute-start(bf16[128,768]{1,0:T(8,128)(2,1)S(1)} %get-tuple-element.24), channel_id=1, source_target_pairs={{0,2},{1,15},{2,4},{3,1},{4,6},{5,3},{6,8},{7,5},{8,10},{9,7},{10,... | collective-permute-start | bytes 589832 | tf_op jit(solution)/shard_map/ppermute | solution.py:248
  135.2 5.4 %collective-permute-done.15.refs_2_ = bf16[128,768]{1,0:T(8,128)(2,1)S(1)} collective-permute-done((bf16[128,768]{1,0:T(8,128)(2,1)S(1)}, bf16[128,768]{1,0:T(8,128)(2,1)S(1)}, u32[]{:S(2)}, u32[]{:S(2)}) %collective-permute-start.15) | collective-permute-done | bytes 196640 | tf_op jit(solution)/shard_map/ppermute | solution.py:248
  (44 shorter events, 13.3 us)
Async XLA Ops:
  5.0 17.6 %copy-start.4 = (bf16[128,768]{1,0:T(8,128)(2,1)S(1)}, bf16[128,768]{1,0:T(8,128)(2,1)}, u32[]{:S(2)}) copy-start(bf16[128,768]{1,0:T(8,128)(2,1)} %get-tuple-element.14) | copy-start | bytes 589828
  5.1 69.0 %all-to-all-start = ((bf16[64,16,768]{2,1,0:T(8,128)(2,1)}), bf16[64,16,768]{2,1,0:T(8,128)(2,1)S(1)}, u32[]{:S(2)}, u32[]{:S(2)}) async-start(bf16[64,16,768]{2,1,0:T(8,128)(2,1)} %get-tuple-element.13), calls=%async_computation | async-start | bytes 3145728 | tf_op jit(solution)/shard_map/all_to_all | solution.py:309
  22.7 23.8 %collective-permute-start = (bf16[128,768]{1,0:T(8,128)(2,1)S(1)}, bf16[128,768]{1,0:T(8,128)(2,1)S(1)}, u32[]{:S(2)}, u32[]{:S(2)}) collective-permute-start(bf16[128,768]{1,0:T(8,128)(2,1)S(1)} %copy-done.4), channel_id=1, source_target_pairs={{0,2},{1,15},{2,4},{3,1},{4,6},{5,3},{6,8},{7,5},{8,10},{9,7},{10,... | collective-permute-start | bytes 589832 | tf_op jit(solution)/shard_map/ppermute | solution.py:248
  24.6 22.0 %collective-permute-start.1 = (bf16[128,768]{1,0:T(8,128)(2,1)S(1)}, bf16[128,768]{1,0:T(8,128)(2,1)S(1)}, u32[]{:S(2)}, u32[]{:S(2)}) collective-permute-start(bf16[128,768]{1,0:T(8,128)(2,1)S(1)} %copy-done.4), channel_id=1, source_target_pairs={{0,6},{1,11},{2,8},{3,13},{4,10},{5,15},{6,12},{7,1},{8,14},{9,3},... | collective-permute-start | bytes 589832 | tf_op jit(solution)/shard_map/ppermute | solution.py:248
  35.9 22.6 %collective-permute-start.3 = (bf16[128,768]{1,0:T(8,128)(2,1)S(1)}, bf16[128,768]{1,0:T(8,128)(2,1)S(1)}, u32[]{:S(2)}, u32[]{:S(2)}) collective-permute-start(bf16[128,768]{1,0:T(8,128)(2,1)S(1)} %copy-done.4), channel_id=1, source_target_pairs={{0,14},{1,3},{2,0},{3,5},{4,2},{5,7},{6,4},{7,9},{8,6},{9,11},{10,... | collective-permute-start | bytes 589832 | tf_op jit(solution)/shard_map/ppermute | solution.py:248
  40.1 19.9 %collective-permute-start.5 = (bf16[128,768]{1,0:T(8,128)(2,1)S(1)}, bf16[128,768]{1,0:T(8,128)(2,1)S(1)}, u32[]{:S(2)}, u32[]{:S(2)}) collective-permute-start(bf16[128,768]{1,0:T(8,128)(2,1)S(1)} %copy-done.4), channel_id=1, source_target_pairs={{0,10},{1,7},{2,12},{3,9},{4,14},{5,11},{6,0},{7,13},{8,2},{9,15},... | collective-permute-start | bytes 589832 | tf_op jit(solution)/shard_map/ppermute | solution.py:248
  46.6 17.8 %collective-permute-start.2 = (bf16[256,768]{1,0:T(8,128)(2,1)S(1)}, bf16[256,768]{1,0:T(8,128)(2,1)S(1)}, u32[]{:S(2)}, u32[]{:S(2)}) collective-permute-start(bf16[256,768]{1,0:T(8,128)(2,1)S(1)} %pad_maximum_fusion.1), channel_id=1, source_target_pairs={{0,2},{1,15},{2,4},{3,1},{4,6},{5,3},{6,8},{7,5},{8,10},{9,7},{10,... | collective-permute-start | bytes 1179656 | tf_op jit(solution)/shard_map/ppermute | solution.py:248
  60.6 24.4 %collective-permute-start.6 = (bf16[5,128,768]{2,1,0:T(8,128)(2,1)}, bf16[5,128,768]{2,1,0:T(8,128)(2,1)}, u32[]{:S(2)}, u32[]{:S(2)}) collective-permute-start(bf16[5,128,768]{2,1,0:T(8,128)(2,1)} %bitcast_dynamic-update-slice_fusion.first_hbm), channel_id=1, source_target_pairs={{0,1},{1,0},{2,3},{3,2},{4,5},{5,4},{6,7},{7,6},{8,9},{9,8},{10,11... | collective-permute-start | bytes 2949128 | tf_op jit(solution)/shard_map/ppermute | solution.py:238
  62.5 7.6 %collective-permute-start.4 = (bf16[128,768]{1,0:T(8,128)(2,1)S(1)}, bf16[128,768]{1,0:T(8,128)(2,1)S(1)}, u32[]{:S(2)}, u32[]{:S(2)}) collective-permute-start(bf16[128,768]{1,0:T(8,128)(2,1)S(1)} %collective-permute-done.3), channel_id=1, source_target_pairs={{0,14},{1,3},{2,0},{3,5},{4,2},{5,7},{6,4},{7,9},{8,6},{9,11},{10,... | collective-permute-start | bytes 589832 | tf_op jit(solution)/shard_map/ppermute | solution.py:248
  71.0 14.0 %collective-permute-start.7 = (bf16[3,128,768]{2,1,0:T(8,128)(2,1)}, bf16[3,128,768]{2,1,0:T(8,128)(2,1)}, u32[]{:S(2)}, u32[]{:S(2)}) collective-permute-start(bf16[3,128,768]{2,1,0:T(8,128)(2,1)} %pad_maximum_fusion.after_hbm.rest_hbm), channel_id=1, source_target_pairs={{0,1},{1,0},{2,3},{3,2},{4,5},{5,4},{6,7},{7,6},{8,9},{9,8},{10,11... | collective-permute-start | bytes 1769480 | tf_op jit(solution)/shard_map/ppermute | solution.py:238
  83.1 25.4 %collective-permute-start.9 = (bf16[4,128,768]{2,1,0:T(8,128)(2,1)}, bf16[4,128,768]{2,1,0:T(8,128)(2,1)S(1)}, u32[]{:S(2)}, u32[]{:S(2)}) collective-permute-start(bf16[4,128,768]{2,1,0:T(8,128)(2,1)} %get-tuple-element.22), channel_id=1, source_target_pairs={{0,1},{1,0},{2,3},{3,2},{4,5},{5,4},{6,7},{7,6},{8,9},{9,8},{10,11... | collective-permute-start | bytes 2359304 | tf_op jit(solution)/shard_map/ppermute | solution.py:238
  93.7 12.9 %copy-start.5 = (bf16[4,128,768]{2,1,0:T(8,128)(2,1)S(1)}, bf16[4,128,768]{2,1,0:T(8,128)(2,1)}, u32[]{:S(2)}) copy-start(bf16[4,128,768]{2,1,0:T(8,128)(2,1)} %get-tuple-element.20) | copy-start | bytes 2359300
  93.7 14.8 %copy-start.2 = (bf16[4,128,768]{2,1,0:T(8,128)(2,1)S(1)}, bf16[4,128,768]{2,1,0:T(8,128)(2,1)}, u32[]{:S(2)}) copy-start(bf16[4,128,768]{2,1,0:T(8,128)(2,1)} %get-tuple-element.21) | copy-start | bytes 2359300
  93.7 39.1 %all-to-all-start.1 = ((bf16[64,16,384]{2,1,0:T(8,128)(2,1)}), bf16[64,16,384]{2,1,0:T(8,128)(2,1)S(1)}, u32[]{:S(2)}, u32[]{:S(2)}) async-start(bf16[64,16,384]{2,1,0:T(8,128)(2,1)} %backward.1), calls=%async_computation.1 | async-start | bytes 1572864 | tf_op jit(solution)/shard_map/all_to_all | solution.py:373
  106.5 13.5 %collective-permute-start.8 = (bf16[4,128,768]{2,1,0:T(8,128)(2,1)S(1)}, bf16[4,128,768]{2,1,0:T(8,128)(2,1)S(1)}, u32[]{:S(2)}, u32[]{:S(2)}) collective-permute-start(bf16[4,128,768]{2,1,0:T(8,128)(2,1)S(1)} %copy-done.5), channel_id=1, source_target_pairs={{0,1},{1,0},{2,3},{3,2},{4,5},{5,4},{6,7},{7,6},{8,9},{9,8},{10,11... | collective-permute-start | bytes 2359304 | tf_op jit(solution)/shard_map/ppermute | solution.py:238
  108.5 14.7 %copy-start.3 = (bf16[4,128,768]{2,1,0:T(8,128)(2,1)S(1)}, bf16[4,128,768]{2,1,0:T(8,128)(2,1)}, u32[]{:S(2)}) copy-start(bf16[4,128,768]{2,1,0:T(8,128)(2,1)} %get-tuple-element.19) | copy-start | bytes 2359300
  108.8 11.3 %collective-permute-start.10 = (bf16[128,768]{1,0:T(8,128)(2,1)S(1)}, bf16[128,768]{1,0:T(8,128)(2,1)S(1)}, u32[]{:S(2)}, u32[]{:S(2)}) collective-permute-start(bf16[128,768]{1,0:T(8,128)(2,1)S(1)} %get-tuple-element.30), channel_id=1, source_target_pairs={{0,14},{1,3},{2,0},{3,5},{4,2},{5,7},{6,4},{7,9},{8,6},{9,11},{10,... | collective-permute-start | bytes 589832 | tf_op jit(solution)/shard_map/ppermute | solution.py:248
  111.8 9.4 %collective-permute-start.12 = (bf16[128,768]{1,0:T(8,128)(2,1)S(1)}, bf16[128,768]{1,0:T(8,128)(2,1)S(1)}, u32[]{:S(2)}, u32[]{:S(2)}) collective-permute-start(bf16[128,768]{1,0:T(8,128)(2,1)S(1)} %get-tuple-element.29), channel_id=1, source_target_pairs={{0,14},{1,3},{2,0},{3,5},{4,2},{5,7},{6,4},{7,9},{8,6},{9,11},{10,... | collective-permute-start | bytes 589832 | tf_op jit(solution)/shard_map/ppermute | solution.py:248
  114.4 8.8 %collective-permute-start.14 = (bf16[128,768]{1,0:T(8,128)(2,1)S(1)}, bf16[128,768]{1,0:T(8,128)(2,1)S(1)}, u32[]{:S(2)}, u32[]{:S(2)}) collective-permute-start(bf16[128,768]{1,0:T(8,128)(2,1)S(1)} %get-tuple-element.28), channel_id=1, source_target_pairs={{0,2},{1,15},{2,4},{3,1},{4,6},{5,3},{6,8},{7,5},{8,10},{9,7},{10,... | collective-permute-start | bytes 589832 | tf_op jit(solution)/shard_map/ppermute | solution.py:248
  117.7 17.0 %collective-permute-start.16 = (bf16[128,768]{1,0:T(8,128)(2,1)S(1)}, bf16[128,768]{1,0:T(8,128)(2,1)S(1)}, u32[]{:S(2)}, u32[]{:S(2)}) collective-permute-start(bf16[128,768]{1,0:T(8,128)(2,1)S(1)} %get-tuple-element.27), channel_id=1, source_target_pairs={{0,6},{1,11},{2,8},{3,13},{4,10},{5,15},{6,12},{7,1},{8,14},{9,3},... | collective-permute-start | bytes 589832 | tf_op jit(solution)/shard_map/ppermute | solution.py:248
  123.2 9.5 %copy-start = (s32[128,1]{0,1:T(1,128)S(1)}, s32[128,1]{0,1:T(1,128)}, u32[]{:S(2)}) copy-start(s32[128,1]{0,1:T(1,128)} %param.9) | copy-start | bytes 1540
  123.4 11.3 %collective-permute-start.11 = (bf16[128,768]{1,0:T(8,128)(2,1)S(1)}, bf16[128,768]{1,0:T(8,128)(2,1)S(1)}, u32[]{:S(2)}, u32[]{:S(2)}) collective-permute-start(bf16[128,768]{1,0:T(8,128)(2,1)S(1)} %get-tuple-element.26), channel_id=1, source_target_pairs={{0,14},{1,3},{2,0},{3,5},{4,2},{5,7},{6,4},{7,9},{8,6},{9,11},{10,... | collective-permute-start | bytes 589832 | tf_op jit(solution)/shard_map/ppermute | solution.py:248
  125.4 9.9 %collective-permute-start.13 = (bf16[128,768]{1,0:T(8,128)(2,1)S(1)}, bf16[128,768]{1,0:T(8,128)(2,1)S(1)}, u32[]{:S(2)}, u32[]{:S(2)}) collective-permute-start(bf16[128,768]{1,0:T(8,128)(2,1)S(1)} %get-tuple-element.25), channel_id=1, source_target_pairs={{0,10},{1,7},{2,12},{3,9},{4,14},{5,11},{6,0},{7,13},{8,2},{9,15},... | collective-permute-start | bytes 589832 | tf_op jit(solution)/shard_map/ppermute | solution.py:248
  129.5 11.2 %collective-permute-start.15 = (bf16[128,768]{1,0:T(8,128)(2,1)S(1)}, bf16[128,768]{1,0:T(8,128)(2,1)S(1)}, u32[]{:S(2)}, u32[]{:S(2)}) collective-permute-start(bf16[128,768]{1,0:T(8,128)(2,1)S(1)} %get-tuple-element.24), channel_id=1, source_target_pairs={{0,2},{1,15},{2,4},{3,1},{4,6},{5,3},{6,8},{7,5},{8,10},{9,7},{10,... | collective-permute-start | bytes 589832 | tf_op jit(solution)/shard_map/ppermute | solution.py:248
  (1 other events, 1.2 us)

commit v8 on v7

--- a/solution.py
+++ b/solution.py
@@ -250,7 +250,7 @@
 
 def gather_features(own):
     m1, p1, m3, p3 = round_z(own, 1), round_z(own, -1), round_z(own, 3), round_z(own, -3)
-    m2, m4 = jnp.split(round_z(jnp.concatenate([m1, m3]), 1), 2)
+    m2, m4 = round_z(m1, 1), round_z(m3, 1)
     p2 = round_z(p1, -1)
     first = jnp.stack([own, m1, p1, m3, p3])
     rest = jnp.stack([m2, m4, p2])

time: 144 us -> 149 us (1.035)
  the two profiles are of different devices: /device:TPU:14 before, /device:TPU:1 now
where the time goes in v8:
time: 149 us; the launch traced here: 148 us
  starting transfers between devices  95.9 us (64%)
  Pallas kernels  23.7 us (16%)
  waiting for transfers between devices  21.2 us (14%)
  local copies, waits for them, and re-layouts  4.72 us (3%)
  other arithmetic  1.95 us (1%)
    ppermute x14, starting transfers between devices, round_z(): return lax.ppermute(x, ('z', 'core'), pairs)  60.6 us
    ppermute x14, waiting for transfers between devices, round_z(): return lax.ppermute(x, ('z', 'core'), pairs)  21.2 us
    all_to_all x1, starting transfers between devices, on_device(): lax.all_to_all(packed, 'expert', split_axis=0, concat_axis=0, tiled=True)  14.2 us
    all_to_all x1, starting transfers between devices, on_device(): lax.all_to_all(part, 'expert', split_axis=0, concat_axis=0, tiled=True)  12.6 us
    pallas_call x1, Pallas kernels, on_device(): call(backward_kernel, shape((peers, chunks, CAP * LANE), BF16), [SMEM] +...  8.64 us
    ppermute x4, starting transfers between devices, over_core(): return lax.ppermute(x, 'core', [(0, 1), (1, 0)])  8.49 us
    pallas_call x1, Pallas kernels, on_device(): call(forward_kernel, (quarter, quarter, quarter, quarter, shape((slots, h...  7.79 us
    pallas_call x1, Pallas kernels, on_device(): call(functools.partial(pack_kernel, peers), (shape((peers, chunks, 2 * CA...  4.39 us
  transfers between devices with their start and end apart: 20, of which 6 were waited for; matrix products, arithmetic and copies ran while one was open for 4% of the time, Pallas kernels for 12%

profile of v8, /device:TPU:1, one launch (start us, length us, event | category | flops | bytes accessed | tf_op | source)
XLA Modules:
  0.0 148.4 jit_solution(12730929494605255169)
XLA Ops:
  0.6 4.4 %pack.1 = (bf16[64,16,768]{2,1,0:T(8,128)(2,1)}, bf16[128,768]{1,0:T(8,128)(2,1)}) custom-call(s32[1,128]{1,0:T(1,128)} %bitcast.42, f32[1,128]{1,0:T(1,128)} %bitcast.52, bf16[128,2048]{1,0:T(8,128)(2,1)} %tok_hbm.1, bf16[128,2048]{1,0:T(8,128)(2,1)} %cot_hbm.1, bf16[128,768]{1,0:T(8,128)(2,1)} %bitcast.51), custom_call_target="tpu_custom_call" | custom-call | flops 201326592 | bytes 4194304 | tf_op jit(solution)/shard_map/pack/pallas_call | solution.py:294
  5.0 14.2 %all-to-all-start = ((bf16[64,16,768]{2,1,0:T(8,128)(2,1)}), bf16[64,16,768]{2,1,0:T(8,128)(2,1)S(1)}, u32[]{:S(2)}, u32[]{:S(2)}) async-start(bf16[64,16,768]{2,1,0:T(8,128)(2,1)} %get-tuple-element.13), calls=%async_computation | async-start | bytes 3145728 | tf_op jit(solution)/shard_map/all_to_all | solution.py:309
  19.2 17.0 %collective-permute-start = (bf16[128,768]{1,0:T(8,128)(2,1)S(1)}, bf16[128,768]{1,0:T(8,128)(2,1)S(1)}, u32[]{:S(2)}, u32[]{:S(2)}) collective-permute-start(bf16[128,768]{1,0:T(8,128)(2,1)S(1)} %copy-done.4), channel_id=1, source_target_pairs={{0,2},{1,15},{2,4},{3,1},{4,6},{5,3},{6,8},{7,5},{8,10},{9,7},{10,... | collective-permute-start | bytes 589832 | tf_op jit(solution)/shard_map/ppermute | solution.py:248
  36.3 1.9 %collective-permute-start.2 = (bf16[128,768]{1,0:T(8,128)(2,1)S(1)}, bf16[128,768]{1,0:T(8,128)(2,1)S(1)}, u32[]{:S(2)}, u32[]{:S(2)}) collective-permute-start(bf16[128,768]{1,0:T(8,128)(2,1)S(1)} %copy-done.4), channel_id=1, source_target_pairs={{0,6},{1,11},{2,8},{3,13},{4,10},{5,15},{6,12},{7,1},{8,14},{9,3},... | collective-permute-start | bytes 589832 | tf_op jit(solution)/shard_map/ppermute | solution.py:248
  38.2 2.2 %collective-permute-start.4 = (bf16[128,768]{1,0:T(8,128)(2,1)S(1)}, bf16[128,768]{1,0:T(8,128)(2,1)S(1)}, u32[]{:S(2)}, u32[]{:S(2)}) collective-permute-start(bf16[128,768]{1,0:T(8,128)(2,1)S(1)} %copy-done.4), channel_id=1, source_target_pairs={{0,14},{1,3},{2,0},{3,5},{4,2},{5,7},{6,4},{7,9},{8,6},{9,11},{10,... | collective-permute-start | bytes 589832 | tf_op jit(solution)/shard_map/ppermute | solution.py:248
  40.4 4.9 %collective-permute-start.6 = (bf16[128,768]{1,0:T(8,128)(2,1)S(1)}, bf16[128,768]{1,0:T(8,128)(2,1)S(1)}, u32[]{:S(2)}, u32[]{:S(2)}) collective-permute-start(bf16[128,768]{1,0:T(8,128)(2,1)S(1)} %copy-done.4), channel_id=1, source_target_pairs={{0,10},{1,7},{2,12},{3,9},{4,14},{5,11},{6,0},{7,13},{8,2},{9,15},... | collective-permute-start | bytes 589832 | tf_op jit(solution)/shard_map/ppermute | solution.py:248
  48.5 5.6 %collective-permute-done.6 = bf16[128,768]{1,0:T(8,128)(2,1)S(1)} collective-permute-done((bf16[128,768]{1,0:T(8,128)(2,1)S(1)}, bf16[128,768]{1,0:T(8,128)(2,1)S(1)}, u32[]{:S(2)}, u32[]{:S(2)}) %collective-permute-start.6) | collective-permute-done | bytes 196640 | tf_op jit(solution)/shard_map/ppermute | solution.py:248
  54.8 2.0 %collective-permute-start.7 = (bf16[5,128,768]{2,1,0:T(8,128)(2,1)}, bf16[5,128,768]{2,1,0:T(8,128)(2,1)}, u32[]{:S(2)}, u32[]{:S(2)}) collective-permute-start(bf16[5,128,768]{2,1,0:T(8,128)(2,1)} %bitcast_dynamic-update-slice_fusion.first_hbm), channel_id=1, source_target_pairs={{0,1},{1,0},{2,3},{3,2},{4,5},{5,4},{6,7},{7,6},{8,9},{9,8},{10,11... | collective-permute-start | bytes 2949128 | tf_op jit(solution)/shard_map/ppermute | solution.py:238
  56.8 3.8 %collective-permute-start.1 = (bf16[128,768]{1,0:T(8,128)(2,1)S(1)}, bf16[128,768]{1,0:T(8,128)(2,1)S(1)}, u32[]{:S(2)}, u32[]{:S(2)}) collective-permute-start(bf16[128,768]{1,0:T(8,128)(2,1)S(1)} %collective-permute-done), channel_id=1, source_target_pairs={{0,2},{1,15},{2,4},{3,1},{4,6},{5,3},{6,8},{7,5},{8,10},{9,7},{10,... | collective-permute-start | bytes 589832 | tf_op jit(solution)/shard_map/ppermute | solution.py:248
  60.6 6.8 %collective-permute-start.3 = (bf16[128,768]{1,0:T(8,128)(2,1)S(1)}, bf16[128,768]{1,0:T(8,128)(2,1)S(1)}, u32[]{:S(2)}, u32[]{:S(2)}) collective-permute-start(bf16[128,768]{1,0:T(8,128)(2,1)S(1)} %collective-permute-done.2), channel_id=1, source_target_pairs={{0,2},{1,15},{2,4},{3,1},{4,6},{5,3},{6,8},{7,5},{8,10},{9,7},{10,... | collective-permute-start | bytes 589832 | tf_op jit(solution)/shard_map/ppermute | solution.py:248
  67.4 1.9 %collective-permute-start.5 = (bf16[128,768]{1,0:T(8,128)(2,1)S(1)}, bf16[128,768]{1,0:T(8,128)(2,1)S(1)}, u32[]{:S(2)}, u32[]{:S(2)}) collective-permute-start(bf16[128,768]{1,0:T(8,128)(2,1)S(1)} %collective-permute-done.4), channel_id=1, source_target_pairs={{0,14},{1,3},{2,0},{3,5},{4,2},{5,7},{6,4},{7,9},{8,6},{9,11},{10,... | collective-permute-start | bytes 589832 | tf_op jit(solution)/shard_map/ppermute | solution.py:248
  70.0 5.0 %collective-permute-done.5 = bf16[128,768]{1,0:T(8,128)(2,1)S(1)} collective-permute-done((bf16[128,768]{1,0:T(8,128)(2,1)S(1)}, bf16[128,768]{1,0:T(8,128)(2,1)S(1)}, u32[]{:S(2)}, u32[]{:S(2)}) %collective-permute-start.5) | collective-permute-done | bytes 196640 | tf_op jit(solution)/shard_map/ppermute | solution.py:248
  79.7 7.8 %forward.1 = (bf16[4,128,768]{2,1,0:T(8,128)(2,1)}, bf16[4,128,768]{2,1,0:T(8,128)(2,1)}, bf16[4,128,768]{2,1,0:T(8,128)(2,1)}, bf16[4,128,768]{2,1,0:T(8,128)(2...) custom-call(s32[2]{0:T(128)} %pad_add_fusion.place_ref, bf16[64,16,768]{2,1,0:T(8,128)(2,1)} %copy-done.1, ...), custom_call_target="tpu_custom_call" | custom-call | flops 1811939328 | bytes 14680064 | tf_op jit(solution)/shard_map/forward/pallas_call | solution.py:316
  87.5 2.4 %collective-permute-start.10 = (bf16[4,128,768]{2,1,0:T(8,128)(2,1)}, bf16[4,128,768]{2,1,0:T(8,128)(2,1)S(1)}, u32[]{:S(2)}, u32[]{:S(2)}) collective-permute-start(bf16[4,128,768]{2,1,0:T(8,128)(2,1)} %get-tuple-element.22), channel_id=1, source_target_pairs={{0,1},{1,0},{2,3},{3,2},{4,5},{5,4},{6,7},{7,6},{8,9},{9,8},{10,11... | collective-permute-start | bytes 2359304 | tf_op jit(solution)/shard_map/ppermute | solution.py:238
  89.9 8.6 %backward.1 = bf16[64,16,384]{2,1,0:T(8,128)(2,1)} custom-call(s32[2]{0:T(128)} %pad_add_fusion.place_ref, f32[192,768]{1,0:T(8,128)} %get-tuple-element.15.gate_hbm, f32[192,768]{1,0:T(8,128)} %get-tuple-element.16.up_hbm, bf16[192,2048]{1,0:T(8,128)(2,1)} %get-tuple-element.17.cot_hbm, bf16[5,128,768]{2,1,0:T(8,128)(2,1)} %bitcast_dynamic-update-slice_fusion.first_hbm, ...), custom_call_target="tpu_custom_call" | custom-call | flops 1811939328 | bytes 14680064 | tf_op jit(solution)/shard_map/backward/pallas_call | solution.py:353
  98.6 12.6 %all-to-all-start.1 = ((bf16[64,16,384]{2,1,0:T(8,128)(2,1)}), bf16[64,16,384]{2,1,0:T(8,128)(2,1)S(1)}, u32[]{:S(2)}, u32[]{:S(2)}) async-start(bf16[64,16,384]{2,1,0:T(8,128)(2,1)} %backward.1), calls=%async_computation.1 | async-start | bytes 1572864 | tf_op jit(solution)/shard_map/all_to_all | solution.py:373
  111.2 2.2 %collective-permute-start.9 = (bf16[4,128,768]{2,1,0:T(8,128)(2,1)S(1)}, bf16[4,128,768]{2,1,0:T(8,128)(2,1)S(1)}, u32[]{:S(2)}, u32[]{:S(2)}) collective-permute-start(bf16[4,128,768]{2,1,0:T(8,128)(2,1)S(1)} %copy-done.5), channel_id=1, source_target_pairs={{0,1},{1,0},{2,3},{3,2},{4,5},{5,4},{6,7},{7,6},{8,9},{9,8},{10,11... | collective-permute-start | bytes 2359304 | tf_op jit(solution)/shard_map/ppermute | solution.py:238
  113.7 1.9 %collective-permute-start.11 = (bf16[128,768]{1,0:T(8,128)(2,1)S(1)}, bf16[128,768]{1,0:T(8,128)(2,1)S(1)}, u32[]{:S(2)}, u32[]{:S(2)}) collective-permute-start(bf16[128,768]{1,0:T(8,128)(2,1)S(1)} %get-tuple-element.30), channel_id=1, source_target_pairs={{0,14},{1,3},{2,0},{3,5},{4,2},{5,7},{6,4},{7,9},{8,6},{9,11},{10,... | collective-permute-start | bytes 589832 | tf_op jit(solution)/shard_map/ppermute | solution.py:248
  117.5 4.6 %collective-permute-start.15 = (bf16[128,768]{1,0:T(8,128)(2,1)S(1)}, bf16[128,768]{1,0:T(8,128)(2,1)S(1)}, u32[]{:S(2)}, u32[]{:S(2)}) collective-permute-start(bf16[128,768]{1,0:T(8,128)(2,1)S(1)} %get-tuple-element.28), channel_id=1, source_target_pairs={{0,2},{1,15},{2,4},{3,1},{4,6},{5,3},{6,8},{7,5},{8,10},{9,7},{10,... | collective-permute-start | bytes 589832 | tf_op jit(solution)/shard_map/ppermute | solution.py:248
  122.1 3.5 %collective-permute-start.17 = (bf16[128,768]{1,0:T(8,128)(2,1)S(1)}, bf16[128,768]{1,0:T(8,128)(2,1)S(1)}, u32[]{:S(2)}, u32[]{:S(2)}) collective-permute-start(bf16[128,768]{1,0:T(8,128)(2,1)S(1)} %get-tuple-element.27), channel_id=1, source_target_pairs={{0,6},{1,11},{2,8},{3,13},{4,10},{5,15},{6,12},{7,1},{8,14},{9,3},... | collective-permute-start | bytes 589832 | tf_op jit(solution)/shard_map/ppermute | solution.py:248
  127.2 2.0 %collective-permute-start.12 = (bf16[128,768]{1,0:T(8,128)(2,1)S(1)}, bf16[128,768]{1,0:T(8,128)(2,1)S(1)}, u32[]{:S(2)}, u32[]{:S(2)}) collective-permute-start(bf16[128,768]{1,0:T(8,128)(2,1)S(1)} %get-tuple-element.26), channel_id=1, source_target_pairs={{0,14},{1,3},{2,0},{3,5},{4,2},{5,7},{6,4},{7,9},{8,6},{9,11},{10,... | collective-permute-start | bytes 589832 | tf_op jit(solution)/shard_map/ppermute | solution.py:248
  129.2 4.3 %collective-permute-start.14 = (bf16[128,768]{1,0:T(8,128)(2,1)S(1)}, bf16[128,768]{1,0:T(8,128)(2,1)S(1)}, u32[]{:S(2)}, u32[]{:S(2)}) collective-permute-start(bf16[128,768]{1,0:T(8,128)(2,1)S(1)} %get-tuple-element.25), channel_id=1, source_target_pairs={{0,10},{1,7},{2,12},{3,9},{4,14},{5,11},{6,0},{7,13},{8,2},{9,15},... | collective-permute-start | bytes 589832 | tf_op jit(solution)/shard_map/ppermute | solution.py:248
  133.5 3.9 %collective-permute-start.16 = (bf16[128,768]{1,0:T(8,128)(2,1)S(1)}, bf16[128,768]{1,0:T(8,128)(2,1)S(1)}, u32[]{:S(2)}, u32[]{:S(2)}) collective-permute-start(bf16[128,768]{1,0:T(8,128)(2,1)S(1)} %get-tuple-element.24), channel_id=1, source_target_pairs={{0,2},{1,15},{2,4},{3,1},{4,6},{5,3},{6,8},{7,5},{8,10},{9,7},{10,... | collective-permute-start | bytes 589832 | tf_op jit(solution)/shard_map/ppermute | solution.py:248
  139.4 8.1 %collective-permute-done.14.refs_1_ = bf16[128,768]{1,0:T(8,128)(2,1)S(1)} collective-permute-done((bf16[128,768]{1,0:T(8,128)(2,1)S(1)}, bf16[128,768]{1,0:T(8,128)(2,1)S(1)}, u32[]{:S(2)}, u32[]{:S(2)}) %collective-permute-start.14) | collective-permute-done | bytes 196640 | tf_op jit(solution)/shard_map/ppermute | solution.py:248
  (44 shorter events, 15.9 us)
Async XLA Ops:
  5.0 14.2 %copy-start.4 = (bf16[128,768]{1,0:T(8,128)(2,1)S(1)}, bf16[128,768]{1,0:T(8,128)(2,1)}, u32[]{:S(2)}) copy-start(bf16[128,768]{1,0:T(8,128)(2,1)} %get-tuple-element.14) | copy-start | bytes 589828
  5.0 73.5 %all-to-all-start = ((bf16[64,16,768]{2,1,0:T(8,128)(2,1)}), bf16[64,16,768]{2,1,0:T(8,128)(2,1)S(1)}, u32[]{:S(2)}, u32[]{:S(2)}) async-start(bf16[64,16,768]{2,1,0:T(8,128)(2,1)} %get-tuple-element.13), calls=%async_computation | async-start | bytes 3145728 | tf_op jit(solution)/shard_map/all_to_all | solution.py:309
  19.2 26.8 %collective-permute-start = (bf16[128,768]{1,0:T(8,128)(2,1)S(1)}, bf16[128,768]{1,0:T(8,128)(2,1)S(1)}, u32[]{:S(2)}, u32[]{:S(2)}) collective-permute-start(bf16[128,768]{1,0:T(8,128)(2,1)S(1)} %copy-done.4), channel_id=1, source_target_pairs={{0,2},{1,15},{2,4},{3,1},{4,6},{5,3},{6,8},{7,5},{8,10},{9,7},{10,... | collective-permute-start | bytes 589832 | tf_op jit(solution)/shard_map/ppermute | solution.py:248
  36.3 11.6 %collective-permute-start.2 = (bf16[128,768]{1,0:T(8,128)(2,1)S(1)}, bf16[128,768]{1,0:T(8,128)(2,1)S(1)}, u32[]{:S(2)}, u32[]{:S(2)}) collective-permute-start(bf16[128,768]{1,0:T(8,128)(2,1)S(1)} %copy-done.4), channel_id=1, source_target_pairs={{0,6},{1,11},{2,8},{3,13},{4,10},{5,15},{6,12},{7,1},{8,14},{9,3},... | collective-permute-start | bytes 589832 | tf_op jit(solution)/shard_map/ppermute | solution.py:248
  38.2 8.9 %collective-permute-start.4 = (bf16[128,768]{1,0:T(8,128)(2,1)S(1)}, bf16[128,768]{1,0:T(8,128)(2,1)S(1)}, u32[]{:S(2)}, u32[]{:S(2)}) collective-permute-start(bf16[128,768]{1,0:T(8,128)(2,1)S(1)} %copy-done.4), channel_id=1, source_target_pairs={{0,14},{1,3},{2,0},{3,5},{4,2},{5,7},{6,4},{7,9},{8,6},{9,11},{10,... | collective-permute-start | bytes 589832 | tf_op jit(solution)/shard_map/ppermute | solution.py:248
  40.4 13.7 %collective-permute-start.6 = (bf16[128,768]{1,0:T(8,128)(2,1)S(1)}, bf16[128,768]{1,0:T(8,128)(2,1)S(1)}, u32[]{:S(2)}, u32[]{:S(2)}) collective-permute-start(bf16[128,768]{1,0:T(8,128)(2,1)S(1)} %copy-done.4), channel_id=1, source_target_pairs={{0,10},{1,7},{2,12},{3,9},{4,14},{5,11},{6,0},{7,13},{8,2},{9,15},... | collective-permute-start | bytes 589832 | tf_op jit(solution)/shard_map/ppermute | solution.py:248
  54.8 35.1 %collective-permute-start.7 = (bf16[5,128,768]{2,1,0:T(8,128)(2,1)}, bf16[5,128,768]{2,1,0:T(8,128)(2,1)}, u32[]{:S(2)}, u32[]{:S(2)}) collective-permute-start(bf16[5,128,768]{2,1,0:T(8,128)(2,1)} %bitcast_dynamic-update-slice_fusion.first_hbm), channel_id=1, source_target_pairs={{0,1},{1,0},{2,3},{3,2},{4,5},{5,4},{6,7},{7,6},{8,9},{9,8},{10,11... | collective-permute-start | bytes 2949128 | tf_op jit(solution)/shard_map/ppermute | solution.py:238
  56.8 12.6 %collective-permute-start.1 = (bf16[128,768]{1,0:T(8,128)(2,1)S(1)}, bf16[128,768]{1,0:T(8,128)(2,1)S(1)}, u32[]{:S(2)}, u32[]{:S(2)}) collective-permute-start(bf16[128,768]{1,0:T(8,128)(2,1)S(1)} %collective-permute-done), channel_id=1, source_target_pairs={{0,2},{1,15},{2,4},{3,1},{4,6},{5,3},{6,8},{7,5},{8,10},{9,7},{10,... | collective-permute-start | bytes 589832 | tf_op jit(solution)/shard_map/ppermute | solution.py:248
  60.6 9.4 %collective-permute-start.3 = (bf16[128,768]{1,0:T(8,128)(2,1)S(1)}, bf16[128,768]{1,0:T(8,128)(2,1)S(1)}, u32[]{:S(2)}, u32[]{:S(2)}) collective-permute-start(bf16[128,768]{1,0:T(8,128)(2,1)S(1)} %collective-permute-done.2), channel_id=1, source_target_pairs={{0,2},{1,15},{2,4},{3,1},{4,6},{5,3},{6,8},{7,5},{8,10},{9,7},{10,... | collective-permute-start | bytes 589832 | tf_op jit(solution)/shard_map/ppermute | solution.py:248
  67.4 7.6 %collective-permute-start.5 = (bf16[128,768]{1,0:T(8,128)(2,1)S(1)}, bf16[128,768]{1,0:T(8,128)(2,1)S(1)}, u32[]{:S(2)}, u32[]{:S(2)}) collective-permute-start(bf16[128,768]{1,0:T(8,128)(2,1)S(1)} %collective-permute-done.4), channel_id=1, source_target_pairs={{0,14},{1,3},{2,0},{3,5},{4,2},{5,7},{6,4},{7,9},{8,6},{9,11},{10,... | collective-permute-start | bytes 589832 | tf_op jit(solution)/shard_map/ppermute | solution.py:248
  76.0 13.9 %collective-permute-start.8 = (bf16[3,128,768]{2,1,0:T(8,128)(2,1)}, bf16[3,128,768]{2,1,0:T(8,128)(2,1)}, u32[]{:S(2)}, u32[]{:S(2)}) collective-permute-start(bf16[3,128,768]{2,1,0:T(8,128)(2,1)} %pad_maximum_fusion.after_hbm.rest_hbm), channel_id=1, source_target_pairs={{0,1},{1,0},{2,3},{3,2},{4,5},{5,4},{6,7},{7,6},{8,9},{9,8},{10,11... | collective-permute-start | bytes 1769480 | tf_op jit(solution)/shard_map/ppermute | solution.py:238
  87.5 25.9 %collective-permute-start.10 = (bf16[4,128,768]{2,1,0:T(8,128)(2,1)}, bf16[4,128,768]{2,1,0:T(8,128)(2,1)S(1)}, u32[]{:S(2)}, u32[]{:S(2)}) collective-permute-start(bf16[4,128,768]{2,1,0:T(8,128)(2,1)} %get-tuple-element.22), channel_id=1, source_target_pairs={{0,1},{1,0},{2,3},{3,2},{4,5},{5,4},{6,7},{7,6},{8,9},{9,8},{10,11... | collective-permute-start | bytes 2359304 | tf_op jit(solution)/shard_map/ppermute | solution.py:238
  98.6 12.6 %copy-start.5 = (bf16[4,128,768]{2,1,0:T(8,128)(2,1)S(1)}, bf16[4,128,768]{2,1,0:T(8,128)(2,1)}, u32[]{:S(2)}) copy-start(bf16[4,128,768]{2,1,0:T(8,128)(2,1)} %get-tuple-element.20) | copy-start | bytes 2359300
  98.6 14.8 %copy-start.2 = (bf16[4,128,768]{2,1,0:T(8,128)(2,1)S(1)}, bf16[4,128,768]{2,1,0:T(8,128)(2,1)}, u32[]{:S(2)}) copy-start(bf16[4,128,768]{2,1,0:T(8,128)(2,1)} %get-tuple-element.21) | copy-start | bytes 2359300
  98.6 38.9 %all-to-all-start.1 = ((bf16[64,16,384]{2,1,0:T(8,128)(2,1)}), bf16[64,16,384]{2,1,0:T(8,128)(2,1)S(1)}, u32[]{:S(2)}, u32[]{:S(2)}) async-start(bf16[64,16,384]{2,1,0:T(8,128)(2,1)} %backward.1), calls=%async_computation.1 | async-start | bytes 1572864 | tf_op jit(solution)/shard_map/all_to_all | solution.py:373
  111.2 14.4 %collective-permute-start.9 = (bf16[4,128,768]{2,1,0:T(8,128)(2,1)S(1)}, bf16[4,128,768]{2,1,0:T(8,128)(2,1)S(1)}, u32[]{:S(2)}, u32[]{:S(2)}) collective-permute-start(bf16[4,128,768]{2,1,0:T(8,128)(2,1)S(1)} %copy-done.5), channel_id=1, source_target_pairs={{0,1},{1,0},{2,3},{3,2},{4,5},{5,4},{6,7},{7,6},{8,9},{9,8},{10,11... | collective-permute-start | bytes 2359304 | tf_op jit(solution)/shard_map/ppermute | solution.py:238
  113.4 13.6 %copy-start.3 = (bf16[4,128,768]{2,1,0:T(8,128)(2,1)S(1)}, bf16[4,128,768]{2,1,0:T(8,128)(2,1)}, u32[]{:S(2)}) copy-start(bf16[4,128,768]{2,1,0:T(8,128)(2,1)} %get-tuple-element.19) | copy-start | bytes 2359300
  113.7 11.9 %collective-permute-start.11 = (bf16[128,768]{1,0:T(8,128)(2,1)S(1)}, bf16[128,768]{1,0:T(8,128)(2,1)S(1)}, u32[]{:S(2)}, u32[]{:S(2)}) collective-permute-start(bf16[128,768]{1,0:T(8,128)(2,1)S(1)} %get-tuple-element.30), channel_id=1, source_target_pairs={{0,14},{1,3},{2,0},{3,5},{4,2},{5,7},{6,4},{7,9},{8,6},{9,11},{10,... | collective-permute-start | bytes 589832 | tf_op jit(solution)/shard_map/ppermute | solution.py:248
  115.6 10.0 %collective-permute-start.13 = (bf16[128,768]{1,0:T(8,128)(2,1)S(1)}, bf16[128,768]{1,0:T(8,128)(2,1)S(1)}, u32[]{:S(2)}, u32[]{:S(2)}) collective-permute-start(bf16[128,768]{1,0:T(8,128)(2,1)S(1)} %get-tuple-element.29), channel_id=1, source_target_pairs={{0,14},{1,3},{2,0},{3,5},{4,2},{5,7},{6,4},{7,9},{8,6},{9,11},{10,... | collective-permute-start | bytes 589832 | tf_op jit(solution)/shard_map/ppermute | solution.py:248
  117.5 9.5 %collective-permute-start.15 = (bf16[128,768]{1,0:T(8,128)(2,1)S(1)}, bf16[128,768]{1,0:T(8,128)(2,1)S(1)}, u32[]{:S(2)}, u32[]{:S(2)}) collective-permute-start(bf16[128,768]{1,0:T(8,128)(2,1)S(1)} %get-tuple-element.28), channel_id=1, source_target_pairs={{0,2},{1,15},{2,4},{3,1},{4,6},{5,3},{6,8},{7,5},{8,10},{9,7},{10,... | collective-permute-start | bytes 589832 | tf_op jit(solution)/shard_map/ppermute | solution.py:248
  122.1 17.3 %collective-permute-start.17 = (bf16[128,768]{1,0:T(8,128)(2,1)S(1)}, bf16[128,768]{1,0:T(8,128)(2,1)S(1)}, u32[]{:S(2)}, u32[]{:S(2)}) collective-permute-start(bf16[128,768]{1,0:T(8,128)(2,1)S(1)} %get-tuple-element.27), channel_id=1, source_target_pairs={{0,6},{1,11},{2,8},{3,13},{4,10},{5,15},{6,12},{7,1},{8,14},{9,3},... | collective-permute-start | bytes 589832 | tf_op jit(solution)/shard_map/ppermute | solution.py:248
  127.2 12.2 %collective-permute-start.12 = (bf16[128,768]{1,0:T(8,128)(2,1)S(1)}, bf16[128,768]{1,0:T(8,128)(2,1)S(1)}, u32[]{:S(2)}, u32[]{:S(2)}) collective-permute-start(bf16[128,768]{1,0:T(8,128)(2,1)S(1)} %get-tuple-element.26), channel_id=1, source_target_pairs={{0,14},{1,3},{2,0},{3,5},{4,2},{5,7},{6,4},{7,9},{8,6},{9,11},{10,... | collective-permute-start | bytes 589832 | tf_op jit(solution)/shard_map/ppermute | solution.py:248
  129.2 18.3 %collective-permute-start.14 = (bf16[128,768]{1,0:T(8,128)(2,1)S(1)}, bf16[128,768]{1,0:T(8,128)(2,1)S(1)}, u32[]{:S(2)}, u32[]{:S(2)}) collective-permute-start(bf16[128,768]{1,0:T(8,128)(2,1)S(1)} %get-tuple-element.25), channel_id=1, source_target_pairs={{0,10},{1,7},{2,12},{3,9},{4,14},{5,11},{6,0},{7,13},{8,2},{9,15},... | collective-permute-start | bytes 589832 | tf_op jit(solution)/shard_map/ppermute | solution.py:248
  133.5 14.0 %collective-permute-start.16 = (bf16[128,768]{1,0:T(8,128)(2,1)S(1)}, bf16[128,768]{1,0:T(8,128)(2,1)S(1)}, u32[]{:S(2)}, u32[]{:S(2)}) collective-permute-start(bf16[128,768]{1,0:T(8,128)(2,1)S(1)} %get-tuple-element.24), channel_id=1, source_target_pairs={{0,2},{1,15},{2,4},{3,1},{4,6},{5,3},{6,8},{7,5},{8,10},{9,7},{10,... | collective-permute-start | bytes 589832 | tf_op jit(solution)/shard_map/ppermute | solution.py:248
  (2 other events, 11.7 us)
